TPU v7x, 128 devices: a whole 4x4x4 slice. The times are simulated.
128 devices in a mesh: lat: 8 (over z_hi, y), lon: 16 (over z_lo, x, core).
Axes of the slice: x: 4, y: 4, z: 4 (z_hi: 2, z_lo: 2; z = z_hi * 2 + z_lo), core: 2. Of those that a mesh axis runs over, the one named last changes fastest.
Arguments:
- fields: bfloat16 [8, 192, 192, 192], P(None, 'lat', 'lon'), may hold values from -6 to 6
- cotangent: bfloat16 [8, 192, 192, 192], P(None, 'lat', 'lon'), may hold values from -6 to 6
- norm_gain: float32 [192], replicated, may hold values from 0.1 to 1.9
- qkv_weight: bfloat16 [192, 576], replicated, may hold values from -0.4375 to 0.4375
- proj_weight: bfloat16 [192, 192], replicated, may hold values from -0.4375 to 0.4375
- bias_table: bfloat16 [21, 6, 144, 144], P(None, None, 'lon'), may hold values from -4 to 240
- window_types: int32 [16], replicated, may hold values from 0 to 20
- valid_mask: int32 [192, 192], replicated, may hold values from 0 to 1, as said below
Outputs:
- mixed_out: bfloat16 [8, 192, 192, 192], P(None, 'lat', 'lon')
- grad_fields: bfloat16 [8, 192, 192, 192], P(None, 'lat', 'lon')
- grad_bias: float32 [16, 6, 144, 144], P('lat', None, 'lon')
Inputs may be any that keep to these rules, and one draw needn't show every extreme that they name: valid_mask is 1 outside the first three and the last three latitude rows.
All inputs are finite; a program needn't handle non-finite values.
Results may differ from a plain program's by a relative error of at most 0.022.
Values may be sent and summed in bfloat16 or wider, within the bound.
No kernel may reach another device: no remote copies, remote signals or barrier semaphores. Data moves between devices by JAX's collectives and lax.ppermute only.
A program may use at most 128 MiB of HBM per device.

v0:
```python
import jax
import jax.numpy as jnp
from jax import lax
from jax.sharding import PartitionSpec as P

HEADS = 6
WZ = 2
WLAT = 12
WLON = 6
WIN = 144
SLAT = 6
SLON = 3


NEGATIVE = -1e30
EPSILON = 1e-05


def from_behind(block, axis, distance):
    devices = range(lax.axis_size(axis))
    route = [((i - distance) % len(devices), i) for i in devices]
    return lax.ppermute(block, axis, route)


def product(pattern, operand_a, operand_b):
    return jnp.einsum(pattern, operand_a, operand_b, preferred_element_type=jnp.float32)


def to_windows(per_cell):
    levels, lat_cells, lon_cells, channels = per_cell.shape
    blocks = per_cell.reshape(
        levels // WZ, WZ, lat_cells // WLAT, WLAT, lon_cells // WLON, WLON, channels
    )
    blocks = blocks.transpose(0, 2, 4, 1, 3, 5, 6)
    return blocks.reshape(levels // WZ, lat_cells // WLAT, lon_cells // WLON, WIN, channels)


def from_windows(per_window, levels, lat_cells, lon_cells):
    channels = per_window.shape[-1]
    blocks = per_window.reshape(
        levels // WZ, lat_cells // WLAT, lon_cells // WLON, WZ, WLAT, WLON, channels
    )
    return blocks.transpose(0, 3, 1, 4, 2, 5, 6).reshape(levels, lat_cells, lon_cells, channels)


def local(
    fields, cotangent, norm_gain, qkv_weight, proj_weight, bias_table, window_types, valid_mask
):
    levels, lat_cells, lon_cells, features = fields.shape
    head_dim = features // HEADS
    scaling = float(head_dim) ** (-0.5)
    lat_at = lax.axis_index("lat")
    lon_at = lax.axis_index("lon")
    lat_total = lat_cells * lax.axis_size("lat")
    lat_windows = lat_cells // WLAT
    lon_windows = lon_cells // WLON
    shifted_cols = from_behind((fields[:, :, :SLON], cotangent[:, :, :SLON]), "lon", -1)
    lon_field = jnp.concatenate([fields[:, :, SLON:], shifted_cols[0]], axis=2)
    lon_cot = jnp.concatenate([cotangent[:, :, SLON:], shifted_cols[1]], axis=2)
    rows_next = from_behind((lon_field[:, :SLAT], lon_cot[:, :SLAT]), "lat", -1)
    shifted_field = jnp.concatenate([lon_field[:, SLAT:], rows_next[0]], axis=1)
    shifted_cot = jnp.concatenate([lon_cot[:, SLAT:], rows_next[1]], axis=1)
    rolled = jnp.roll(valid_mask, (-SLAT, -SLON), (0, 1))
    key_tile = (
        lax.dynamic_slice(rolled, (lat_at * lat_cells, lon_at * lon_cells), (lat_cells, lon_cells))
        == 1
    )
    my_types = lax.dynamic_slice_in_dim(window_types, lat_at * lat_windows, lat_windows)
    onehot = (
        my_types[:, None] == jnp.arange(bias_table.shape[0], dtype=jnp.int32)[None, :]
    ).astype(jnp.bfloat16)
    full_table = lax.all_gather(bias_table, "lon", axis=2, tiled=True)
    picked = jnp.einsum(
        "pt,thij->phij", onehot, full_table, preferred_element_type=jnp.float32
    ).astype(jnp.bfloat16)
    bias_wide = picked.astype(jnp.float32)
    field_wide = shifted_field.astype(jnp.float32)
    center_mean = jnp.mean(field_wide, axis=-1, keepdims=True)
    centered = field_wide - center_mean
    variance = jnp.mean(centered * centered, axis=-1, keepdims=True)
    inverse_std = lax.rsqrt(variance + EPSILON)
    hat_field = centered * inverse_std
    normed = (hat_field * norm_gain).astype(jnp.bfloat16)
    packed = jnp.dot(
        normed.reshape(-1, features), qkv_weight, preferred_element_type=jnp.float32
    ).astype(jnp.bfloat16)
    win_packed = to_windows(packed.reshape(levels, lat_cells, lon_cells, 3 * features))
    win_cot = to_windows(shifted_cot)
    key_grid = key_tile.reshape(lat_windows, WLAT, lon_windows, WLON).transpose(0, 2, 1, 3)
    key_valid = jnp.broadcast_to(
        key_grid[:, :, None], (lat_windows, lon_windows, WZ, WLAT, WLON)
    ).reshape(lat_windows, lon_windows, WIN)
    row_region = lat_at * lat_cells + jnp.arange(lat_cells, dtype=jnp.int32) >= lat_total - SLAT
    token_region = jnp.broadcast_to(
        row_region.reshape(lat_windows, 1, 1, WLAT, 1), (lat_windows, 1, WZ, WLAT, WLON)
    ).reshape(lat_windows, 1, WIN)
    allowed = key_valid[:, :, None, :] & (
        token_region[:, :, :, None] == token_region[:, :, None, :]
    )

    def group_step(pieces):
        packed_group, cot_group = pieces
        shape_heads = (lat_windows, lon_windows, WIN, HEADS, head_dim)
        queries = packed_group[..., :features].reshape(shape_heads)
        key_heads = packed_group[..., features : 2 * features].reshape(shape_heads)
        values = packed_group[..., 2 * features :].reshape(shape_heads)
        scores = product("abihd,abjhd->abhij", queries, key_heads) * scaling + bias_wide[:, None]
        scores = jnp.where(allowed[:, :, None], scores, NEGATIVE)
        row_max = jnp.max(scores, axis=-1, keepdims=True)
        exponent = jnp.exp(scores - row_max)
        soft_full = exponent / jnp.sum(exponent, axis=-1, keepdims=True)
        soft_bf = soft_full.astype(jnp.bfloat16)
        attended = (
            product("abhij,abjhd->abihd", soft_bf, values)
            .astype(jnp.bfloat16)
            .reshape(-1, features)
        )
        projected = jnp.dot(attended, proj_weight, preferred_element_type=jnp.float32).astype(
            jnp.bfloat16
        )
        grad_attended = jnp.dot(
            cot_group.reshape(-1, features), proj_weight.T, preferred_element_type=jnp.float32
        ).astype(jnp.bfloat16)
        grad_attended = grad_attended.reshape(shape_heads)
        grad_soft = product("abihd,abjhd->abhij", grad_attended, values)
        grad_values = product("abhij,abihd->abjhd", soft_bf, grad_attended).astype(jnp.bfloat16)
        grad_scores = soft_full * (
            grad_soft - jnp.sum(soft_full * grad_soft, axis=-1, keepdims=True)
        )
        bias_part = jnp.sum(grad_scores, axis=1)
        grad_scores_bf = grad_scores.astype(jnp.bfloat16)
        grad_queries = (product("abhij,abjhd->abihd", grad_scores_bf, key_heads) * scaling).astype(
            jnp.bfloat16
        )
        grad_keys = (product("abhij,abihd->abjhd", grad_scores_bf, queries) * scaling).astype(
            jnp.bfloat16
        )
        token_shape = (lat_windows, lon_windows, WIN, features)
        grad_packed = jnp.concatenate(
            [
                grad_queries.reshape(token_shape),
                grad_keys.reshape(token_shape),
                grad_values.reshape(token_shape),
            ],
            axis=-1,
        )
        return (projected.reshape(token_shape), grad_packed, bias_part)

    proj_windows, grad_windows, bias_parts = lax.map(group_step, (win_packed, win_cot))
    bias_buffer = jnp.sum(bias_parts, axis=0)
    proj_buffer = from_windows(proj_windows, levels, lat_cells, lon_cells)
    grad_packed = from_windows(grad_windows, levels, lat_cells, lon_cells).reshape(-1, 3 * features)
    grad_normed = jnp.dot(grad_packed, qkv_weight.T, preferred_element_type=jnp.float32).reshape(
        levels, lat_cells, lon_cells, features
    )
    grad_hatted = grad_normed * norm_gain
    grad_buffer = (
        inverse_std
        * (
            grad_hatted
            - jnp.mean(grad_hatted, axis=-1, keepdims=True)
            - hat_field * jnp.mean(grad_hatted * hat_field, axis=-1, keepdims=True)
        )
    ).astype(jnp.bfloat16)
    rows_prev = from_behind(
        (proj_buffer[:, lat_cells - SLAT :], grad_buffer[:, lat_cells - SLAT :]), "lat", 1
    )
    lon_proj = jnp.concatenate([rows_prev[0], proj_buffer[:, : lat_cells - SLAT]], axis=1)
    lon_grad = jnp.concatenate([rows_prev[1], grad_buffer[:, : lat_cells - SLAT]], axis=1)
    beside = from_behind(
        (lon_proj[:, :, lon_cells - SLON :], lon_grad[:, :, lon_cells - SLON :]), "lon", 1
    )
    own_proj = jnp.concatenate([beside[0], lon_proj[:, :, : lon_cells - SLON]], axis=2)
    own_grad = jnp.concatenate([beside[1], lon_grad[:, :, : lon_cells - SLON]], axis=2)
    mixed_out = (fields.astype(jnp.float32) + own_proj.astype(jnp.float32)).astype(jnp.bfloat16)
    grad_fields = (cotangent.astype(jnp.float32) + own_grad.astype(jnp.float32)).astype(
        jnp.bfloat16
    )
    grad_bias = lax.psum_scatter(
        bias_buffer.astype(jnp.bfloat16), "lon", scatter_dimension=2, tiled=True
    ).astype(jnp.float32)
    return (mixed_out, grad_fields, grad_bias)


def solution(mesh):
    in_specs = (
        P(None, "lat", "lon", None),
        P(None, "lat", "lon", None),
        P(),
        P(),
        P(),
        P(None, None, "lon", None),
        P(),
        P(),
    )
    out_specs = (
        P(None, "lat", "lon", None),
        P(None, "lat", "lon", None),
        P("lat", None, "lon", None),
    )
    return jax.shard_map(local, mesh=mesh, in_specs=in_specs, out_specs=out_specs, check_vma=False)
```

profile of v0, /device:TPU:1, one launch (start us, length us, event | category | flops | bytes accessed | tf_op | source)
XLA Modules:
  0.0 307.2 jit_solution(6898259712456541330)
XLA Ops:
  12.8 3.6 %collective-permute-start = (bf16[8,24,3,192]{3,1,2,0:T(8,128)(2,1)}, bf16[8,24,3,192]{3,1,2,0:T(8,128)(2,1)}, u32[]{:S(2)}, u32[]{:S(2)}) collective-permute-start(bf16[8,24,3,192]{3,1,2,0:T(8,128)(2,1)} %slice.74), channel_id=1, source_target_pairs={{1,0},{2,1},{3,2},{4,3},{5,4},{6,5},{7,6},{8,7},{9,8},{10,9},{11,1... | collective-permute-start | bytes 663560 | tf_op jit(solution)/shard_map/ppermute | solution.py:22
  23.3 5.8 %collective-permute-start.1 = (bf16[8,6,12,192]{3,1,2,0:T(8,128)(2,1)S(1)}, bf16[8,6,12,192]{3,1,2,0:T(8,128)(2,1)S(1)}, u32[]{:S(2)}, u32[]{:S(2)}) collective-permute-start(bf16[8,6,12,192]{3,1,2,0:T(8,128)(2,1)S(1)} %pad_maximum_fusion.5), channel_id=1, source_target_pairs={{16,0},{32,16},{48,32},{64,48},{80,64},{96,80},{112,96},{0,112},{1... | collective-permute-start | bytes 663560 | tf_op jit(solution)/shard_map/ppermute | solution.py:22
  33.3 3.6 %collective-permute-done.1 = bf16[8,6,12,192]{3,1,2,0:T(8,128)(2,1)S(1)} collective-permute-done((bf16[8,6,12,192]{3,1,2,0:T(8,128)(2,1)S(1)}, bf16[8,6,12,192]{3,1,2,0:T(8,128)(2,1)S(1)}, u32[]{:S(2)}, u32[]{:S(2)}) %collective-permute-start.1) | collective-permute-done | bytes 221216 | tf_op jit(solution)/shard_map/ppermute | solution.py:22
  41.8 3.7 %collective-permute-done.3 = bf16[8,6,12,192]{3,1,2,0:T(8,128)(2,1)} collective-permute-done((bf16[8,6,12,192]{3,1,2,0:T(8,128)(2,1)}, bf16[8,6,12,192]{3,1,2,0:T(8,128)(2,1)}, u32[]{:S(2)}, u32[]{:S(2)}) %collective-permute-start.3) | collective-permute-done | bytes 221216 | tf_op jit(solution)/shard_map/ppermute | solution.py:22
  55.5 4.3 %convolution_convert_fusion.4 = bf16[2304,576]{0,1:T(8,128)(2,1)} fusion(bf16[192,576]{1,0:T(8,128)(2,1)S(1)} %copy-done, f32[2304,192]{1,0:T(8,128)} %reshape.137, f32[192]{0:T(256)S(1)} %copy-done.21, f32[2304]{0:T(1024)S(1)} %copy-done.19, f32[2304]{0:T(1024)S(1)} %copy-done.20), kind=kOutput, calls=%fused_computation.38 | convolution fusion | flops 512704512 | bytes 4664064 | tf_op jit(solution)/shard_map/dot_general | solution.py:84
  59.8 4.0 %copy.94 = bf16[2304,576]{1,0:T(8,128)(2,1)S(1)} copy(bf16[2304,576]{0,1:T(8,128)(2,1)} %convolution_convert_fusion.4) | data formatting | bytes 5308416 | tf_op jit(solution)/shard_map/convert_element_type | solution.py:86
  67.2 6.9 %copy.95 = bf16[4,2,2,2,12,6,576]{6,2,5,4,3,1,0:T(2,128)(2,1)} copy(bf16[4,2,2,2,12,6,576]{6,5,2,4,1,3,0:T(8,128)(2,1)} %bitcast.131) | data formatting | bytes 5308416 | tf_op jit(solution)/shard_map/transpose | solution.py:34
  76.0 6.0 %fusion.22 = f32[2,6,144,144]{3,0,2,1:T(2,128)S(1)} fusion(bf16[21,6,144,144]{3,0,2,1:T(8,128)(2,1)} %all-gather.2.cloned.1.call-done, s32[2]{0:T(128)S(1)} %copy-done.23), kind=kOutput, calls=%fused_computation.48 | convolution fusion | flops 10948650 | bytes 6220808 | tf_op jit(solution)/shard_map/pt,thij->phij/dot_general | solution.py:73
  84.5 127.0 %while.15 = (s32[]{:T(128)}, bf16[4,2,2,144,192]{4,2,3,1,0:T(2,128)(2,1)}, bf16[4,2,2,144,576]{4,2,3,1,0:T(2,128)(2,1)}, f32[4,2,6,144,144]{4,3,2,1,0:T(8,128)},...) while((s32[]{:T(128)}, ...), condition=%wide.region_7.8_spmd.clone, body=%wide.region_2.7_spmd.clone.sunk | while | flops 287204096 | bytes 51840792 | solution.py:149
  88.3 4.8 %fusion.91 = (f32[2,2,6,144]{3,2,1,0:T(8,128)S(1)}, f32[2,2,6,144,144]{3,4,2,1,0:T(8,128)}) fusion(f32[2,6,144,144]{2,3,1,0:T(8,128)} %get-tuple-element.274, pred[2,2,144,144]{2,3,1,0:T(8,128)(4,1)S(1)} %broadcast_and_fusion.2, bf16[2,2,144,6,32]{2,4,3,1,0:T(8,128)(2,1)S(1)} %bitcast.123, bf16[2,2,144,6,32]{2,4,3,1,0:T(8,128)(2,1)S(1)} %bitcast.125), kind=kOutput, calls=%fused_computation.84.clone.1 | convolution fusion | flops 34338960 | bytes 3525120 | tf_op jit(solution)/shard_map/while/body/eval_jaxpr/sub | solution.py:110
  99.3 3.6 %convolution_convert_fusion.11 = bf16[2,2,6,32,144]{4,3,2,1,0:T(8,128)(2,1)} fusion(bf16[2,2,144,6,32]{2,1,0,4,3:T(2,128)(2,1)S(1)} %reshape.153, f32[2,2,6,144,144]{3,4,2,1,0:T(8,128)} %get-tuple-element.239, f32[2,2,6,144]{3,2,1,0:T(8,128)S(1)} %get-tuple-element.240), kind=kOutput, calls=%fused_computation.18.clone.1 | convolution fusion | flops 32956416 | bytes 2446848 | tf_op jit(solution)/shard_map/while/body/eval_jaxpr/abhij,abihd->abjhd/dot_general | solution.py:26
  120.0 4.8 %fusion.91 = (f32[2,2,6,144]{3,2,1,0:T(8,128)S(1)}, f32[2,2,6,144,144]{3,4,2,1,0:T(8,128)}) fusion(f32[2,6,144,144]{2,3,1,0:T(8,128)} %get-tuple-element.274, pred[2,2,144,144]{2,3,1,0:T(8,128)(4,1)S(1)} %broadcast_and_fusion.2, bf16[2,2,144,6,32]{2,4,3,1,0:T(8,128)(2,1)S(1)} %bitcast.123, bf16[2,2,144,6,32]{2,4,3,1,0:T(8,128)(2,1)S(1)} %bitcast.125), kind=kOutput, calls=%fused_computation.84.clone.1 | convolution fusion | flops 34338960 | bytes 3525120 | tf_op jit(solution)/shard_map/while/body/eval_jaxpr/sub | solution.py:110
  131.0 3.6 %convolution_convert_fusion.11 = bf16[2,2,6,32,144]{4,3,2,1,0:T(8,128)(2,1)} fusion(bf16[2,2,144,6,32]{2,1,0,4,3:T(2,128)(2,1)S(1)} %reshape.153, f32[2,2,6,144,144]{3,4,2,1,0:T(8,128)} %get-tuple-element.239, f32[2,2,6,144]{3,2,1,0:T(8,128)S(1)} %get-tuple-element.240), kind=kOutput, calls=%fused_computation.18.clone.1 | convolution fusion | flops 32956416 | bytes 2446848 | tf_op jit(solution)/shard_map/while/body/eval_jaxpr/abhij,abihd->abjhd/dot_general | solution.py:26
  151.7 4.8 %fusion.91 = (f32[2,2,6,144]{3,2,1,0:T(8,128)S(1)}, f32[2,2,6,144,144]{3,4,2,1,0:T(8,128)}) fusion(f32[2,6,144,144]{2,3,1,0:T(8,128)} %get-tuple-element.274, pred[2,2,144,144]{2,3,1,0:T(8,128)(4,1)S(1)} %broadcast_and_fusion.2, bf16[2,2,144,6,32]{2,4,3,1,0:T(8,128)(2,1)S(1)} %bitcast.123, bf16[2,2,144,6,32]{2,4,3,1,0:T(8,128)(2,1)S(1)} %bitcast.125), kind=kOutput, calls=%fused_computation.84.clone.1 | convolution fusion | flops 34338960 | bytes 3525120 | tf_op jit(solution)/shard_map/while/body/eval_jaxpr/sub | solution.py:110
  162.7 3.6 %convolution_convert_fusion.11 = bf16[2,2,6,32,144]{4,3,2,1,0:T(8,128)(2,1)} fusion(bf16[2,2,144,6,32]{2,1,0,4,3:T(2,128)(2,1)S(1)} %reshape.153, f32[2,2,6,144,144]{3,4,2,1,0:T(8,128)} %get-tuple-element.239, f32[2,2,6,144]{3,2,1,0:T(8,128)S(1)} %get-tuple-element.240), kind=kOutput, calls=%fused_computation.18.clone.1 | convolution fusion | flops 32956416 | bytes 2446848 | tf_op jit(solution)/shard_map/while/body/eval_jaxpr/abhij,abihd->abjhd/dot_general | solution.py:26
  183.4 4.8 %fusion.91 = (f32[2,2,6,144]{3,2,1,0:T(8,128)S(1)}, f32[2,2,6,144,144]{3,4,2,1,0:T(8,128)}) fusion(f32[2,6,144,144]{2,3,1,0:T(8,128)} %get-tuple-element.274, pred[2,2,144,144]{2,3,1,0:T(8,128)(4,1)S(1)} %broadcast_and_fusion.2, bf16[2,2,144,6,32]{2,4,3,1,0:T(8,128)(2,1)S(1)} %bitcast.123, bf16[2,2,144,6,32]{2,4,3,1,0:T(8,128)(2,1)S(1)} %bitcast.125), kind=kOutput, calls=%fused_computation.84.clone.1 | convolution fusion | flops 34338960 | bytes 3525120 | tf_op jit(solution)/shard_map/while/body/eval_jaxpr/sub | solution.py:110
  194.4 3.6 %convolution_convert_fusion.11 = bf16[2,2,6,32,144]{4,3,2,1,0:T(8,128)(2,1)} fusion(bf16[2,2,144,6,32]{2,1,0,4,3:T(2,128)(2,1)S(1)} %reshape.153, f32[2,2,6,144,144]{3,4,2,1,0:T(8,128)} %get-tuple-element.239, f32[2,2,6,144]{3,2,1,0:T(8,128)S(1)} %get-tuple-element.240), kind=kOutput, calls=%fused_computation.18.clone.1 | convolution fusion | flops 32956416 | bytes 2446848 | tf_op jit(solution)/shard_map/while/body/eval_jaxpr/abhij,abihd->abjhd/dot_general | solution.py:26
  215.9 3.9 %reduce_sum.76 = bf16[2,6,144,144]{3,2,1,0:T(8,128)(2,1)S(1)} reduce(f32[4,2,6,144,144]{4,3,2,1,0:T(8,128)} %get-tuple-element.54, f32[]{:T(128)} %constant.31.clone.1), dimensions={0}, to_apply=%region_10.11 | reduce | flops 746496 | bytes 4478980 | tf_op jit(solution)/shard_map/reduce_sum | solution.py:150
  222.8 4.4 %copy.119 = bf16[4,2,2,12,2,6,576]{6,3,2,5,4,1,0:T(8,128)(2,1)} copy(bf16[4,2,2,12,2,6,576]{6,4,5,3,1,2,0:T(2,128)(2,1)} %bitcast.140) | data formatting | bytes 5308416 | tf_op jit(solution)/shard_map/dot_general | solution.py:153
  227.2 6.6 %reshape.149 = bf16[8,24,12,576]{3,1,2,0:T(8,128)(2,1)} reshape(bf16[4,2,2,12,2,6,576]{6,3,2,5,4,1,0:T(8,128)(2,1)} %copy.119) | data formatting | bytes 5308416 | tf_op jit(solution)/shard_map/dot_general | solution.py:153
  233.8 3.5 %multiply_reduce_fusion.3 = (f32[8,24,12]{1,2,0:T(8,128)S(1)}, f32[8,24,12]{1,2,0:T(8,128)S(1)}, f32[8,24,12,192]{3,1,2,0:T(8,128)S(1)}) fusion(f32[192]{0:T(256)S(1)} %copy-done.21, f32[8,24,12]{1,2,0:T(8,128)S(1)} %copy-done.17, f32[8,24,12]{1,2,0:T(8,128)S(1)} %broadcast_multiply_fusion.2, bf16[8,6,12,192]{3,1,2,0:T(8,128)(2,1)S(1)} %copy-done.9, ...), kind=kOutput, calls=%fused_computation.45 | convolution fusion | flops 514027008 | bytes 5567232 | tf_op jit(solution)/shard_map/dot_general | solution.py:153
  240.4 10.2 %collective-permute-done.4 = bf16[8,6,12,192]{3,0,2,1:T(8,128)(2,1)S(1)} collective-permute-done((bf16[8,6,12,192]{3,0,2,1:T(8,128)(2,1)}, bf16[8,6,12,192]{3,0,2,1:T(8,128)(2,1)S(1)}, u32[]{:S(2)}, u32[]{:S(2)}) %collective-permute-start.4) | collective-permute-done | bytes 221216 | tf_op jit(solution)/shard_map/ppermute | solution.py:22
  250.7 18.7 %collective-permute-done.6 = bf16[8,6,12,192]{3,1,2,0:T(8,128)(2,1)S(1)} collective-permute-done((bf16[8,6,12,192]{3,1,2,0:T(8,128)(2,1)S(1)}, bf16[8,6,12,192]{3,1,2,0:T(8,128)(2,1)S(1)}, u32[]{:S(2)}, u32[]{:S(2)}) %collective-permute-start.6) | collective-permute-done | bytes 221216 | tf_op jit(solution)/shard_map/ppermute | solution.py:22
  275.4 23.4 %reduce-scatter.2.cloned.1.call-done = bf16[2,6,9,144]{3,1,0,2:T(8,128)(2,1)} async-done(((bf16[2,6,144,144]{3,1,0,2:T(8,128)(2,1)}), bf16[2,6,9,144]{3,1,0,2:T(8,128)(2,1)}) %reduce-scatter.2.cloned.1.call-update) | async-done | bytes 31120 | tf_op jit(solution)/shard_map/reduce_scatter | solution.py:179
  (230 shorter events, 149.8 us)
Async XLA Ops:
  7.2 48.3 %copy-start = (bf16[192,576]{1,0:T(8,128)(2,1)S(1)}, bf16[192,576]{1,0:T(8,128)(2,1)}, u32[]{:S(2)}) copy-start(bf16[192,576]{1,0:T(8,128)(2,1)} %param.13) | copy-start | bytes 663556
  7.2 11.0 %copy-start.10 = (bf16[8,24,12,192]{3,1,2,0:T(8,128)(2,1)S(1)}, bf16[8,24,12,192]{3,1,2,0:T(8,128)(2,1)}, u32[]{:S(2)}) copy-start(bf16[8,24,12,192]{3,1,2,0:T(8,128)(2,1)} %param.10) | copy-start | bytes 2654212
  7.2 68.8 %all-gather.2.cloned.1.call-start = ((), (), s32[]{:S(2)}) async-start(), calls=%async_computation.1 | async-start | bytes 11280384 | tf_op jit(solution)/shard_map/all_gather | solution.py:72
  7.9 290.9 %reduce-scatter.2.cloned.1.call-start = ((), (), s32[]{:S(2)}) async-start(), calls=%async_computation.2 | async-start | bytes 1253376 | tf_op jit(solution)/shard_map/reduce_scatter | solution.py:179
  9.7 8.9 %slice-start = ((s32[192,192]{1,0:T(8,128)}), s32[6,192]{1,0:T(8,128)S(1)}, s32[]{:S(2)}) async-start(s32[192,192]{1,0:T(8,128)} %param.17), calls=%async_computation.3 | async-start | bytes 16384 | tf_op jit(solution)/shard_map/jit(_roll_static)/slice | solution.py:63
  9.7 19.4 %collective-permute-start.2 = (bf16[8,24,3,192]{3,1,2,0:T(8,128)(2,1)}, bf16[8,24,3,192]{3,1,2,0:T(8,128)(2,1)S(1)}, u32[]{:S(2)}, u32[]{:S(2)}) collective-permute-start(bf16[8,24,3,192]{3,1,2,0:T(8,128)(2,1)} %slice.82), channel_id=1, source_target_pairs={{1,0},{2,1},{3,2},{4,3},{5,4},{6,5},{7,6},{8,7},{9,8},{10,9},{11,1... | collective-permute-start | bytes 663560 | tf_op jit(solution)/shard_map/ppermute | solution.py:22
  12.8 9.5 %collective-permute-start = (bf16[8,24,3,192]{3,1,2,0:T(8,128)(2,1)}, bf16[8,24,3,192]{3,1,2,0:T(8,128)(2,1)}, u32[]{:S(2)}, u32[]{:S(2)}) collective-permute-start(bf16[8,24,3,192]{3,1,2,0:T(8,128)(2,1)} %slice.74), channel_id=1, source_target_pairs={{1,0},{2,1},{3,2},{4,3},{5,4},{6,5},{7,6},{8,7},{9,8},{10,9},{11,1... | collective-permute-start | bytes 663560 | tf_op jit(solution)/shard_map/ppermute | solution.py:22
  23.3 13.6 %collective-permute-start.1 = (bf16[8,6,12,192]{3,1,2,0:T(8,128)(2,1)S(1)}, bf16[8,6,12,192]{3,1,2,0:T(8,128)(2,1)S(1)}, u32[]{:S(2)}, u32[]{:S(2)}) collective-permute-start(bf16[8,6,12,192]{3,1,2,0:T(8,128)(2,1)S(1)} %pad_maximum_fusion.5), channel_id=1, source_target_pairs={{16,0},{32,16},{48,32},{64,48},{80,64},{96,80},{112,96},{0,112},{1... | collective-permute-start | bytes 663560 | tf_op jit(solution)/shard_map/ppermute | solution.py:22
  30.0 15.5 %collective-permute-start.3 = (bf16[8,6,12,192]{3,1,2,0:T(8,128)(2,1)}, bf16[8,6,12,192]{3,1,2,0:T(8,128)(2,1)}, u32[]{:S(2)}, u32[]{:S(2)}) collective-permute-start(bf16[8,6,12,192]{3,1,2,0:T(8,128)(2,1)} %pad_maximum_fusion.4), channel_id=1, source_target_pairs={{16,0},{32,16},{48,32},{64,48},{80,64},{96,80},{112,96},{0,112},{1... | collective-permute-start | bytes 663560 | tf_op jit(solution)/shard_map/ppermute | solution.py:22
  31.7 20.9 %copy-start.3 = (bf16[8,18,12,192]{3,1,2,0:T(8,128)(2,1)}, bf16[8,18,12,192]{3,1,2,0:T(8,128)(2,1)S(1)}, u32[]{:S(2)}) copy-start(bf16[8,18,12,192]{3,1,2,0:T(8,128)(2,1)S(1)} %slice_maximum_fusion.1) | copy-start | bytes 1990660
  40.2 6.7 %copy-start.16 = (f32[8,24,12]{1,2,0:T(8,128)}, f32[8,24,12]{1,2,0:T(8,128)S(1)}, u32[]{:S(2)}) copy-start(f32[8,24,12]{1,2,0:T(8,128)S(1)} %add_rsqrt_fusion) | copy-start | bytes 27652
  47.6 5.1 %copy-start.8 = (bf16[8,6,12,192]{3,1,2,0:T(8,128)(2,1)S(1)}, bf16[8,6,12,192]{3,1,2,0:T(8,128)(2,1)}, u32[]{:S(2)}) copy-start(bf16[8,6,12,192]{3,1,2,0:T(8,128)(2,1)} %copy-done.7) | copy-start | bytes 663556
  67.2 8.8 %copy-start.23 = (s32[2]{0:T(128)S(1)}, s32[2]{0:T(128)}, u32[]{:S(2)}) copy-start(s32[2]{0:T(128)} %dynamic_slice.15) | copy-start | bytes 28
  110.0 5.1 %copy-start.1 = (f32[1,2,6,144,144]{4,3,2,1,0:T(8,128)S(1)}, f32[1,2,6,144,144]{4,3,2,1,0:T(8,128)}, u32[]{:S(2)}) copy-start(f32[1,2,6,144,144]{4,3,2,1,0:T(8,128)} %copy.160) | copy-start | bytes 2985988 | tf_op jit(solution)/shard_map/while
  141.7 5.1 %copy-start.1 = (f32[1,2,6,144,144]{4,3,2,1,0:T(8,128)S(1)}, f32[1,2,6,144,144]{4,3,2,1,0:T(8,128)}, u32[]{:S(2)}) copy-start(f32[1,2,6,144,144]{4,3,2,1,0:T(8,128)} %copy.160) | copy-start | bytes 2985988 | tf_op jit(solution)/shard_map/while
  173.4 5.1 %copy-start.1 = (f32[1,2,6,144,144]{4,3,2,1,0:T(8,128)S(1)}, f32[1,2,6,144,144]{4,3,2,1,0:T(8,128)}, u32[]{:S(2)}) copy-start(f32[1,2,6,144,144]{4,3,2,1,0:T(8,128)} %copy.160) | copy-start | bytes 2985988 | tf_op jit(solution)/shard_map/while
  221.2 29.4 %collective-permute-start.4 = (bf16[8,6,12,192]{3,0,2,1:T(8,128)(2,1)}, bf16[8,6,12,192]{3,0,2,1:T(8,128)(2,1)S(1)}, u32[]{:S(2)}, u32[]{:S(2)}) collective-permute-start(bf16[8,6,12,192]{3,0,2,1:T(8,128)(2,1)} %slice.105), channel_id=1, source_target_pairs={{112,0},{0,16},{16,32},{32,48},{48,64},{64,80},{80,96},{96,112},{1... | collective-permute-start | bytes 663560 | tf_op jit(solution)/shard_map/ppermute | solution.py:22
  227.2 6.6 %copy-start.4 = (bf16[8,18,12,192]{3,1,2,0:T(8,128)(2,1)S(1)}, bf16[8,18,12,192]{3,1,2,0:T(8,128)(2,1)}, u32[]{:S(2)}) copy-start(bf16[8,18,12,192]{3,1,2,0:T(8,128)(2,1)} %copy-done.3) | copy-start | bytes 1990660
  227.2 6.6 %copy-start.9 = (bf16[8,6,12,192]{3,1,2,0:T(8,128)(2,1)S(1)}, bf16[8,6,12,192]{3,1,2,0:T(8,128)(2,1)}, u32[]{:S(2)}) copy-start(bf16[8,6,12,192]{3,1,2,0:T(8,128)(2,1)} %copy-done.7) | copy-start | bytes 663556
  227.2 6.6 %copy-start.17 = (f32[8,24,12]{1,2,0:T(8,128)S(1)}, f32[8,24,12]{1,2,0:T(8,128)}, u32[]{:S(2)}) copy-start(f32[8,24,12]{1,2,0:T(8,128)} %copy-done.16) | copy-start | bytes 27652
  239.0 30.7 %copy-start.11 = (bf16[8,24,12,192]{3,1,2,0:T(8,128)(2,1)S(1)}, bf16[8,24,12,192]{3,1,2,0:T(8,128)(2,1)}, u32[]{:S(2)}) copy-start(bf16[8,24,12,192]{3,1,2,0:T(8,128)(2,1)} %param.10) | copy-start | bytes 2654212
  239.0 30.4 %collective-permute-start.6 = (bf16[8,6,12,192]{3,1,2,0:T(8,128)(2,1)S(1)}, bf16[8,6,12,192]{3,1,2,0:T(8,128)(2,1)S(1)}, u32[]{:S(2)}, u32[]{:S(2)}) collective-permute-start(bf16[8,6,12,192]{3,1,2,0:T(8,128)(2,1)S(1)} %slice.107), channel_id=1, source_target_pairs={{112,0},{0,16},{16,32},{32,48},{48,64},{64,80},{80,96},{96,112},{1... | collective-permute-start | bytes 663560 | tf_op jit(solution)/shard_map/ppermute | solution.py:22
  250.7 19.0 %collective-permute-start.5 = (bf16[8,24,3,192]{3,0,2,1:T(8,128)(2,1)S(1)}, bf16[8,24,3,192]{3,0,2,1:T(8,128)(2,1)S(1)}, u32[]{:S(2)}, u32[]{:S(2)}) collective-permute-start(bf16[8,24,3,192]{3,0,2,1:T(8,128)(2,1)S(1)} %pad_maximum_fusion.7), channel_id=1, source_target_pairs={{15,0},{0,1},{1,2},{2,3},{3,4},{4,5},{5,6},{6,7},{7,8},{8,9},{9,10... | collective-permute-start | bytes 663560 | tf_op jit(solution)/shard_map/ppermute | solution.py:22
  269.6 4.1 %collective-permute-start.7 = (bf16[8,24,3,192]{3,1,2,0:T(8,128)(2,1)S(1)}, bf16[8,24,3,192]{3,1,2,0:T(8,128)(2,1)S(1)}, u32[]{:S(2)}, u32[]{:S(2)}) collective-permute-start(bf16[8,24,3,192]{3,1,2,0:T(8,128)(2,1)S(1)} %pad_maximum_fusion.6), channel_id=1, source_target_pairs={{15,0},{0,1},{1,2},{2,3},{3,4},{4,5},{5,6},{6,7},{7,8},{8,9},{9,10... | collective-permute-start | bytes 663560 | tf_op jit(solution)/shard_map/ppermute | solution.py:22
  (21 other events, 51.0 us)
Sparse Core Ops, SparseCore 0:
  9.7 66.3 all-gather.1
  221.4 77.3 reduce-scatter.1
where the time goes:
time: 311 us; the launch traced here: 307 us
  local copies, waits for them, and re-layouts  119 us (38%)
  matrix products  66.2 us (21%)
  waiting for transfers between devices  63.8 us (21%)
  other arithmetic  28.6 us (9%)
  between operations  14.5 us (5%)
  starting transfers between devices  14.4 us (5%)
    dynamic_update_slice x20, local copies, waits for them, and re-layouts, local(): lax.map(group_step, (win_packed, win_cot))  45.2 us
    ppermute x8, waiting for transfers between devices, from_behind(): return lax.ppermute(block, axis, route)  37.8 us
    dot_general x20, matrix products, product(): jnp.einsum(pattern, operand_a, operand_b, preferred_element_type=jnp.floa...  31.1 us
    reduce_scatter x1, waiting for transfers between devices, local(): lax.psum_scatter(bias_buffer.astype(jnp.bfloat16), 'lon', scatter_dimensi...  23.4 us
    sub x4, matrix products, group_step(): exponent = jnp.exp(scores - row_max)  19.1 us
    ppermute x8, starting transfers between devices, from_behind(): return lax.ppermute(block, axis, route)  14.3 us
    dynamic_slice x12, local copies, waits for them, and re-layouts, local(): lax.map(group_step, (win_packed, win_cot))  13.3 us
    dot_general x2, local copies, waits for them, and re-layouts, local(): jnp.dot(grad_packed, qkv_weight.T, preferred_element_type=jnp.float32)  11 us
  transfers between devices with their start and end apart: 10, of which 7 were waited for; matrix products, arithmetic and copies ran while one was open for 22% of the time, Pallas kernels for 0%

commit v1 on v0

v1 whole, which is shorter than its diff:
```python
import functools

import jax
import jax.numpy as jnp
import numpy as np
from jax import lax
from jax.experimental import pallas as pl
from jax.experimental.pallas import tpu as pltpu
from jax.sharding import PartitionSpec as P

HEADS = 6
WZ = 2
WLAT = 12
WLON = 6
WIN = 144
SLAT = 6
SLON = 3
HEAD_DIM = 32
MAIN = 128
REST = WIN - MAIN
LANES = 896
ROWS = 64

NEGATIVE = -1e30
EPSILON = 1e-05
LOG2E = 1.4426950408889634
SCALE = float(HEAD_DIM) ** (-0.5)

F32 = jnp.float32
BF16 = jnp.bfloat16


def nn(a, b):
    return lax.dot_general(a, b, (((1,), (0,)), ((), ())), preferred_element_type=F32)


def nt(a, b):
    return lax.dot_general(a, b, (((1,), (1,)), ((), ())), preferred_element_type=F32)


def tn(a, b):
    return lax.dot_general(a, b, (((0,), (0,)), ((), ())), preferred_element_type=F32)


def lane_of(head, query):
    return np.where(query < MAIN, head * MAIN + query, HEADS * MAIN + head * REST + query - MAIN)


def window_picks():
    pick = np.zeros((2, WIN, WZ, WLAT, 16), np.float32)
    for w in range(2):
        for t in range(WIN):
            z, r, c = t // (WLAT * WLON), (t // WLON) % WLAT, t % WLON
            pick[w, t, z, r, SLON + WLON * w + c] = 1
    return pick.reshape(2, WIN, WZ * WLAT * 16)


def bias_picks(parts):
    per = WIN // parts
    pick = np.zeros((parts, ROWS, LANES), np.float32)
    for k in range(parts):
        for h in range(HEADS):
            for r in range(per):
                pick[k, h * per + r, lane_of(h, k * per + r)] = 1
    return pick.reshape(parts * ROWS, LANES)


def head_blocks(tokens, head_masks):
    pieces = [tokens[:MAIN] * head_masks[h] for h in range(HEADS)]
    pieces += [tokens[MAIN:] * head_masks[h] for h in range(HEADS)]
    pieces.append(jnp.zeros((LANES - HEADS * WIN, tokens.shape[1]), tokens.dtype))
    return jnp.concatenate(pieces, axis=0)


def own_heads(wide):
    main, rest = [], []
    for h in range(HEADS):
        rows = wide[h * HEAD_DIM : (h + 1) * HEAD_DIM]
        main.append(rows[:, h * MAIN : (h + 1) * MAIN])
        left = HEADS * MAIN + h * REST
        rest.append(rows[:, left : left + REST])
    return jnp.concatenate(
        [jnp.concatenate(main, axis=0), jnp.concatenate(rest, axis=0)], axis=1
    )


def kernel(
    at_ref,
    fields_ref,
    cot_ref,
    east_f_ref,
    east_c_ref,
    south_f_ref,
    south_c_ref,
    corner_f_ref,
    corner_c_ref,
    gain_ref,
    qkv_ref,
    proj_ref,
    bias_ref,
    valid_ref,
    pick_ref,
    unpick_ref,
    bias_pick_ref,
    eye_ref,
    proj_out_ref,
    grad_out_ref,
    bias_out_ref,
    weights,
    bias_t,
    bias_sum,
    tile,
):
    step = pl.program_id(0)
    features = fields_ref.shape[-1]

    @pl.when(step == 0)
    def prepare():
        eye = eye_ref[...]
        for n in range(3):
            weights[n] = qkv_ref[:, n * features : (n + 1) * features]
        weights[3] = nt(eye, weights[1]).astype(BF16)
        weights[4] = nt(eye, weights[2]).astype(BF16)
        weights[5] = nt(eye, proj_ref[...]).astype(BF16)
        bias_sum[...] = jnp.zeros_like(bias_sum)
        tile[...] = jnp.zeros_like(tile)
        for b in range(2):
            table = bias_ref[:, b].reshape(-1, WIN)
            wide = tn(table, bias_pick_ref[...]) * LOG2E
            if b == 0:
                bias_t[0] = wide
            else:
                key = lax.broadcasted_iota(jnp.int32, (WIN, 1), 0)
                lane = lax.broadcasted_iota(jnp.int32, (1, LANES), 1)
                query = jnp.where(
                    lane < HEADS * MAIN, lane % MAIN, MAIN + (lane - HEADS * MAIN) % REST
                )
                key_row = (key // WLON) % WLAT
                query_row = (query // WLON) % WLAT
                last = at_ref[0] == 7
                same = (key_row < SLAT) == (query_row < SLAT)
                lat_rows = valid_ref.shape[0]
                valid_rows = jnp.concatenate(
                    [valid_ref[lat_rows - SLAT :, :], valid_ref[:SLAT, :]], axis=0
                ).astype(F32)
                row_pick = (
                    key_row == lax.broadcasted_iota(jnp.int32, (WIN, WLAT), 1)
                ).astype(F32)
                key_valid = nn(row_pick, valid_rows)
                column = lax.broadcasted_iota(jnp.int32, (WIN, valid_ref.shape[1]), 1)
                for w in range(2):
                    wanted = at_ref[1] * (2 * WLON) + SLON + WLON * w + key % WLON
                    wanted = jnp.where(wanted >= valid_ref.shape[1], wanted - valid_ref.shape[1], wanted)
                    is_valid = (
                        jnp.sum(jnp.where(column == wanted, key_valid, 0.0), axis=1, keepdims=True)
                        > 0.5
                    )
                    allowed = jnp.logical_and(same, is_valid) | jnp.logical_not(last)
                    bias_t[1 + w] = jnp.where(allowed, wide, NEGATIVE)

    gain = gain_ref[...]
    eye = eye_ref[...]
    lane_head = lax.broadcasted_iota(jnp.int32, (1, features), 1) // HEAD_DIM
    head_masks = [(lane_head == h).astype(F32).astype(BF16) for h in range(HEADS)]
    for b in range(2):
        for n, (own, east, south, corner) in enumerate(
            (
                (fields_ref, east_f_ref, south_f_ref, corner_f_ref),
                (cot_ref, east_c_ref, south_c_ref, corner_c_ref),
            )
        ):
            wide = 2 * WLON
            if b == 0:
                tile[n, :, :, :wide] = own[:, SLAT : SLAT + WLAT]
                tile[n, :, :, wide : wide + SLON] = east[:, SLAT : SLAT + WLAT]
            else:
                tile[n, :, :SLAT, :wide] = own[:, SLAT + WLAT :]
                tile[n, :, :SLAT, wide : wide + SLON] = east[:, SLAT + WLAT :]
                tile[n, :, SLAT:, :wide] = south[...]
                tile[n, :, SLAT:, wide : wide + SLON] = corner[...]
        flat_f = tile[0].reshape(-1, features)
        flat_c = tile[1].reshape(-1, features)
        proj_tile = None
        grads = []
        bias_grad = None
        for w in range(2):
            pick = pick_ref[w]
            x = nn(pick, flat_f)
            cot = nn(pick, flat_c).astype(BF16)
            mean = jnp.mean(x, axis=1, keepdims=True)
            centered = x - mean
            variance = jnp.mean(centered * centered, axis=1, keepdims=True)
            inverse = lax.rsqrt(variance + EPSILON)
            hat = centered * inverse
            normed = (hat * gain).astype(BF16)
            queries = nn(normed, weights[0]).astype(BF16)
            keys = nn(normed, weights[1]).astype(BF16)
            values = nn(normed, weights[2]).astype(BF16)
            keys_t = nt(weights[3], normed).astype(BF16)
            values_t = nt(weights[4], normed).astype(BF16)
            grad_att = nt(cot, proj_ref[...]).astype(BF16)
            q_blocks = head_blocks(queries, head_masks)
            g_blocks = head_blocks(grad_att, head_masks)
            scores = nt(keys, q_blocks) * (SCALE * LOG2E) + bias_t[b * (1 + w)]
            exponent = jnp.exp2(scores - jnp.max(scores, axis=0, keepdims=True))
            soft = exponent * (1.0 / jnp.sum(exponent, axis=0, keepdims=True))
            soft_bf = soft.astype(BF16)
            grad_soft = nt(values, g_blocks)
            delta = jnp.sum(soft * grad_soft, axis=0, keepdims=True)
            grad_scores = soft * (grad_soft - delta)
            bias_grad = grad_scores if bias_grad is None else bias_grad + grad_scores
            grad_bf = grad_scores.astype(BF16)
            grad_values = nn(soft_bf, g_blocks).astype(BF16)
            grad_keys = (nn(grad_bf, q_blocks) * SCALE).astype(BF16)
            attended_t = own_heads(nn(values_t, soft_bf)).astype(BF16)
            grad_queries_t = (own_heads(nn(keys_t, grad_bf)) * SCALE).astype(BF16)
            projected_t = nn(weights[5], attended_t).astype(BF16)
            grad_queries = nt(eye[:WIN, :WIN], grad_queries_t).astype(BF16)
            part = nt(unpick_ref[w], projected_t)
            proj_tile = part if proj_tile is None else proj_tile + part
            grad_normed = (
                nt(grad_queries, weights[0]) + nt(grad_keys, weights[1]) + nt(grad_values, weights[2])
            )
            grad_hat = grad_normed * gain
            grad_x = inverse * (
                grad_hat
                - jnp.mean(grad_hat, axis=1, keepdims=True)
                - hat * jnp.mean(grad_hat * hat, axis=1, keepdims=True)
            )
            grads.append(grad_x.astype(BF16))
        bias_sum[b] += bias_grad
        grad_tile = nn(unpick_ref[0], grads[0]) + nn(unpick_ref[1], grads[1])
        proj_out_ref[:, b] = proj_tile.astype(BF16).reshape(WZ, WLAT, 16, features)
        grad_out_ref[:, b] = grad_tile.astype(BF16).reshape(WZ, WLAT, 16, features)

    @pl.when(step == pl.num_programs(0) - 1)
    def finish():
        for b in range(2):
            rows = nt(bias_pick_ref[...], bias_sum[b].astype(BF16)).astype(BF16)
            bias_out_ref[:, b] = rows.reshape(-1, ROWS, WIN)


def attend(at, fields, cotangent, halos, gain, qkv_weight, proj_weight, bias, valid_mask, parts):
    levels, lat_cells, lon_cells, features = fields.shape
    picks = window_picks()
    constants = (
        jnp.asarray(picks, BF16),
        jnp.asarray(picks.transpose(0, 2, 1), BF16),
        jnp.asarray(bias_picks(parts), BF16),
        jnp.asarray(np.eye(features), BF16),
    )

    def by_level(array):
        return pl.BlockSpec((WZ,) + array.shape[1:], lambda g: (g,) + (0,) * (array.ndim - 1))

    def whole(array):
        return pl.BlockSpec(array.shape, lambda g: (0,) * array.ndim)

    tiled = (fields, cotangent) + tuple(halos)
    fixed = (gain, qkv_weight, proj_weight, bias, valid_mask) + constants
    out_tile = jax.ShapeDtypeStruct((levels, 2, WLAT, 16, features), BF16)
    bias_out = jax.ShapeDtypeStruct(bias.shape, BF16)
    return pl.pallas_call(
        kernel,
        grid=(levels // WZ,),
        out_shape=(out_tile, out_tile, bias_out),
        in_specs=[pl.BlockSpec(memory_space=pltpu.SMEM)]
        + [by_level(a) for a in tiled]
        + [whole(a) for a in fixed],
        out_specs=(by_level(out_tile), by_level(out_tile), whole(bias_out)),
        scratch_shapes=[
            pltpu.VMEM((6, features, features), BF16),
            pltpu.VMEM((3, WIN, LANES), F32),
            pltpu.VMEM((2, WIN, LANES), F32),
            pltpu.VMEM((2, WZ, WLAT, 16, features), BF16),
        ],
        compiler_params=pltpu.CompilerParams(vmem_limit_bytes=48 * 1024 * 1024),
    )(at, *tiled, *fixed)


def shift(block, lat_step, lon_step):
    lats, lons = lax.axis_size("lat"), lax.axis_size("lon")
    route = [
        (((a + lat_step) % lats) * lons + (o + lon_step) % lons, a * lons + o)
        for a in range(lats)
        for o in range(lons)
    ]
    return lax.ppermute(block, ("lat", "lon"), route)


def local(
    fields, cotangent, norm_gain, qkv_weight, proj_weight, bias_table, window_types, valid_mask
):
    levels, lat_cells, lon_cells, features = fields.shape
    lat_at = lax.axis_index("lat")
    lon_at = lax.axis_index("lon")
    parts = lax.axis_size("lon")
    per = WIN // parts
    east = [shift(a[:, :, :SLON], 0, 1) for a in (fields, cotangent)]
    south = [shift(a[:, :SLAT], 1, 0) for a in (fields, cotangent)]
    corner = [shift(a[:, :SLAT, :SLON], 1, 1) for a in (fields, cotangent)]
    my_types = lax.dynamic_slice_in_dim(window_types, lat_at * 2, 2)
    mine = jnp.stack(
        [lax.dynamic_index_in_dim(bias_table, my_types[b], 0, keepdims=False) for b in range(2)]
    ).reshape(2, HEADS * per, WIN)
    mine = jnp.pad(mine, ((0, 0), (0, ROWS - HEADS * per), (0, 0)))
    bias = lax.all_gather(mine, "lon")
    at = jnp.stack([lat_at, lon_at]).astype(jnp.int32)
    proj_buffer, grad_buffer, bias_parts = attend(
        at,
        fields,
        cotangent,
        east + south + corner,
        norm_gain.reshape(1, -1),
        qkv_weight,
        proj_weight,
        bias,
        valid_mask,
        parts,
    )
    bias_mine = lax.all_to_all(bias_parts, "lon", 0, 0, tiled=True)
    grad_bias = jnp.sum(bias_mine.astype(F32), axis=0)[:, : HEADS * per].reshape(
        2, HEADS, per, WIN
    )

    def bring_back(wide, base):
        wide = wide.reshape(levels, lat_cells, 16, features)
        inside = lat_cells - SLAT
        beyond = lon_cells + SLON
        west = shift(wide[:, :inside, lon_cells:beyond], 0, -1)
        north = shift(wide[:, inside:, SLON:lon_cells], -1, 0)
        corner = shift(wide[:, inside:, lon_cells:beyond], -1, -1)
        top = jnp.concatenate([corner, north], axis=2)
        rest = jnp.concatenate([west, wide[:, :inside, SLON:lon_cells]], axis=2)
        own = jnp.concatenate([top, rest], axis=1)
        return (base.astype(F32) + own.astype(F32)).astype(BF16)

    return bring_back(proj_buffer, fields), bring_back(grad_buffer, cotangent), grad_bias


def solution(mesh):
    in_specs = (
        P(None, "lat", "lon", None),
        P(None, "lat", "lon", None),
        P(),
        P(),
        P(),
        P(None, None, "lon", None),
        P(),
        P(),
    )
    out_specs = (
        P(None, "lat", "lon", None),
        P(None, "lat", "lon", None),
        P("lat", None, "lon", None),
    )
    return jax.shard_map(local, mesh=mesh, in_specs=in_specs, out_specs=out_specs, check_vma=False)
```

time: 311 us -> 137 us (0.44); the launches traced: 307 us -> 137 us
  local copies, waits for them, and re-layouts: 119 us -> 23.7 us
  matrix products: 66.2 us -> 0 us
  waiting for transfers between devices: 63.8 us -> 16.3 us
  Pallas kernels: 0 us -> 34 us
  other arithmetic: 28.6 us -> 4.85 us
  blocking collectives: 0 us -> 19.9 us
  starting transfers between devices: 14.4 us -> 33.5 us
  between operations: 14.5 us -> 4.33 us
    dot_general x31 -> x0, matrix products: 47.1 us -> none  [the longest x20 31.1 us: product(): jnp.einsum(pattern, operand_a, operand_b, preferred_element_type=jnp.floa...]
    dynamic_update_slice x20 -> x0, local copies, waits for them, and re-layouts: 45.2 us -> none  [local(): lax.map(group_step, (win_packed, win_cot))]
    pallas_call x0 -> x1, Pallas kernels: none -> 34 us  [attend(): pl.pallas_call(kernel, grid=(levels // WZ,), out_shape=(out_tile, out_til...]
    reduce_scatter x1 -> x0, waiting for transfers between devices: 23.4 us -> none  [local(): lax.psum_scatter(bias_buffer.astype(jnp.bfloat16), 'lon', scatter_dimensi...]
    ppermute x8 -> x12, waiting for transfers between devices: 37.8 us -> 16.3 us  [shift(): return lax.ppermute(block, ('lat', 'lon'), route)]
    all_gather x0 -> x1, blocking collectives: none -> 19.9 us  [local(): bias = lax.all_gather(mine, 'lon')]
    sub x4 -> x0, matrix products: 19.1 us -> none  [group_step(): exponent = jnp.exp(scores - row_max)]
    ppermute x8 -> x12, starting transfers between devices: 14.3 us -> 29.9 us  [shift(): return lax.ppermute(block, ('lat', 'lon'), route)]
  transfers between devices with their start and end apart: 10 -> 13, of which waited for: 7 -> 5; matrix products, arithmetic and copies ran while one was open for 22% -> 14% of each run, Pallas kernels for 0% -> 0%
where the time goes in v1:
time: 137 us
  Pallas kernels  34 us (25%)
  starting transfers between devices  33.5 us (24%)
  local copies, waits for them, and re-layouts  23.7 us (17%)
  blocking collectives  19.9 us (15%)
  waiting for transfers between devices  16.3 us (12%)
  other arithmetic  4.85 us (4%)
  between operations  4.33 us (3%)
    pallas_call x1, Pallas kernels, attend(): pl.pallas_call(kernel, grid=(levels // WZ,), out_shape=(out_tile, out_til...  34 us
    ppermute x12, starting transfers between devices, shift(): return lax.ppermute(block, ('lat', 'lon'), route)  29.9 us
    all_gather x1, blocking collectives, local(): bias = lax.all_gather(mine, 'lon')  19.9 us
    ppermute x12, waiting for transfers between devices, shift(): return lax.ppermute(block, ('lat', 'lon'), route)  16.3 us
    unnamed x45, local copies, waits for them, and re-layouts  9.08 us
    convert_element_type x2, other arithmetic, bring_back(): return (base.astype(F32) + own.astype(F32)).astype(BF16)  4.57 us
    all_to_all x1, starting transfers between devices, local(): bias_mine = lax.all_to_all(bias_parts, 'lon', 0, 0, tiled=True)  3.56 us
  transfers between devices with their start and end apart: 13, of which 5 were waited for; matrix products, arithmetic and copies ran while one was open for 14% of the time, Pallas kernels for 0%

profile of v1, /device:TPU:1, one launch (start us, length us, event | category | flops | bytes accessed | tf_op | source)
XLA Modules:
  0.0 136.7 jit_solution(10347488367234778225)
XLA Ops:
  0.6 1.7 %copy.62.fields_ref = bf16[8,24,12,192]{3,2,1,0:T(8,128)(2,1)S(1)} copy(bf16[8,24,12,192]{3,1,2,0:T(8,128)(2,1)} %param.12) | data formatting | bytes 1769472 | tf_op args[0]
  3.1 7.4 %collective-permute-start.4 = (bf16[8,6,3,192]{3,2,1,0:T(4,128)(2,1)}, bf16[8,6,3,192]{3,2,1,0:T(4,128)(2,1)}, u32[]{:S(2)}, u32[]{:S(2)}) collective-permute-start(bf16[8,6,3,192]{3,2,1,0:T(4,128)(2,1)} %slice.72), channel_id=1, source_target_pairs={{17,0},{18,1},{19,2},{20,3},{21,4},{22,5},{23,6},{24,7},{25,8},{26... | collective-permute-start | bytes 165896 | tf_op jit(solution)/shard_map/ppermute | solution.py:288
  11.4 2.2 %collective-permute-start = (bf16[8,24,3,192]{3,2,1,0:T(4,128)(2,1)}, bf16[8,24,3,192]{3,2,1,0:T(4,128)(2,1)S(1)}, u32[]{:S(2)}, u32[]{:S(2)}) collective-permute-start(bf16[8,24,3,192]{3,2,1,0:T(4,128)(2,1)} %slice.68), channel_id=1, source_target_pairs={{1,0},{2,1},{3,2},{4,3},{5,4},{6,5},{7,6},{8,7},{9,8},{10,9},{11,1... | collective-permute-start | bytes 663560 | tf_op jit(solution)/shard_map/ppermute | solution.py:288
  14.3 1.4 collective-permute-start.2
  17.0 1.1 collective-permute-start.1
  23.1 1.2 constant_dynamic-slice_fusion.1
  24.4 19.9 %all-gather = bf16[32,64,144]{2,1,0:T(8,128)(2,1)S(1)} all-gather(bf16[2,64,144]{2,1,0:T(8,128)(2,1)S(1)} %pad.4.clone), channel_id=2, replica_groups=mesh['lat'=8,'lon'=16] {'lon'}, dimensions={0}, use_global_device_ids=true | all-gather | bytes 626688 | tf_op jit(solution)/shard_map/all_gather | solution.py:307
  44.3 1.6 %slice.73 = bf16[8,6,3,192]{3,2,1,0:T(4,128)(2,1)} slice(bf16[8,24,12,192]{3,2,1,0:T(8,128)(2,1)} %copy-done.8), slice={[0:8], [0:6], [0:3], [0:192]} | slice | bytes 110592 | tf_op jit(solution)/shard_map/slice | solution.py:301
  45.9 10.1 %collective-permute-start.5 = (bf16[8,6,3,192]{3,2,1,0:T(4,128)(2,1)}, bf16[8,6,3,192]{3,2,1,0:T(4,128)(2,1)S(1)}, u32[]{:S(2)}, u32[]{:S(2)}) collective-permute-start(bf16[8,6,3,192]{3,2,1,0:T(4,128)(2,1)} %slice.73), channel_id=1, source_target_pairs={{17,0},{18,1},{19,2},{20,3},{21,4},{22,5},{23,6},{24,7},{25,8},{26... | collective-permute-start | bytes 165896 | tf_op jit(solution)/shard_map/ppermute | solution.py:288
  56.1 1.9 %collective-permute-done.5.corner_c_ref = bf16[8,6,3,192]{3,2,1,0:T(4,128)(2,1)S(1)} collective-permute-done((bf16[8,6,3,192]{3,2,1,0:T(4,128)(2,1)}, bf16[8,6,3,192]{3,2,1,0:T(4,128)(2,1)S(1)}, u32[]{:S(2)}, u32[]{:S(2)}) %collective-permute-start.5) | collective-permute-done | bytes 55328 | tf_op jit(solution)/shard_map/ppermute | solution.py:288
  58.1 0.9 copy-done.3
  59.0 0.9 copy-done.4
  60.8 34.0 %shard_map.139 = (bf16[8,2,12,16,192]{4,3,2,1,0:T(8,128)(2,1)}, bf16[8,2,12,16,192]{4,3,2,1,0:T(8,128)(2,1)}, bf16[16,2,64,144]{3,2,1,0:T(8,128)(2,1)}) custom-call(s32[2]{0:T(128)S(1)} %pad_add_fusion.at_ref, bf16[8,24,12,192]{3,2,1,0:T(8,128)(2,1)} %copy-done.7, bf16[8,24,12,192]{3,2,1,0:T(8,128)(2,1)} %copy-done.8, ...), custom_call_target="tpu_custom_call" | custom-call | tf_op jit(solution)/shard_map/pallas_call | solution.py:263
  94.8 1.4 %slice.80 = bf16[8,18,3,192]{3,2,1,0:T(4,128)(2,1)S(1)} slice(bf16[8,24,16,192]{3,2,1,0:T(8,128)(2,1)} %bitcast.16), slice={[0:8], [0:18], [12:15], [0:192]} | slice | bytes 331776 | tf_op jit(solution)/shard_map/slice | solution.py:330
  96.2 1.1 slice.79
  98.1 2.0 %collective-permute-start.11 = (bf16[8,18,3,192]{3,1,2,0:T(8,128)(2,1)}, bf16[8,18,3,192]{3,1,2,0:T(8,128)(2,1)}, u32[]{:S(2)}, u32[]{:S(2)}) collective-permute-start(bf16[8,18,3,192]{3,1,2,0:T(8,128)(2,1)} %copy.81), channel_id=1, source_target_pairs={{15,0},{0,1},{1,2},{2,3},{3,4},{4,5},{5,6},{6,7},{7,8},{8,9},{9,10... | collective-permute-start | bytes 497672 | tf_op jit(solution)/shard_map/ppermute | solution.py:288
  100.9 1.0 slice.78
  105.5 3.6 %all-to-all-start = ((bf16[16,2,64,144]{3,2,1,0:T(8,128)(2,1)}), bf16[16,2,64,144]{3,2,1,0:T(8,128)(2,1)S(1)}, u32[]{:S(2)}, u32[]{:S(2)}) async-start(bf16[16,2,64,144]{3,2,1,0:T(8,128)(2,1)} %get-tuple-element.8), calls=%async_computation | async-start | bytes 2097152 | tf_op jit(solution)/shard_map/all_to_all | solution.py:321
  109.1 4.9 %collective-permute-start.6 = (bf16[8,6,3,192]{3,1,2,0:T(8,128)(2,1)S(1)}, bf16[8,6,3,192]{3,1,2,0:T(8,128)(2,1)S(1)}, u32[]{:S(2)}, u32[]{:S(2)}) collective-permute-start(bf16[8,6,3,192]{3,1,2,0:T(8,128)(2,1)S(1)} %copy.75), channel_id=1, source_target_pairs={{127,0},{112,1},{113,2},{114,3},{115,4},{116,5},{117,6},{118,7},{1... | collective-permute-start | bytes 165896 | tf_op jit(solution)/shard_map/ppermute | solution.py:288
  114.0 1.0 copy.77
  117.2 2.8 %add_convert_fusion = bf16[8,24,12,192]{3,1,2,0:T(8,128)(2,1)} fusion(bf16[8,24,12,192]{3,1,2,0:T(8,128)(2,1)S(1)} %copy-done.10, bf16[8,18,9,192]{3,1,2,0:T(8,128)(2,1)S(1)} %copy.82, bf16[8,18,3,192]{3,1,2,0:T(8,128)(2,1)} %collective-permute-done.11, bf16[8,6,9,192]{3,1,2,0:T(8,128)(2,1)} %collective-permute-done.10, ...), kind=kLoop, calls=%fused_computation | loop fusion | flops 4866048 | bytes 2654208 | tf_op jit(solution)/shard_map/convert_element_type | solution.py:336
  120.9 3.2 %collective-permute-done.8 = bf16[8,18,3,192]{3,1,2,0:T(8,128)(2,1)S(1)} collective-permute-done((bf16[8,18,3,192]{3,1,2,0:T(8,128)(2,1)S(1)}, bf16[8,18,3,192]{3,1,2,0:T(8,128)(2,1)S(1)}, u32[]{:S(2)}, u32[]{:S(2)}) %collective-permute-start.8) | collective-permute-done | bytes 165920 | tf_op jit(solution)/shard_map/ppermute | solution.py:288
  124.1 10.0 %collective-permute-done.7 = bf16[8,6,9,192]{3,1,2,0:T(8,128)(2,1)S(1)} collective-permute-done((bf16[8,6,9,192]{3,1,2,0:T(8,128)(2,1)S(1)}, bf16[8,6,9,192]{3,1,2,0:T(8,128)(2,1)S(1)}, u32[]{:S(2)}, u32[]{:S(2)}) %collective-permute-start.7) | collective-permute-done | bytes 165920 | tf_op jit(solution)/shard_map/ppermute | solution.py:288
  134.1 1.7 %add_convert_fusion.1 = bf16[8,24,12,192]{3,1,2,0:T(8,128)(2,1)} fusion(bf16[8,24,12,192]{3,1,2,0:T(8,128)(2,1)S(1)} %copy-done.11, bf16[8,18,9,192]{3,1,2,0:T(8,128)(2,1)S(1)} %copy.78, bf16[8,18,3,192]{3,1,2,0:T(8,128)(2,1)S(1)} %collective-permute-done.8, bf16[8,6,9,192]{3,1,2,0:T(8,128)(2,1)S(1)} %collective-permute-done.7, ...), kind=kLoop, calls=%fused_computation.1 | loop fusion | flops 4866048 | bytes 2654208 | tf_op jit(solution)/shard_map/convert_element_type | solution.py:336
  (75 shorter events, 15.3 us)
Async XLA Ops:
  0.6 15.1 %copy-start.9 = (bf16[8,24,12,192]{3,1,2,0:T(8,128)(2,1)S(1)}, bf16[8,24,12,192]{3,1,2,0:T(8,128)(2,1)}, u32[]{:S(2)}) copy-start(bf16[8,24,12,192]{3,1,2,0:T(8,128)(2,1)} %param.13) | copy-start | bytes 2654212
  2.3 13.7 %copy-start.7 = (bf16[8,24,12,192]{3,2,1,0:T(8,128)(2,1)}, bf16[8,24,12,192]{3,2,1,0:T(8,128)(2,1)S(1)}, u32[]{:S(2)}) copy-start(bf16[8,24,12,192]{3,2,1,0:T(8,128)(2,1)S(1)} %copy.62.fields_ref) | copy-start | bytes 2654212
  3.1 42.9 %collective-permute-start.4 = (bf16[8,6,3,192]{3,2,1,0:T(4,128)(2,1)}, bf16[8,6,3,192]{3,2,1,0:T(4,128)(2,1)}, u32[]{:S(2)}, u32[]{:S(2)}) collective-permute-start(bf16[8,6,3,192]{3,2,1,0:T(4,128)(2,1)} %slice.72), channel_id=1, source_target_pairs={{17,0},{18,1},{19,2},{20,3},{21,4},{22,5},{23,6},{24,7},{25,8},{26... | collective-permute-start | bytes 165896 | tf_op jit(solution)/shard_map/ppermute | solution.py:288
  11.4 46.6 %collective-permute-start = (bf16[8,24,3,192]{3,2,1,0:T(4,128)(2,1)}, bf16[8,24,3,192]{3,2,1,0:T(4,128)(2,1)S(1)}, u32[]{:S(2)}, u32[]{:S(2)}) collective-permute-start(bf16[8,24,3,192]{3,2,1,0:T(4,128)(2,1)} %slice.68), channel_id=1, source_target_pairs={{1,0},{2,1},{3,2},{4,3},{5,4},{6,5},{7,6},{8,7},{9,8},{10,9},{11,1... | collective-permute-start | bytes 663560 | tf_op jit(solution)/shard_map/ppermute | solution.py:288
  14.3 4.7 %copy-start.15 = (s32[16]{0:T(128)S(1)}, s32[16]{0:T(128)}, u32[]{:S(2)}) copy-start(s32[16]{0:T(128)} %param.18) | copy-start | bytes 196
  14.3 43.7 %collective-permute-start.2 = (bf16[8,6,12,192]{3,2,1,0:T(8,128)(2,1)}, bf16[8,6,12,192]{3,2,1,0:T(8,128)(2,1)S(1)}, u32[]{:S(2)}, u32[]{:S(2)}) collective-permute-start(bf16[8,6,12,192]{3,2,1,0:T(8,128)(2,1)} %slice.70), channel_id=1, source_target_pairs={{16,0},{17,1},{18,2},{19,3},{20,4},{21,5},{22,6},{23,7},{24,8},{25... | collective-permute-start | bytes 663560 | tf_op jit(solution)/shard_map/ppermute | solution.py:288
  16.0 2.1 %copy-start.8 = (bf16[8,24,12,192]{3,2,1,0:T(8,128)(2,1)}, bf16[8,24,12,192]{3,2,1,0:T(8,128)(2,1)S(1)}, u32[]{:S(2)}) copy-start(bf16[8,24,12,192]{3,2,1,0:T(8,128)(2,1)S(1)} %copy.63.cot_ref) | copy-start | bytes 2654212
  16.0 42.0 %copy-start = (bf16[2,384,144]{2,1,0:T(8,128)(2,1)S(1)}, bf16[2,384,144]{2,1,0:T(8,128)(2,1)}, u32[]{:S(2)}) copy-start(bf16[2,384,144]{2,1,0:T(8,128)(2,1)} %constant.35.clone.unpick_ref) | copy-start | bytes 663556
  16.0 42.0 %copy-start.1 = (bf16[192,576]{1,0:T(8,128)(2,1)S(1)}, bf16[192,576]{1,0:T(8,128)(2,1)}, u32[]{:S(2)}) copy-start(bf16[192,576]{1,0:T(8,128)(2,1)} %qkv_ref.1) | copy-start | bytes 663556
  16.1 42.0 %copy-start.2 = (bf16[2,144,384]{2,1,0:T(8,128)(2,1)S(1)}, bf16[2,144,384]{2,1,0:T(8,128)(2,1)}, u32[]{:S(2)}) copy-start(bf16[2,144,384]{2,1,0:T(8,128)(2,1)} %constant.34.clone.pick_ref) | copy-start | bytes 663556
  16.1 42.0 %copy-start.6 = (f32[192]{0:T(256)S(1)}, f32[192]{0:T(256)}, u32[]{:S(2)}) copy-start(f32[192]{0:T(256)} %param.14) | copy-start | bytes 2308
  17.0 41.1 %collective-permute-start.1 = (bf16[8,24,3,192]{3,2,1,0:T(4,128)(2,1)}, bf16[8,24,3,192]{3,2,1,0:T(4,128)(2,1)S(1)}, u32[]{:S(2)}, u32[]{:S(2)}) collective-permute-start(bf16[8,24,3,192]{3,2,1,0:T(4,128)(2,1)} %slice.69), channel_id=1, source_target_pairs={{1,0},{2,1},{3,2},{4,3},{5,4},{6,5},{7,6},{8,7},{9,8},{10,9},{11,1... | collective-permute-start | bytes 663560 | tf_op jit(solution)/shard_map/ppermute | solution.py:288
  18.9 39.2 %collective-permute-start.3 = (bf16[8,6,12,192]{3,2,1,0:T(8,128)(2,1)}, bf16[8,6,12,192]{3,2,1,0:T(8,128)(2,1)S(1)}, u32[]{:S(2)}, u32[]{:S(2)}) collective-permute-start(bf16[8,6,12,192]{3,2,1,0:T(8,128)(2,1)} %slice.71), channel_id=1, source_target_pairs={{16,0},{17,1},{18,2},{19,3},{20,4},{21,5},{22,6},{23,7},{24,8},{25... | collective-permute-start | bytes 663560 | tf_op jit(solution)/shard_map/ppermute | solution.py:288
  45.9 12.1 %collective-permute-start.5 = (bf16[8,6,3,192]{3,2,1,0:T(4,128)(2,1)}, bf16[8,6,3,192]{3,2,1,0:T(4,128)(2,1)S(1)}, u32[]{:S(2)}, u32[]{:S(2)}) collective-permute-start(bf16[8,6,3,192]{3,2,1,0:T(4,128)(2,1)} %slice.73), channel_id=1, source_target_pairs={{17,0},{18,1},{19,2},{20,3},{21,4},{22,5},{23,6},{24,7},{25,8},{26... | collective-permute-start | bytes 165896 | tf_op jit(solution)/shard_map/ppermute | solution.py:288
  94.8 7.7 %copy-start.12 = (bf16[8,2,12,16,192]{4,3,2,1,0:T(8,128)(2,1)S(1)}, bf16[8,2,12,16,192]{4,3,2,1,0:T(8,128)(2,1)}, u32[]{:S(2)}) copy-start(bf16[8,2,12,16,192]{4,3,2,1,0:T(8,128)(2,1)} %get-tuple-element.6) | copy-start | bytes 3538948
  94.8 8.7 %copy-start.13 = (bf16[8,2,12,16,192]{4,3,2,1,0:T(8,128)(2,1)S(1)}, bf16[8,2,12,16,192]{4,3,2,1,0:T(8,128)(2,1)}, u32[]{:S(2)}) copy-start(bf16[8,2,12,16,192]{4,3,2,1,0:T(8,128)(2,1)} %get-tuple-element.7) | copy-start | bytes 3538948
  98.1 18.6 %collective-permute-start.11 = (bf16[8,18,3,192]{3,1,2,0:T(8,128)(2,1)}, bf16[8,18,3,192]{3,1,2,0:T(8,128)(2,1)}, u32[]{:S(2)}, u32[]{:S(2)}) collective-permute-start(bf16[8,18,3,192]{3,1,2,0:T(8,128)(2,1)} %copy.81), channel_id=1, source_target_pairs={{15,0},{0,1},{1,2},{2,3},{3,4},{4,5},{5,6},{6,7},{7,8},{8,9},{9,10... | collective-permute-start | bytes 497672 | tf_op jit(solution)/shard_map/ppermute | solution.py:288
  100.9 15.8 %collective-permute-start.10 = (bf16[8,6,9,192]{3,1,2,0:T(8,128)(2,1)}, bf16[8,6,9,192]{3,1,2,0:T(8,128)(2,1)}, u32[]{:S(2)}, u32[]{:S(2)}) collective-permute-start(bf16[8,6,9,192]{3,1,2,0:T(8,128)(2,1)} %copy.80), channel_id=1, source_target_pairs={{112,0},{113,1},{114,2},{115,3},{116,4},{117,5},{118,6},{119,7},{1... | collective-permute-start | bytes 497672 | tf_op jit(solution)/shard_map/ppermute | solution.py:288
  102.6 14.1 %collective-permute-start.9 = (bf16[8,6,3,192]{3,1,2,0:T(8,128)(2,1)}, bf16[8,6,3,192]{3,1,2,0:T(8,128)(2,1)}, u32[]{:S(2)}, u32[]{:S(2)}) collective-permute-start(bf16[8,6,3,192]{3,1,2,0:T(8,128)(2,1)} %copy.79), channel_id=1, source_target_pairs={{127,0},{112,1},{113,2},{114,3},{115,4},{116,5},{117,6},{118,7},{1... | collective-permute-start | bytes 165896 | tf_op jit(solution)/shard_map/ppermute | solution.py:288
  105.5 30.3 %all-to-all-start = ((bf16[16,2,64,144]{3,2,1,0:T(8,128)(2,1)}), bf16[16,2,64,144]{3,2,1,0:T(8,128)(2,1)S(1)}, u32[]{:S(2)}, u32[]{:S(2)}) async-start(bf16[16,2,64,144]{3,2,1,0:T(8,128)(2,1)} %get-tuple-element.8), calls=%async_computation | async-start | bytes 2097152 | tf_op jit(solution)/shard_map/all_to_all | solution.py:321
  109.1 11.8 %collective-permute-start.6 = (bf16[8,6,3,192]{3,1,2,0:T(8,128)(2,1)S(1)}, bf16[8,6,3,192]{3,1,2,0:T(8,128)(2,1)S(1)}, u32[]{:S(2)}, u32[]{:S(2)}) collective-permute-start(bf16[8,6,3,192]{3,1,2,0:T(8,128)(2,1)S(1)} %copy.75), channel_id=1, source_target_pairs={{127,0},{112,1},{113,2},{114,3},{115,4},{116,5},{117,6},{118,7},{1... | collective-permute-start | bytes 165896 | tf_op jit(solution)/shard_map/ppermute | solution.py:288
  115.0 9.1 %collective-permute-start.8 = (bf16[8,18,3,192]{3,1,2,0:T(8,128)(2,1)S(1)}, bf16[8,18,3,192]{3,1,2,0:T(8,128)(2,1)S(1)}, u32[]{:S(2)}, u32[]{:S(2)}) collective-permute-start(bf16[8,18,3,192]{3,1,2,0:T(8,128)(2,1)S(1)} %copy.77), channel_id=1, source_target_pairs={{15,0},{0,1},{1,2},{2,3},{3,4},{4,5},{5,6},{6,7},{7,8},{8,9},{9,10... | collective-permute-start | bytes 497672 | tf_op jit(solution)/shard_map/ppermute | solution.py:288
  116.3 17.8 %copy-start.11 = (bf16[8,24,12,192]{3,1,2,0:T(8,128)(2,1)S(1)}, bf16[8,24,12,192]{3,1,2,0:T(8,128)(2,1)}, u32[]{:S(2)}) copy-start(bf16[8,24,12,192]{3,1,2,0:T(8,128)(2,1)} %param.12) | copy-start | bytes 2654212
  116.7 17.4 %collective-permute-start.7 = (bf16[8,6,9,192]{3,1,2,0:T(8,128)(2,1)S(1)}, bf16[8,6,9,192]{3,1,2,0:T(8,128)(2,1)S(1)}, u32[]{:S(2)}, u32[]{:S(2)}) collective-permute-start(bf16[8,6,9,192]{3,1,2,0:T(8,128)(2,1)S(1)} %copy.76), channel_id=1, source_target_pairs={{112,0},{113,1},{114,2},{115,3},{116,4},{117,5},{118,6},{119,7},{1... | collective-permute-start | bytes 497672 | tf_op jit(solution)/shard_map/ppermute | solution.py:288
  (5 other events, 5.2 us)

commit v2 on v0

v2 whole, which is shorter than its diff:
```python
import functools

import jax
import jax.numpy as jnp
import numpy as np
from jax import lax
from jax.experimental import pallas as pl
from jax.experimental.pallas import tpu as pltpu
from jax.sharding import PartitionSpec as P

HEADS = 6
WZ = 2
WLAT = 12
WLON = 6
WIN = 144
SLAT = 6
SLON = 3
HEAD_DIM = 32
MAIN = 128
REST = WIN - MAIN
LANES = 896
ROWS = 64

NEGATIVE = -1e30
EPSILON = 1e-05
LOG2E = 1.4426950408889634
SCALE = float(HEAD_DIM) ** (-0.5)

F32 = jnp.float32
BF16 = jnp.bfloat16


def nn(a, b):
    return lax.dot_general(a, b, (((1,), (0,)), ((), ())), preferred_element_type=F32)


def nt(a, b):
    return lax.dot_general(a, b, (((1,), (1,)), ((), ())), preferred_element_type=F32)


def tn(a, b):
    return lax.dot_general(a, b, (((0,), (0,)), ((), ())), preferred_element_type=F32)


def lane_of(head, query):
    return np.where(query < MAIN, head * MAIN + query, HEADS * MAIN + head * REST + query - MAIN)


COLS = 2 * WLON
LATS = 2 * WLAT
PAIR = WZ * COLS * LATS
STRIP = 112
CORNER = 48


def tokens(columns, rows):
    return [(z, c, r) for z in range(WZ) for c in columns for r in rows]


def window(b, w):
    return [
        (z, SLON + WLON * w + c, SLAT + WLAT * b + r)
        for z in range(WZ)
        for r in range(WLAT)
        for c in range(WLON)
    ]


def pick(wanted, sources):
    where, at = {}, 0
    for source, length in sources:
        for n, token in enumerate(source):
            where.setdefault(token, at + n)
        at += length
    out = np.zeros((len(wanted), at), np.float32)
    for n, token in enumerate(wanted):
        if token in where:
            out[n, where[token]] = 1
    return out


def padded(rows, length):
    return np.pad(rows, ((0, length - rows.shape[0]), (0, 0)))


OWN_WEST = tokens(range(SLON, SLON + WLON), range(LATS))
OWN_EAST = tokens(range(SLON + WLON, COLS), range(LATS))
EAST = tokens(range(COLS, COLS + SLON), range(SLAT, LATS))
SOUTH = tokens(range(SLON, COLS), range(LATS, LATS + SLAT))
FAR = tokens(range(COLS, COLS + SLON), range(LATS, LATS + SLAT))


def sources_of(b, w):
    if w == 0:
        parts = [(OWN_WEST, len(OWN_WEST))]
    else:
        parts = [(OWN_EAST, len(OWN_EAST)), (EAST, STRIP)]
    if b == 1:
        parts.append((SOUTH, STRIP))
        if w == 1:
            parts.append((FAR, CORNER))
    return parts


def send_picks():
    own = [(tokens(range(COLS), range(LATS)), PAIR)]
    west = pick(tokens(range(SLON), range(SLAT, LATS)), own)
    north = pick(tokens(range(SLON, COLS), range(SLAT)), own)
    corner = pick(tokens(range(SLON), range(SLAT)), own)
    return np.concatenate([padded(west, STRIP), padded(north, STRIP), padded(corner, CORNER)])


def land_picks():
    places = tokens(range(COLS), range(LATS))
    sources = [
        (tokens(range(SLON), range(SLAT, LATS)), STRIP),
        (tokens(range(SLON, COLS), range(SLAT)), STRIP),
        (tokens(range(SLON), range(SLAT)), CORNER),
    ]
    return pick(places, sources)


def bias_picks(parts):
    per = WIN // parts
    pick = np.zeros((parts, ROWS, LANES), np.float32)
    for k in range(parts):
        for h in range(HEADS):
            for r in range(per):
                pick[k, h * per + r, lane_of(h, k * per + r)] = 1
    return pick.reshape(parts * ROWS, LANES)


def head_blocks(tokens, head_masks):
    pieces = [tokens[:MAIN] * head_masks[h] for h in range(HEADS)]
    pieces += [tokens[MAIN:] * head_masks[h] for h in range(HEADS)]
    pieces.append(jnp.zeros((LANES - HEADS * WIN, tokens.shape[1]), tokens.dtype))
    return jnp.concatenate(pieces, axis=0)


def own_heads(wide):
    main, rest = [], []
    for h in range(HEADS):
        rows = wide[h * HEAD_DIM : (h + 1) * HEAD_DIM]
        main.append(rows[:, h * MAIN : (h + 1) * MAIN])
        left = HEADS * MAIN + h * REST
        rest.append(rows[:, left : left + REST])
    return jnp.concatenate(
        [jnp.concatenate(main, axis=0), jnp.concatenate(rest, axis=0)], axis=1
    )


def pack(rows_a, rows_b):
    return jnp.concatenate(
        [
            rows_a[:, :MAIN],
            rows_b[:, :MAIN],
            jnp.concatenate([rows_a[:, MAIN:], rows_b[:, MAIN:]], axis=1),
        ],
        axis=0,
    ).astype(BF16)


def unpack(packed):
    count = packed.shape[0] // 3
    half = packed.shape[1] // 2
    last = packed[2 * count :]
    return (
        jnp.concatenate([packed[:count], last[:, :half]], axis=1),
        jnp.concatenate([packed[count : 2 * count], last[:, half:]], axis=1),
    )


def pack_kernel(
    types_ref, fields_ref, cot_ref, table_ref, pick_ref, eye_ref, east_ref, south_ref, far_ref, mine_ref
):
    features = fields_ref.shape[-1]
    rows = [
        nn(pick_ref[...], ref[...].reshape(-1, features)) for ref in (fields_ref, cot_ref)
    ]
    at = 0
    for ref, count in ((east_ref, STRIP), (south_ref, STRIP), (far_ref, CORNER)):
        ref[0] = pack(*(r[at : at + count] for r in rows))
        at += count

    @pl.when(pl.program_id(0) == 0)
    def choose_bias():
        table = table_ref[...].astype(F32)
        kind = lax.broadcasted_iota(jnp.int32, (1, table.shape[1], 1), 1)
        chosen = []
        for b in range(2):
            one = jnp.sum(jnp.where(kind == types_ref[b], table, 0.0), axis=1)
            chosen.append(one.astype(BF16))
            chosen.append(jnp.zeros((ROWS - one.shape[0], WIN), BF16))
        mine_ref[...] = nt(eye_ref[...], jnp.concatenate(chosen, axis=0)).astype(BF16)


def prepare(b, at_ref, qkv_ref, proj_ref, bias_ref, valid_ref, bias_pick_ref, eye, weights, bias_t):
    features = proj_ref.shape[0]
    for n in range(3):
        weights[n] = qkv_ref[:, n * features : (n + 1) * features]
    weights[3] = nt(eye, weights[1]).astype(BF16)
    weights[4] = nt(eye, weights[2]).astype(BF16)
    weights[5] = nt(eye, proj_ref[...]).astype(BF16)
    table = jnp.concatenate(
        [bias_ref[k, :, b * ROWS : (b + 1) * ROWS] for k in range(bias_ref.shape[0])], axis=1
    )
    wide = nn(table, bias_pick_ref[...]) * LOG2E
    if b == 0:
        bias_t[0] = wide
        return
    key = lax.broadcasted_iota(jnp.int32, (WIN, 1), 0)
    lane = lax.broadcasted_iota(jnp.int32, (1, LANES), 1)
    query = jnp.where(lane < HEADS * MAIN, lane % MAIN, MAIN + (lane - HEADS * MAIN) % REST)
    key_row = (key // WLON) % WLAT
    query_row = (query // WLON) % WLAT
    last = at_ref[0] == at_ref[2] - 1
    same = (key_row < SLAT) == (query_row < SLAT)
    lat_rows, lon_columns = valid_ref.shape
    valid_rows = jnp.concatenate(
        [valid_ref[lat_rows - SLAT :, :], valid_ref[:SLAT, :]], axis=0
    ).astype(F32)
    row_pick = (key_row == lax.broadcasted_iota(jnp.int32, (WIN, WLAT), 1)).astype(F32)
    key_valid = nn(row_pick, valid_rows)
    column = lax.broadcasted_iota(jnp.int32, (WIN, lon_columns), 1)
    for w in range(2):
        wanted = at_ref[1] * COLS + SLON + WLON * w + key % WLON
        wanted = jnp.where(wanted >= lon_columns, wanted - lon_columns, wanted)
        is_valid = (
            jnp.sum(jnp.where(column == wanted, key_valid, 0.0), axis=1, keepdims=True) > 0.5
        )
        allowed = jnp.logical_and(same, is_valid) | jnp.logical_not(last)
        bias_t[w] = jnp.where(allowed, wide, NEGATIVE)


def one_window(flat_f, flat_c, chosen, gain, proj_weight, weights, bias, eye, head_masks):
    x = nn(chosen, flat_f)
    cot = nn(chosen, flat_c).astype(BF16)
    mean = jnp.mean(x, axis=1, keepdims=True)
    centered = x - mean
    variance = jnp.mean(centered * centered, axis=1, keepdims=True)
    inverse = lax.rsqrt(variance + EPSILON)
    hat = centered * inverse
    normed = (hat * gain).astype(BF16)
    queries = nn(normed, weights[0]).astype(BF16)
    keys = nn(normed, weights[1]).astype(BF16)
    values = nn(normed, weights[2]).astype(BF16)
    keys_t = nt(weights[3], normed).astype(BF16)
    values_t = nt(weights[4], normed).astype(BF16)
    grad_att = nt(cot, proj_weight).astype(BF16)
    q_blocks = head_blocks(queries, head_masks)
    g_blocks = head_blocks(grad_att, head_masks)
    scores = nt(keys, q_blocks) * (SCALE * LOG2E) + bias
    exponent = jnp.exp2(scores - jnp.max(scores, axis=0, keepdims=True))
    soft = exponent * (1.0 / jnp.sum(exponent, axis=0, keepdims=True))
    soft_bf = soft.astype(BF16)
    grad_soft = nt(values, g_blocks)
    delta = jnp.sum(soft * grad_soft, axis=0, keepdims=True)
    grad_scores = soft * (grad_soft - delta)
    grad_bf = grad_scores.astype(BF16)
    grad_values = nn(soft_bf, g_blocks).astype(BF16)
    grad_keys = (nn(grad_bf, q_blocks) * SCALE).astype(BF16)
    attended_t = own_heads(nn(values_t, soft_bf)).astype(BF16)
    grad_queries_t = (own_heads(nn(keys_t, grad_bf)) * SCALE).astype(BF16)
    projected_t = nn(weights[5], attended_t).astype(BF16)
    projected = nt(eye[:WIN, :WIN], projected_t).astype(BF16)
    grad_queries = nt(eye[:WIN, :WIN], grad_queries_t).astype(BF16)
    grad_normed = (
        nt(grad_queries, weights[0]) + nt(grad_keys, weights[1]) + nt(grad_values, weights[2])
    )
    grad_hat = grad_normed * gain
    grad_x = inverse * (
        grad_hat
        - jnp.mean(grad_hat, axis=1, keepdims=True)
        - hat * jnp.mean(grad_hat * hat, axis=1, keepdims=True)
    )
    return projected, grad_x.astype(BF16), grad_scores


def attend_kernel(b, *refs):
    (at_ref, fields_ref, cot_ref, east_ref), refs = refs[:4], refs[4:]
    if b == 1:
        (south_ref, far_ref), refs = refs[:2], refs[2:]
    else:
        (before_p_ref, before_g_ref), refs = refs[:2], refs[2:]
    (gain_ref, qkv_ref, proj_ref, bias_ref, valid_ref, bias_pick_ref, eye_ref), refs = (
        refs[:7],
        refs[7:],
    )
    (pick_w_ref, pick_e_ref, place_ref), refs = refs[:3], refs[3:]
    if b == 1:
        (win_p_ref, win_g_ref, strip_ref, bias_out_ref), refs = refs[:4], refs[4:]
    else:
        (mixed_ref, grad_ref, strip_ref, bias_out_ref), refs = refs[:4], refs[4:]
    weights, bias_t, bias_sum = refs
    step = pl.program_id(0)
    features = fields_ref.shape[-1]
    eye = eye_ref[...]

    @pl.when(step == 0)
    def start():
        bias_sum[...] = jnp.zeros_like(bias_sum)
        prepare(
            b, at_ref, qkv_ref, proj_ref, bias_ref, valid_ref, bias_pick_ref, eye, weights, bias_t
        )

    gain = gain_ref[...]
    lane_head = lax.broadcasted_iota(jnp.int32, (1, features), 1) // HEAD_DIM
    head_masks = [(lane_head == h).astype(F32).astype(BF16) for h in range(HEADS)]
    flats = [[], []]
    halo = unpack(east_ref[0])
    if b == 1:
        south, far = unpack(south_ref[0]), unpack(far_ref[0])
    for n, ref in enumerate((fields_ref, cot_ref)):
        west = [ref[:, SLON : SLON + WLON].reshape(-1, features)]
        right = [ref[:, SLON + WLON :].reshape(-1, features), halo[n]]
        if b == 1:
            west.append(south[n])
            right += [south[n], far[n]]
        flats[0].append(jnp.concatenate(west, axis=0))
        flats[1].append(jnp.concatenate(right, axis=0))
    done = [
        one_window(
            *flats[w],
            (pick_w_ref, pick_e_ref)[w][...],
            gain,
            proj_ref[...],
            weights,
            bias_t[w * b],
            eye,
            head_masks,
        )
        for w in range(2)
    ]
    bias_sum[...] += done[0][2] + done[1][2]
    if b == 1:
        placed = []
        for n, ref in enumerate((win_p_ref, win_g_ref)):
            both = jnp.concatenate([done[0][n], done[1][n]], axis=0)
            ref[0] = both
            placed.append(nn(place_ref[...], both))
        strip_ref[0, : 3 * STRIP] = pack(*(p[:STRIP] for p in placed))
        strip_ref[0, 3 * STRIP :] = pack(*(p[STRIP:] for p in placed))
    else:
        placed = []
        for n, (ref, base, out) in enumerate(
            ((before_p_ref, fields_ref, mixed_ref), (before_g_ref, cot_ref, grad_ref))
        ):
            both = jnp.concatenate([done[0][n], done[1][n], ref[0]], axis=0)
            part = nn(place_ref[...], both)
            placed.append(part)
            inner = part[STRIP:].reshape(WZ, COLS - SLON, LATS, features)
            out[:, :SLON] = base[:, :SLON]
            out[:, SLON:] = (base[:, SLON:].astype(F32) + inner).astype(BF16)
        strip_ref[0] = pack(*(p[:STRIP] for p in placed))

    @pl.when(step == pl.num_programs(0) - 1)
    def finish():
        wide = nt(bias_sum[...].astype(BF16), bias_pick_ref[...])
        top, low = wide[:80], wide[80:]
        for k in range(bias_out_ref.shape[0]):
            left = top[:, k * ROWS : (k + 1) * ROWS]
            right = low[:, k * ROWS : (k + 1) * ROWS]
            right = jnp.concatenate([right, jnp.zeros((160 - WIN, ROWS), F32)], axis=0)
            bias_out_ref[k] = jnp.concatenate([left, right], axis=1).astype(BF16)


def land_kernel(
    mixed_ref, grad_ref, west_ref, north_ref, far_ref, bias0_ref, bias1_ref, place_ref,
    out_m_ref, out_g_ref, out_b_ref
):
    features = mixed_ref.shape[-1]
    pieces = [unpack(p) for p in (west_ref[0], north_ref[0, : 3 * STRIP], far_ref[0])]
    for n, (base, out) in enumerate(((mixed_ref, out_m_ref), (grad_ref, out_g_ref))):
        part = nn(place_ref[...], jnp.concatenate([p[n] for p in pieces], axis=0))
        out[...] = (base[...].astype(F32) + part.reshape(base.shape)).astype(BF16)

    @pl.when(pl.program_id(0) == 0)
    def bias():
        count = out_b_ref.shape[0]
        for b, ref in enumerate((bias0_ref, bias1_ref)):
            total = ref[0].astype(F32)
            for k in range(1, ref.shape[0]):
                total = total + ref[k].astype(F32)
            turned = total.T
            whole = jnp.concatenate([turned[:ROWS], turned[ROWS:, : WIN - 80]], axis=1)
            out_b_ref[:, b, :] = whole[:count]


def by_pair(array, size=1):
    return pl.BlockSpec((size,) + array.shape[1:], lambda g: (g,) + (0,) * (array.ndim - 1))


def whole(array):
    return pl.BlockSpec(array.shape, lambda g: (0,) * array.ndim)


def shape_of(*dims, kind=BF16):
    return jax.ShapeDtypeStruct(dims, kind)


def call(body, name, steps, inputs, outputs, scratch=(), flops=10**9):
    in_specs = [spec for _, spec in inputs]
    bytes_moved = sum(a.size * a.dtype.itemsize for a, _ in inputs) + sum(
        int(np.prod(a.shape)) * a.dtype.itemsize for a, _ in outputs
    )
    return pl.pallas_call(
        body,
        name=name,
        grid=(steps,),
        out_shape=tuple(a for a, _ in outputs),
        in_specs=in_specs,
        out_specs=tuple(spec for _, spec in outputs),
        scratch_shapes=list(scratch),
        compiler_params=pltpu.CompilerParams(vmem_limit_bytes=64 * 1024 * 1024),
        cost_estimate=pl.CostEstimate(
            flops=flops, bytes_accessed=bytes_moved, transcendentals=0
        ),
    )(*(a for a, _ in inputs))


def paired(array, size=1):
    return (array, by_pair(array, size))


def entire(array):
    return (array, whole(array))


def in_smem(array):
    return (array, pl.BlockSpec(memory_space=pltpu.SMEM))


def shift(block, lat_step, lon_step):
    lats, lons = lax.axis_size("lat"), lax.axis_size("lon")
    route = [
        (((a + lat_step) % lats) * lons + (o + lon_step) % lons, a * lons + o)
        for a in range(lats)
        for o in range(lons)
    ]
    return lax.ppermute(block, ("lat", "lon"), route)


def local(
    fields, cotangent, norm_gain, qkv_weight, proj_weight, bias_table, window_types, valid_mask
):
    fields = fields.transpose(0, 2, 1, 3)
    cotangent = cotangent.transpose(0, 2, 1, 3)
    levels, lon_cells, lat_cells, features = fields.shape
    lat_at = lax.axis_index("lat")
    lon_at = lax.axis_index("lon")
    parts = lax.axis_size("lon")
    per = WIN // parts
    pairs = levels // WZ
    at = jnp.stack([lat_at, lon_at, lax.axis_size("lat")]).astype(jnp.int32)
    my_types = lax.dynamic_slice_in_dim(window_types, lat_at * 2, 2)
    eye = jnp.asarray(np.eye(features), BF16)
    bias_pick = jnp.asarray(bias_picks(parts), BF16)
    strip = shape_of(pairs, 3 * STRIP, MAIN)
    corner = shape_of(pairs, 3 * CORNER, MAIN)
    both_strips = shape_of(pairs, 3 * (STRIP + CORNER), MAIN)

    table = bias_table.transpose(1, 2, 0, 3).reshape(HEADS * per, -1, WIN)
    send = jnp.asarray(send_picks(), BF16)
    east, south, far, mine = call(
        pack_kernel,
        "pack",
        pairs,
        [
            in_smem(my_types),
            paired(fields, WZ),
            paired(cotangent, WZ),
            entire(table),
            entire(send),
            entire(jnp.asarray(np.eye(WIN), BF16)),
        ],
        [paired(strip), paired(strip), paired(corner), entire(shape_of(WIN, 2 * ROWS))],
    )
    south = shift(south, 1, 0)
    far = shift(far, 1, 1)
    east = shift(east, 0, 1)
    bias = lax.all_to_all(
        jnp.broadcast_to(mine[None], (parts,) + mine.shape), "lon", 0, 0, tiled=True
    )

    shared = [
        entire(a)
        for a in (norm_gain.reshape(1, -1), qkv_weight, proj_weight, bias, valid_mask, bias_pick, eye)
    ]
    bias_block = shape_of(parts, 80, 2 * ROWS)
    window_pair = shape_of(pairs, 2 * WIN, features)

    def scratch(tables):
        return (
            pltpu.VMEM((6, features, features), BF16),
            pltpu.VMEM((tables, WIN, LANES), F32),
            pltpu.VMEM((WIN, LANES), F32),
        )

    def window_picks(b):
        return [
            entire(jnp.asarray(pick(window(b, w), sources_of(b, w)), BF16)) for w in range(2)
        ]

    b_order = [(window(1, 0) + window(1, 1), 2 * WIN)]
    place_b = np.concatenate(
        [padded(pick(SOUTH, b_order), STRIP), padded(pick(FAR, b_order), CORNER)]
    )
    win_p, win_g, north, bias_part1 = call(
        functools.partial(attend_kernel, 1),
        "attend_south",
        pairs,
        [in_smem(at), paired(fields, WZ), paired(cotangent, WZ), paired(east), paired(south), paired(far)]
        + shared
        + window_picks(1)
        + [entire(jnp.asarray(place_b, BF16))],
        [paired(window_pair), paired(window_pair), paired(both_strips), entire(bias_block)],
        scratch(2),
        10**10,
    )
    north = shift(north, -1, 0)
    bias_part1 = lax.all_to_all(bias_part1, "lon", 0, 0, tiled=True)

    all_order = [(window(0, 0) + window(0, 1) + window(1, 0) + window(1, 1), 4 * WIN)]
    place_a = np.concatenate(
        [
            padded(pick(EAST, all_order), STRIP),
            pick(tokens(range(SLON, COLS), range(LATS)), all_order),
        ]
    )
    mixed, grad, west, bias_part0 = call(
        functools.partial(attend_kernel, 0),
        "attend_own",
        pairs,
        [in_smem(at), paired(fields, WZ), paired(cotangent, WZ), paired(east), paired(win_p), paired(win_g)]
        + shared
        + window_picks(0)
        + [entire(jnp.asarray(place_a, BF16))],
        [paired(fields, WZ), paired(cotangent, WZ), paired(strip), entire(bias_block)],
        scratch(1),
        10**10,
    )
    west = shift(west, 0, -1)
    far_back = shift(north[:, 3 * STRIP :], 0, -1)
    bias_part0 = lax.all_to_all(bias_part0, "lon", 0, 0, tiled=True)

    out_bias = shape_of(HEADS * per, 2, WIN, kind=F32)
    mixed, grad, grad_bias = call(
        land_kernel,
        "land",
        pairs,
        [
            paired(mixed, WZ),
            paired(grad, WZ),
            paired(west),
            paired(north),
            paired(far_back),
            entire(bias_part0),
            entire(bias_part1),
            entire(jnp.asarray(land_picks(), BF16)),
        ],
        [paired(fields, WZ), paired(cotangent, WZ), entire(out_bias)],
    )
    grad_bias = grad_bias.reshape(HEADS, per, 2, WIN).transpose(2, 0, 1, 3)
    return mixed.transpose(0, 2, 1, 3), grad.transpose(0, 2, 1, 3), grad_bias


def solution(mesh):
    in_specs = (
        P(None, "lat", "lon", None),
        P(None, "lat", "lon", None),
        P(),
        P(),
        P(),
        P(None, None, "lon", None),
        P(),
        P(),
    )
    out_specs = (
        P(None, "lat", "lon", None),
        P(None, "lat", "lon", None),
        P("lat", None, "lon", None),
    )
    return jax.shard_map(local, mesh=mesh, in_specs=in_specs, out_specs=out_specs, check_vma=False)
```

time: 311 us -> 110 us (0.35)
  the two profiles are of different devices: /device:TPU:1 before, /device:TPU:16 now
where the time goes in v2:
time: 110 us
  Pallas kernels  52.9 us (48%)
  starting transfers between devices  33.8 us (31%)
  waiting for transfers between devices  16.8 us (15%)
  local copies, waits for them, and re-layouts  4.69 us (4%)
    pallas_call x4, Pallas kernels, call(): pl.pallas_call(body, name=name, grid=(steps,), out_shape=tuple((a for a,...  52.9 us
    ppermute x6, starting transfers between devices, shift(): return lax.ppermute(block, ('lat', 'lon'), route)  12.6 us
    all_to_all x1, starting transfers between devices, local(): bias_part1 = lax.all_to_all(bias_part1, 'lon', 0, 0, tiled=True)  9.12 us
    ppermute x6, waiting for transfers between devices, shift(): return lax.ppermute(block, ('lat', 'lon'), route)  9.01 us
    all_to_all x1, waiting for transfers between devices, local(): bias_part0 = lax.all_to_all(bias_part0, 'lon', 0, 0, tiled=True)  7.76 us
    all_to_all x1, starting transfers between devices, local(): bias_part0 = lax.all_to_all(bias_part0, 'lon', 0, 0, tiled=True)  6.33 us
    all_to_all x1, starting transfers between devices, local(): lax.all_to_all(jnp.broadcast_to(mine[None], (parts,) + mine.shape), 'lon'...  5.8 us
  transfers between devices with their start and end apart: 9, of which 3 were waited for; matrix products, arithmetic and copies ran while one was open for 1% of the time, Pallas kernels for 19%

profile of v2, /device:TPU:16, one launch (start us, length us, event | category | flops | bytes accessed | tf_op | source)
XLA Modules:
  0.0 109.7 jit_solution(18241117861709171619)
XLA Ops:
  0.6 1.2 %dynamic_slice.3.types_ref = s32[2]{0:T(128)} dynamic-slice(s32[16]{0:T(128)} %param.25, s32[]{:T(128)S(6)} %select_n.3), dynamic_slice_sizes={2} | dynamic-slice | bytes 20 | tf_op jit(solution)/shard_map/dynamic_slice | solution.py:455
  1.9 5.5 %pack.1 = (bf16[4,336,128]{2,1,0:T(8,128)(2,1)}, bf16[4,336,128]{2,1,0:T(8,128)(2,1)}, bf16[4,144,128]{2,1,0:T(8,128)(2,1)}, bf16[144,128]{1,0:T(8,128)(2,1)}) custom-call(s32[2]{0:T(128)} %dynamic_slice.3.types_ref, bf16[8,12,24,192]{3,2,1,0:T(8,128)(2,1)} %bitcast.13, bf16[8,12,24,192]{3,2,1,0:T(8,128)(2,1)} %bitcast.16, bf16[54,21,144]{2,1,0:T(8,128)(2,1)} %bitcast.21, ...), custom_call_target="tpu_custom_call" | custom-call | flops 1000000000 | bytes 3323336 | tf_op jit(solution)/shard_map/pack/pallas_call | solution.py:406
  7.4 0.0 copy-start.2
  7.4 1.7 %broadcast_in_dim.2 = bf16[16,144,128]{2,1,0:T(8,128)(2,1)} broadcast(bf16[144,128]{1,0:T(8,128)(2,1)} %get-tuple-element.21), dimensions={1,2} | broadcast | bytes 626688 | tf_op jit(solution)/shard_map/broadcast_in_dim | solution.py:482
  9.1 5.8 %all-to-all-start = ((bf16[16,144,128]{2,1,0:T(8,128)(2,1)}), bf16[16,144,128]{2,1,0:T(8,128)(2,1)}, u32[]{:S(2)}, u32[]{:S(2)}) async-start(bf16[16,144,128]{2,1,0:T(8,128)(2,1)} %broadcast_in_dim.2), calls=%async_computation | async-start | bytes 1179648 | tf_op jit(solution)/shard_map/all_to_all | solution.py:481
  14.9 3.8 %collective-permute-start = (bf16[4,336,128]{2,1,0:T(8,128)(2,1)S(1)}, bf16[4,336,128]{2,1,0:T(8,128)(2,1)}, u32[]{:S(2)}, u32[]{:S(2)}) collective-permute-start(bf16[4,336,128]{2,1,0:T(8,128)(2,1)S(1)} %copy-done.2), channel_id=1, source_target_pairs={{1,0},{2,1},{3,2},{4,3},{5,4},{6,5},{7,6},{8,7},{9,8},{10,9},{11,1... | collective-permute-start | bytes 1032200 | tf_op jit(solution)/shard_map/ppermute | solution.py:440
  18.8 0.4 collective-permute-start.1
  19.2 0.6 pad_add_fusion.refs_0_
  19.8 7.7 %collective-permute-done.2.refs_5_ = bf16[4,144,128]{2,1,0:T(8,128)(2,1)S(1)} collective-permute-done((bf16[4,144,128]{2,1,0:T(8,128)(2,1)S(1)}, bf16[4,144,128]{2,1,0:T(8,128)(2,1)S(1)}, u32[]{:S(2)}, u32[]{:S(2)}) %collective-permute-start.2) | collective-permute-done | bytes 147488 | tf_op jit(solution)/shard_map/ppermute | solution.py:440
  27.6 0.8 copy-done.1
  28.4 0.0 all-to-all-done.refs_9_
  28.4 20.5 %attend_south.1 = (bf16[4,288,192]{2,1,0:T(8,128)(2,1)}, bf16[4,288,192]{2,1,0:T(8,128)(2,1)}, bf16[4,480,128]{2,1,0:T(8,128)(2,1)}, bf16[16,80,128]{2,1,0:T(8,128)(2,1)}) custom-call(s32[3]{0:T(128)} %pad_add_fusion.refs_0_, bf16[8,12,24,192]{3,2,1,0:T(8,128)(2,1)} %bitcast.14, bf16[8,12,24,192]{3,2,1,0:T(8,128)(2,1)} %bitcast.17, ...), custom_call_target="tpu_custom_call" | custom-call | flops 10000000000 | bytes 7577868 | tf_op jit(solution)/shard_map/attend_south/pallas_call | solution.py:406
  48.8 9.1 %all-to-all-start.2 = ((bf16[16,80,128]{2,1,0:T(8,128)(2,1)}), bf16[16,80,128]{2,1,0:T(8,128)(2,1)}, u32[]{:S(2)}, u32[]{:S(2)}) async-start(bf16[16,80,128]{2,1,0:T(8,128)(2,1)} %get-tuple-element.29), calls=%async_computation.2 | async-start | bytes 655360 | tf_op jit(solution)/shard_map/all_to_all | solution.py:521
  58.0 7.8 %collective-permute-start.4 = (bf16[4,480,128]{2,1,0:T(8,128)(2,1)}, bf16[4,480,128]{2,1,0:T(8,128)(2,1)}, u32[]{:S(2)}, u32[]{:S(2)}) collective-permute-start(bf16[4,480,128]{2,1,0:T(8,128)(2,1)} %get-tuple-element.27), channel_id=1, source_target_pairs={{112,0},{113,1},{114,2},{115,3},{116,4},{117,5},{118,6},{119,7},{1... | collective-permute-start | bytes 1474568 | tf_op jit(solution)/shard_map/ppermute | solution.py:440
  65.8 21.1 %attend_own.1 = (bf16[8,12,24,192]{3,2,1,0:T(8,128)(2,1)}, bf16[8,12,24,192]{3,2,1,0:T(8,128)(2,1)}, bf16[4,336,128]{2,1,0:T(8,128)(2,1)}, bf16[16,80,128]{2,1,0:T(8,128)(2,1)}) custom-call(s32[3]{0:T(128)} %pad_add_fusion.refs_0_, bf16[8,12,24,192]{3,2,1,0:T(8,128)(2,1)} %bitcast.15, bf16[8,12,24,192]{3,2,1,0:T(8,128)(2,1)} %bitcast.18, ...), custom_call_target="tpu_custom_call" | custom-call | flops 10000000000 | bytes 9164556 | tf_op jit(solution)/shard_map/attend_own/pallas_call | solution.py:406
  86.9 0.1 collective-permute-start.3
  87.0 6.3 %all-to-all-start.1 = ((bf16[16,80,128]{2,1,0:T(8,128)(2,1)}), bf16[16,80,128]{2,1,0:T(8,128)(2,1)}, u32[]{:S(2)}, u32[]{:S(2)}) async-start(bf16[16,80,128]{2,1,0:T(8,128)(2,1)} %get-tuple-element.28), calls=%async_computation.1 | async-start | bytes 655360 | tf_op jit(solution)/shard_map/all_to_all | solution.py:544
  93.3 0.0 collective-permute-done.4.north_ref
  93.4 0.9 slice.4
  94.3 0.4 collective-permute-start.5
  94.7 7.8 %all-to-all-done.1.bias0_ref = bf16[16,80,128]{2,1,0:T(8,128)(2,1)} async-done(((bf16[16,80,128]{2,1,0:T(8,128)(2,1)}), bf16[16,80,128]{2,1,0:T(8,128)(2,1)}, u32[]{:S(2)}, u32[]{:S(2)}) %all-to-all-start.1) | async-done | bytes 327712 | tf_op jit(solution)/shard_map/all_to_all | solution.py:544
  102.5 0.0 collective-permute-done.3.west_ref
  102.5 1.3 %collective-permute-done.5.far_ref = bf16[4,144,128]{2,1,0:T(8,128)(2,1)} collective-permute-done((bf16[4,144,128]{2,1,0:T(8,128)(2,1)S(1)}, bf16[4,144,128]{2,1,0:T(8,128)(2,1)}, u32[]{:S(2)}, u32[]{:S(2)}) %collective-permute-start.5) | collective-permute-done | bytes 147488 | tf_op jit(solution)/shard_map/ppermute | solution.py:440
  103.7 5.8 %land.1 = (bf16[8,12,24,192]{3,2,1,0:T(8,128)(2,1)}, bf16[8,12,24,192]{3,2,1,0:T(8,128)(2,1)}, f32[54,2,144]{2,1,0:T(2,128)}) custom-call(bf16[8,12,24,192]{3,2,1,0:T(8,128)(2,1)} %get-tuple-element.24.mixed_ref, bf16[8,12,24,192]{3,2,1,0:T(8,128)(2,1)} %get-tuple-element.25.grad_ref, bf16[4,336,128]{2,1,0:T(8,128)(2,1)} %collective-permute-done.3.west_ref, ...), custom_call_target="tpu_custom_call" | custom-call | flops 1000000000 | bytes 5552896 | tf_op jit(solution)/shard_map/land/pallas_call | solution.py:406
  (12 shorter events, 0.0 us)
Async XLA Ops:
  7.4 7.6 %copy-start.2 = (bf16[4,336,128]{2,1,0:T(8,128)(2,1)S(1)}, bf16[4,336,128]{2,1,0:T(8,128)(2,1)}, u32[]{:S(2)}) copy-start(bf16[4,336,128]{2,1,0:T(8,128)(2,1)} %get-tuple-element.18) | copy-start | bytes 1032196
  7.4 11.4 %copy-start = (bf16[4,336,128]{2,1,0:T(8,128)(2,1)S(1)}, bf16[4,336,128]{2,1,0:T(8,128)(2,1)}, u32[]{:S(2)}) copy-start(bf16[4,336,128]{2,1,0:T(8,128)(2,1)} %get-tuple-element.19) | copy-start | bytes 1032196
  7.4 11.8 %copy-start.4 = (bf16[4,144,128]{2,1,0:T(8,128)(2,1)S(1)}, bf16[4,144,128]{2,1,0:T(8,128)(2,1)}, u32[]{:S(2)}) copy-start(bf16[4,144,128]{2,1,0:T(8,128)(2,1)} %get-tuple-element.20) | copy-start | bytes 442372
  9.1 19.2 %all-to-all-start = ((bf16[16,144,128]{2,1,0:T(8,128)(2,1)}), bf16[16,144,128]{2,1,0:T(8,128)(2,1)}, u32[]{:S(2)}, u32[]{:S(2)}) async-start(bf16[16,144,128]{2,1,0:T(8,128)(2,1)} %broadcast_in_dim.2), calls=%async_computation | async-start | bytes 1179648 | tf_op jit(solution)/shard_map/all_to_all | solution.py:481
  14.9 12.6 %collective-permute-start = (bf16[4,336,128]{2,1,0:T(8,128)(2,1)S(1)}, bf16[4,336,128]{2,1,0:T(8,128)(2,1)}, u32[]{:S(2)}, u32[]{:S(2)}) collective-permute-start(bf16[4,336,128]{2,1,0:T(8,128)(2,1)S(1)} %copy-done.2), channel_id=1, source_target_pairs={{1,0},{2,1},{3,2},{4,3},{5,4},{6,5},{7,6},{8,7},{9,8},{10,9},{11,1... | collective-permute-start | bytes 1032200 | tf_op jit(solution)/shard_map/ppermute | solution.py:440
  18.8 8.8 %collective-permute-start.1 = (bf16[4,336,128]{2,1,0:T(8,128)(2,1)S(1)}, bf16[4,336,128]{2,1,0:T(8,128)(2,1)S(1)}, u32[]{:S(2)}, u32[]{:S(2)}) collective-permute-start(bf16[4,336,128]{2,1,0:T(8,128)(2,1)S(1)} %copy-done), channel_id=1, source_target_pairs={{16,0},{17,1},{18,2},{19,3},{20,4},{21,5},{22,6},{23,7},{24,8},{25... | collective-permute-start | bytes 1032200 | tf_op jit(solution)/shard_map/ppermute | solution.py:440
  19.2 8.4 %collective-permute-start.2 = (bf16[4,144,128]{2,1,0:T(8,128)(2,1)S(1)}, bf16[4,144,128]{2,1,0:T(8,128)(2,1)S(1)}, u32[]{:S(2)}, u32[]{:S(2)}) collective-permute-start(bf16[4,144,128]{2,1,0:T(8,128)(2,1)S(1)} %copy-done.4), channel_id=1, source_target_pairs={{17,0},{18,1},{19,2},{20,3},{21,4},{22,5},{23,6},{24,7},{25,8},{26... | collective-permute-start | bytes 442376 | tf_op jit(solution)/shard_map/ppermute | solution.py:440
  27.6 0.8 copy-start.3
  27.6 0.8 copy-start.1
  48.8 38.2 %all-to-all-start.2 = ((bf16[16,80,128]{2,1,0:T(8,128)(2,1)}), bf16[16,80,128]{2,1,0:T(8,128)(2,1)}, u32[]{:S(2)}, u32[]{:S(2)}) async-start(bf16[16,80,128]{2,1,0:T(8,128)(2,1)} %get-tuple-element.29), calls=%async_computation.2 | async-start | bytes 655360 | tf_op jit(solution)/shard_map/all_to_all | solution.py:521
  58.0 35.4 %collective-permute-start.4 = (bf16[4,480,128]{2,1,0:T(8,128)(2,1)}, bf16[4,480,128]{2,1,0:T(8,128)(2,1)}, u32[]{:S(2)}, u32[]{:S(2)}) collective-permute-start(bf16[4,480,128]{2,1,0:T(8,128)(2,1)} %get-tuple-element.27), channel_id=1, source_target_pairs={{112,0},{113,1},{114,2},{115,3},{116,4},{117,5},{118,6},{119,7},{1... | collective-permute-start | bytes 1474568 | tf_op jit(solution)/shard_map/ppermute | solution.py:440
  86.9 15.6 %collective-permute-start.3 = (bf16[4,336,128]{2,1,0:T(8,128)(2,1)}, bf16[4,336,128]{2,1,0:T(8,128)(2,1)}, u32[]{:S(2)}, u32[]{:S(2)}) collective-permute-start(bf16[4,336,128]{2,1,0:T(8,128)(2,1)} %get-tuple-element.26), channel_id=1, source_target_pairs={{15,0},{0,1},{1,2},{2,3},{3,4},{4,5},{5,6},{6,7},{7,8},{8,9},{9,10... | collective-permute-start | bytes 1032200 | tf_op jit(solution)/shard_map/ppermute | solution.py:440
  87.0 15.5 %all-to-all-start.1 = ((bf16[16,80,128]{2,1,0:T(8,128)(2,1)}), bf16[16,80,128]{2,1,0:T(8,128)(2,1)}, u32[]{:S(2)}, u32[]{:S(2)}) async-start(bf16[16,80,128]{2,1,0:T(8,128)(2,1)} %get-tuple-element.28), calls=%async_computation.1 | async-start | bytes 655360 | tf_op jit(solution)/shard_map/all_to_all | solution.py:544
  94.3 9.5 %collective-permute-start.5 = (bf16[4,144,128]{2,1,0:T(8,128)(2,1)S(1)}, bf16[4,144,128]{2,1,0:T(8,128)(2,1)}, u32[]{:S(2)}, u32[]{:S(2)}) collective-permute-start(bf16[4,144,128]{2,1,0:T(8,128)(2,1)S(1)} %slice.4), channel_id=1, source_target_pairs={{15,0},{0,1},{1,2},{2,3},{3,4},{4,5},{5,6},{6,7},{7,8},{8,9},{9,10... | collective-permute-start | bytes 442376 | tf_op jit(solution)/shard_map/ppermute | solution.py:440

commit v3 on v2

v3 whole, which is shorter than its diff:
```python
import functools

import jax
import jax.numpy as jnp
import numpy as np
from jax import lax
from jax.experimental import pallas as pl
from jax.experimental.pallas import tpu as pltpu
from jax.sharding import PartitionSpec as P

HEADS = 6
WZ = 2
WLAT = 12
WLON = 6
WIN = 144
SLAT = 6
SLON = 3
HEAD_DIM = 32
MAIN = 128
REST = WIN - MAIN
LANES = 896
ROWS = 64

NEGATIVE = -1e30
EPSILON = 1e-05
LOG2E = 1.4426950408889634
SCALE = float(HEAD_DIM) ** (-0.5)

F32 = jnp.float32
BF16 = jnp.bfloat16


def nn(a, b):
    return lax.dot_general(a, b, (((1,), (0,)), ((), ())), preferred_element_type=F32)


def nt(a, b):
    return lax.dot_general(a, b, (((1,), (1,)), ((), ())), preferred_element_type=F32)


def tn(a, b):
    return lax.dot_general(a, b, (((0,), (0,)), ((), ())), preferred_element_type=F32)


def lane_of(head, query):
    return np.where(query < MAIN, head * MAIN + query, HEADS * MAIN + head * REST + query - MAIN)


COLS = 2 * WLON
LATS = 2 * WLAT
PAIR = WZ * COLS * LATS
STRIP = 112
CORNER = 48


def tokens(columns, rows):
    return [(z, c, r) for z in range(WZ) for c in columns for r in rows]


def window(b, w):
    return [
        (z, SLON + WLON * w + c, SLAT + WLAT * b + r)
        for z in range(WZ)
        for r in range(WLAT)
        for c in range(WLON)
    ]


def pick(wanted, sources):
    where, at = {}, 0
    for source, length in sources:
        for n, token in enumerate(source):
            where.setdefault(token, at + n)
        at += length
    out = np.zeros((len(wanted), at), np.float32)
    for n, token in enumerate(wanted):
        if token in where:
            out[n, where[token]] = 1
    return out


def padded(rows, length):
    return np.pad(rows, ((0, length - rows.shape[0]), (0, 0)))


OWN_WEST = tokens(range(SLON, SLON + WLON), range(LATS))
OWN_EAST = tokens(range(SLON + WLON, COLS), range(LATS))
EAST_COLUMNS = range(COLS, COLS + SLON)
EAST = tokens(EAST_COLUMNS, range(SLAT, LATS))
SOUTH = tokens(range(SLON, COLS), range(LATS, LATS + SLAT))
FAR = tokens(EAST_COLUMNS, range(LATS, LATS + SLAT))


def sources_of(b, w):
    if w == 0:
        parts = [(OWN_WEST, len(OWN_WEST))]
    else:
        parts = [(OWN_EAST, len(OWN_EAST)), (EAST, STRIP)]
    if b == 1:
        parts.append((SOUTH, STRIP))
        if w == 1:
            parts.append((FAR, CORNER))
    return parts


def send_picks():
    own = [(tokens(range(COLS), range(LATS)), PAIR)]
    west = pick(tokens(range(SLON), range(SLAT, LATS)), own)
    north = pick(tokens(range(SLON, COLS), range(SLAT)), own)
    corner = pick(tokens(range(SLON), range(SLAT)), own)
    return np.concatenate([padded(west, STRIP), padded(north, STRIP), padded(corner, CORNER)])


def land_picks():
    sources = [
        (tokens(range(SLON), range(SLAT, LATS)), STRIP),
        (tokens(range(SLON, COLS), range(SLAT)), STRIP),
        (tokens(range(SLON), range(SLAT)), CORNER),
    ]
    return pick(tokens(range(COLS), range(LATS)), sources)


def bias_picks(parts):
    per = WIN // parts
    pick = np.zeros((parts, ROWS, LANES), np.float32)
    for k in range(parts):
        for h in range(HEADS):
            for r in range(per):
                pick[k, h * per + r, lane_of(h, k * per + r)] = 1
    return pick.reshape(parts * ROWS, LANES)


def head_blocks(tokens, head_masks):
    pieces = [tokens[:MAIN] * head_masks[h] for h in range(HEADS)]
    pieces += [tokens[MAIN:] * head_masks[h] for h in range(HEADS)]
    pieces.append(jnp.zeros((LANES - HEADS * WIN, tokens.shape[1]), tokens.dtype))
    return jnp.concatenate(pieces, axis=0)


def own_heads(wide):
    main, rest = [], []
    for h in range(HEADS):
        rows = wide[h * HEAD_DIM : (h + 1) * HEAD_DIM]
        main.append(rows[:, h * MAIN : (h + 1) * MAIN])
        left = HEADS * MAIN + h * REST
        rest.append(rows[:, left : left + REST])
    return jnp.concatenate(
        [jnp.concatenate(main, axis=0), jnp.concatenate(rest, axis=0)], axis=1
    )


def pack(rows_a, rows_b):
    return jnp.concatenate(
        [
            rows_a[:, :MAIN],
            rows_b[:, :MAIN],
            jnp.concatenate([rows_a[:, MAIN:], rows_b[:, MAIN:]], axis=1),
        ],
        axis=0,
    ).astype(BF16)


def unpack(packed):
    count = packed.shape[0] // 3
    half = packed.shape[1] // 2
    last = packed[2 * count :]
    return (
        jnp.concatenate([packed[:count], last[:, :half]], axis=1),
        jnp.concatenate([packed[count : 2 * count], last[:, half:]], axis=1),
    )


def pack_kernel(
    at_ref,
    types_ref,
    fields_ref,
    cot_ref,
    table_ref,
    pick_ref,
    eye_ref,
    east_ref,
    south_ref,
    far_ref,
    mine_ref,
):
    features = fields_ref.shape[-1]
    table = table_ref[...].astype(F32)
    kind = lax.broadcasted_iota(jnp.int32, (1, table.shape[1], 1), 1)
    chosen = []
    for b in range(2):
        one = jnp.sum(jnp.where(kind == types_ref[2 * at_ref[0] + b], table, 0.0), axis=1)
        chosen.append(one.astype(BF16))
        chosen.append(jnp.zeros((ROWS - one.shape[0], WIN), BF16))
    mine = nt(eye_ref[...], jnp.concatenate(chosen, axis=0)).astype(BF16)
    mine_ref[...] = jnp.broadcast_to(mine[None], mine_ref.shape)
    for g in range(east_ref.shape[0]):
        rows = [
            nn(pick_ref[...], ref[WZ * g : WZ * (g + 1)].reshape(-1, features))
            for ref in (fields_ref, cot_ref)
        ]
        at = 0
        for ref, count in ((east_ref, STRIP), (south_ref, STRIP), (far_ref, CORNER)):
            ref[g] = pack(*(r[at : at + count] for r in rows))
            at += count


def prepare_weights(qkv_ref, proj_ref, eye, weights):
    features = proj_ref.shape[0]
    for n in range(3):
        weights[n] = qkv_ref[:, n * features : (n + 1) * features]
    weights[3] = nt(eye, weights[1]).astype(BF16)
    weights[4] = nt(eye, weights[2]).astype(BF16)
    weights[5] = nt(eye, proj_ref[...]).astype(BF16)


def wide_bias(b, bias_ref, bias_pick_ref):
    table = jnp.concatenate(
        [bias_ref[k, :, b * ROWS : (b + 1) * ROWS] for k in range(bias_ref.shape[0])], axis=1
    )
    return nn(table, bias_pick_ref[...]) * LOG2E


def masked_tables(wide, at_ref, valid_ref, tables):
    key = lax.broadcasted_iota(jnp.int32, (WIN, 1), 0)
    lane = lax.broadcasted_iota(jnp.int32, (1, LANES), 1)
    query = jnp.where(lane < HEADS * MAIN, lane % MAIN, MAIN + (lane - HEADS * MAIN) % REST)
    key_row = (key // WLON) % WLAT
    query_row = (query // WLON) % WLAT
    last = at_ref[0] == at_ref[2] - 1
    same = (key_row < SLAT) == (query_row < SLAT)
    lat_rows, lon_columns = valid_ref.shape
    valid_rows = jnp.concatenate(
        [valid_ref[lat_rows - SLAT :, :], valid_ref[:SLAT, :]], axis=0
    ).astype(F32)
    row_pick = (key_row == lax.broadcasted_iota(jnp.int32, (WIN, WLAT), 1)).astype(F32)
    key_valid = nn(row_pick, valid_rows)
    column = lax.broadcasted_iota(jnp.int32, (WIN, lon_columns), 1)
    for w in range(2):
        wanted = at_ref[1] * COLS + SLON + WLON * w + key % WLON
        wanted = jnp.where(wanted >= lon_columns, wanted - lon_columns, wanted)
        is_valid = (
            jnp.sum(jnp.where(column == wanted, key_valid, 0.0), axis=1, keepdims=True) > 0.5
        )
        allowed = jnp.logical_and(same, is_valid) | jnp.logical_not(last)
        tables[w] = jnp.where(allowed, wide, NEGATIVE)


def one_window(flat_f, flat_c, chosen, gain, proj_weight, weights, bias, eye, head_masks):
    x = nn(chosen, flat_f)
    cot = nn(chosen, flat_c).astype(BF16)
    mean = jnp.mean(x, axis=1, keepdims=True)
    centered = x - mean
    variance = jnp.mean(centered * centered, axis=1, keepdims=True)
    inverse = lax.rsqrt(variance + EPSILON)
    hat = centered * inverse
    normed = (hat * gain).astype(BF16)
    queries = nn(normed, weights[0]).astype(BF16)
    keys = nn(normed, weights[1]).astype(BF16)
    values = nn(normed, weights[2]).astype(BF16)
    keys_t = nt(weights[3], normed).astype(BF16)
    values_t = nt(weights[4], normed).astype(BF16)
    grad_att = nt(cot, proj_weight).astype(BF16)
    q_blocks = head_blocks(queries, head_masks)
    g_blocks = head_blocks(grad_att, head_masks)
    scores = nt(keys, q_blocks) * (SCALE * LOG2E) + bias
    exponent = jnp.exp2(scores - jnp.max(scores, axis=0, keepdims=True))
    soft = exponent * (1.0 / jnp.sum(exponent, axis=0, keepdims=True))
    soft_bf = soft.astype(BF16)
    grad_soft = nt(values, g_blocks)
    delta = jnp.sum(soft * grad_soft, axis=0, keepdims=True)
    grad_scores = soft * (grad_soft - delta)
    grad_bf = grad_scores.astype(BF16)
    grad_values = nn(soft_bf, g_blocks).astype(BF16)
    grad_keys = (nn(grad_bf, q_blocks) * SCALE).astype(BF16)
    attended_t = own_heads(nn(values_t, soft_bf)).astype(BF16)
    grad_queries_t = (own_heads(nn(keys_t, grad_bf)) * SCALE).astype(BF16)
    projected_t = nn(weights[5], attended_t).astype(BF16)
    projected = nt(eye[:WIN, :WIN], projected_t).astype(BF16)
    grad_queries = nt(eye[:WIN, :WIN], grad_queries_t).astype(BF16)
    grad_normed = (
        nt(grad_queries, weights[0]) + nt(grad_keys, weights[1]) + nt(grad_values, weights[2])
    )
    grad_hat = grad_normed * gain
    grad_x = inverse * (
        grad_hat
        - jnp.mean(grad_hat, axis=1, keepdims=True)
        - hat * jnp.mean(grad_hat * hat, axis=1, keepdims=True)
    )
    return projected, grad_x.astype(BF16), grad_scores


def run_windows(todo, r, tables, pair):
    features = r["fields"].shape[-1]
    levels = slice(WZ * pair, WZ * (pair + 1))
    lane_head = lax.broadcasted_iota(jnp.int32, (1, features), 1) // HEAD_DIM
    head_masks = [(lane_head == h).astype(F32).astype(BF16) for h in range(HEADS)]
    eye = r["eye"][...]
    halos = {k: unpack(r[k][pair]) for k in ("east", "south", "far") if k in r}
    done, total = [], None
    for b, w in todo:
        flats = []
        for n, ref in enumerate((r["fields"], r["cot"])):
            columns = slice(SLON, SLON + WLON) if w == 0 else slice(SLON + WLON, COLS)
            parts = [ref[levels, columns].reshape(-1, features)]
            if w == 1:
                parts.append(halos["east"][n])
            if b == 1:
                parts.append(halos["south"][n])
                if w == 1:
                    parts.append(halos["far"][n])
            flats.append(jnp.concatenate(parts, axis=0))
        projected, grad, scores = one_window(
            *flats,
            r["pick%d" % w][...],
            r["gain"][...],
            r["proj"][...],
            r["weights"],
            tables(w),
            eye,
            head_masks,
        )
        done.append((projected, grad))
        total = scores if total is None else total + scores
    return done, total


def first_kernel(names, group, *refs):
    r = dict(zip(names, refs))

    @pl.when(pl.program_id(0) == 0)
    def start():
        prepare_weights(r["qkv"], r["proj"], r["eye"][...], r["weights"])
        r["table"][...] = wide_bias(0, r["bias"], r["bias_pick"])
        r["sum"][...] = jnp.zeros_like(r["sum"])

    totals = []
    for pair in range(group):
        done, total = run_windows([(0, 1)], r, lambda w: r["table"][...], pair)
        r["win_p"][pair], r["win_g"][pair] = done[0]
        totals.append(total)
    r["sum"][...] += sum(totals[1:], totals[0])


def south_kernel(names, group, *refs):
    r = dict(zip(names, refs))

    @pl.when(pl.program_id(0) == 0)
    def start():
        wide = wide_bias(1, r["bias"], r["bias_pick"])
        masked_tables(wide, r["at"], r["valid"], r["tables"])
        r["sum"][...] = jnp.zeros_like(r["sum"])

    for pair in range(group):
        done, total = run_windows([(1, 0), (1, 1)], r, lambda w: r["tables"][w], pair)
        r["sum"][...] += total
        placed = []
        for n, (first, out) in enumerate(
            ((r["first_p"], r["win_p"]), (r["first_g"], r["win_g"]))
        ):
            both = jnp.concatenate([done[0][n], done[1][n]], axis=0)
            out[pair] = both
            placed.append(nn(r["place"][...], jnp.concatenate([first[pair], both], axis=0)))
        r["west"][pair] = pack(*(p[:STRIP] for p in placed))
        r["north"][pair] = pack(*(p[STRIP : 2 * STRIP] for p in placed))
        r["corner"][pair] = pack(*(p[2 * STRIP :] for p in placed))


def last_kernel(names, group, *refs):
    r = dict(zip(names, refs))
    step = pl.program_id(0)
    features = r["fields"].shape[-1]

    @pl.when(step == 0)
    def start():
        r["sum"][...] = r["sum0"][...]

    for pair in range(group):
        done, total = run_windows([(0, 0)], r, lambda w: r["table"][...], pair)
        r["sum"][...] += total
        levels = slice(WZ * pair, WZ * (pair + 1))
        for n, (first, south, base, out) in enumerate(
            (
                (r["first_p"], r["south_p"], r["fields"], r["mixed"]),
                (r["first_g"], r["south_g"], r["cot"], r["grad"]),
            )
        ):
            every = jnp.concatenate([done[0][n], first[pair], south[pair]], axis=0)
            part = nn(r["place"][...], every)
            inner = part.reshape(WZ, COLS - SLON, LATS, features)
            out[levels, :SLON] = base[levels, :SLON]
            out[levels, SLON:] = (base[levels, SLON:].astype(F32) + inner).astype(BF16)

    @pl.when(step == pl.num_programs(0) - 1)
    def finish():
        out = r["bias_out"]
        for b, ref in enumerate((r["sum"], r["sum1"])):
            wide = nt(ref[...].astype(BF16), r["bias_pick"][...])
            top, low = wide[:80], wide[80:]
            for k in range(out.shape[0]):
                left = top[:, k * ROWS : (k + 1) * ROWS]
                right = low[:, k * ROWS : (k + 1) * ROWS]
                right = jnp.concatenate([right, jnp.zeros((160 - WIN, ROWS), F32)], axis=0)
                block = jnp.concatenate([left, right], axis=1).astype(BF16)
                out[k, 80 * b : 80 * (b + 1)] = block


def add_strips(strips, base_refs, place_ref, out_refs):
    for pair in range(strips[0].shape[0]):
        pieces = [unpack(ref[pair]) for ref in strips]
        levels = slice(WZ * pair, WZ * (pair + 1))
        for n, (base, out) in enumerate(zip(base_refs, out_refs)):
            own = base[levels]
            part = nn(place_ref[...], jnp.concatenate([p[n] for p in pieces], axis=0))
            out[levels] = (own.astype(F32) + part.reshape(own.shape)).astype(BF16)


def land_kernel(
    mixed_ref, grad_ref, west_ref, north_ref, far_ref, place_ref, out_m_ref, out_g_ref
):
    strips = (west_ref, north_ref, far_ref)
    add_strips(strips, (mixed_ref, grad_ref), place_ref, (out_m_ref, out_g_ref))


def bias_kernel(bias_ref, out_ref):
    count = out_ref.shape[0]
    total = bias_ref[0].astype(F32)
    for k in range(1, bias_ref.shape[0]):
        total = total + bias_ref[k].astype(F32)
    for b in range(2):
        turned = total[80 * b : 80 * (b + 1)].T
        whole = jnp.concatenate([turned[:ROWS], turned[ROWS:, : WIN - 80]], axis=1)
        out_ref[:, b, :] = whole[:count]


def by_pair(array, size=1):
    return pl.BlockSpec((size,) + array.shape[1:], lambda g: (g,) + (0,) * (array.ndim - 1))


def whole(array):
    return pl.BlockSpec(array.shape, lambda g: (0,) * array.ndim)


def shape_of(*dims, kind=BF16):
    return jax.ShapeDtypeStruct(dims, kind)


def call(body, name, steps, inputs, outputs, scratch=(), flops=10**9, aliases=()):
    in_specs = [spec for _, spec in inputs]
    bytes_moved = sum(a.size * a.dtype.itemsize for a, _ in inputs) + sum(
        int(np.prod(a.shape)) * a.dtype.itemsize for a, _ in outputs
    )
    return pl.pallas_call(
        body,
        name=name,
        grid=(steps,),
        out_shape=tuple(a for a, _ in outputs),
        in_specs=in_specs,
        out_specs=tuple(spec for _, spec in outputs),
        scratch_shapes=list(scratch),
        input_output_aliases=dict(aliases),
        compiler_params=pltpu.CompilerParams(vmem_limit_bytes=64 * 1024 * 1024),
        cost_estimate=pl.CostEstimate(
            flops=flops, bytes_accessed=bytes_moved, transcendentals=0
        ),
    )(*(a for a, _ in inputs))


def paired(array, size=1):
    return (array, by_pair(array, size))


def entire(array):
    return (array, whole(array))


def in_smem(array):
    return (array, pl.BlockSpec(memory_space=pltpu.SMEM))


def attend(body, name, steps, inputs, outputs, scratch=()):
    scratch = dict(scratch)
    names = list(inputs) + list(outputs) + list(scratch)
    group = inputs["fields"][1].block_shape[0] // WZ
    results = call(
        functools.partial(body, names, group),
        name,
        steps,
        list(inputs.values()),
        list(outputs.values()),
        list(scratch.values()),
        10**10,
    )
    return dict(zip(outputs, results))


def shift(block, lat_step, lon_step):
    lats, lons = lax.axis_size("lat"), lax.axis_size("lon")
    route = [
        (((a + lat_step) % lats) * lons + (o + lon_step) % lons, a * lons + o)
        for a in range(lats)
        for o in range(lons)
    ]
    return lax.ppermute(block, ("lat", "lon"), route)


def local(
    fields, cotangent, norm_gain, qkv_weight, proj_weight, bias_table, window_types, valid_mask
):
    fields = fields.transpose(0, 2, 1, 3)
    cotangent = cotangent.transpose(0, 2, 1, 3)
    levels, lon_cells, lat_cells, features = fields.shape
    lat_at = lax.axis_index("lat")
    lon_at = lax.axis_index("lon")
    parts = lax.axis_size("lon")
    per = WIN // parts
    pairs = levels // WZ
    at = jnp.stack([lat_at, lon_at, lax.axis_size("lat")]).astype(jnp.int32)
    strip = shape_of(pairs, 3 * STRIP, MAIN)
    corner = shape_of(pairs, 3 * CORNER, MAIN)

    table = bias_table.transpose(1, 2, 0, 3).reshape(HEADS * per, -1, WIN)
    east, south, far, mine = call(
        pack_kernel,
        "pack",
        1,
        [
            in_smem(at),
            in_smem(window_types),
            entire(fields),
            entire(cotangent),
            entire(table),
            entire(jnp.asarray(send_picks(), BF16)),
            entire(jnp.asarray(np.eye(WIN), BF16)),
        ],
        [entire(strip), entire(strip), entire(corner), entire(shape_of(parts, WIN, 2 * ROWS))],
    )
    east = shift(east, 0, 1)
    bias = lax.all_to_all(mine, "lon", 0, 0, tiled=True)
    south, far, bias = lax.optimization_barrier((south, far, bias))
    south = shift(south, 1, 0)
    far = shift(far, 1, 1)

    gain = norm_gain.reshape(1, -1)
    windows = {(b, w): window(b, w) for b in range(2) for w in range(2)}
    steps = 2
    group = pairs // steps

    def constant(rows):
        return entire(jnp.asarray(rows, BF16))

    def split(array):
        return paired(array, group)

    def strip_of(count):
        return split(shape_of(pairs, 3 * count, MAIN))

    def tokens_of(count):
        return split(shape_of(pairs, count, features))

    def picked(b, w):
        return constant(pick(windows[b, w], sources_of(b, w)))

    wide_sum = entire(shape_of(WIN, LANES, kind=F32))
    common = {
        "fields": paired(fields, WZ * group),
        "cot": paired(cotangent, WZ * group),
        "gain": entire(gain),
        "proj": entire(proj_weight),
        "eye": constant(np.eye(features)),
    }
    bias_pick = constant(bias_picks(parts))
    first = attend(
        first_kernel,
        "attend_first",
        steps,
        common
        | {
            "east": split(east),
            "qkv": entire(qkv_weight),
            "bias": entire(bias),
            "bias_pick": bias_pick,
            "pick1": picked(0, 1),
        },
        {
            "win_p": tokens_of(WIN),
            "win_g": tokens_of(WIN),
            "weights": entire(shape_of(6, features, features)),
            "table": wide_sum,
            "sum": wide_sum,
        },
    )
    order = [(windows[0, 1] + windows[1, 0] + windows[1, 1], 3 * WIN)]
    place = [
        padded(pick(EAST, order), STRIP),
        padded(pick(SOUTH, order), STRIP),
        padded(pick(FAR, order), CORNER),
    ]
    below = attend(
        south_kernel,
        "attend_south",
        steps,
        common
        | {
            "at": in_smem(at),
            "east": split(east),
            "south": split(south),
            "far": split(far),
            "first_p": split(first["win_p"]),
            "first_g": split(first["win_g"]),
            "weights": entire(first["weights"]),
            "bias": entire(bias),
            "valid": entire(valid_mask),
            "bias_pick": bias_pick,
            "pick0": picked(1, 0),
            "pick1": picked(1, 1),
            "place": constant(np.concatenate(place)),
        },
        {
            "win_p": tokens_of(2 * WIN),
            "win_g": tokens_of(2 * WIN),
            "west": strip_of(STRIP),
            "north": strip_of(STRIP),
            "corner": strip_of(CORNER),
            "sum": wide_sum,
        },
        {"tables": pltpu.VMEM((2, WIN, LANES), F32)},
    )
    north = shift(below["north"], -1, 0)
    far_back = shift(below["corner"], -1, -1)
    west = shift(below["west"], 0, -1)
    every = [(windows[0, 0] + windows[0, 1] + windows[1, 0] + windows[1, 1], 4 * WIN)]
    place = pick(tokens(range(SLON, COLS), range(LATS)), every)
    last = attend(
        last_kernel,
        "attend_last",
        steps,
        common
        | {
            "first_p": split(first["win_p"]),
            "first_g": split(first["win_g"]),
            "south_p": split(below["win_p"]),
            "south_g": split(below["win_g"]),
            "weights": entire(first["weights"]),
            "table": entire(first["table"]),
            "sum0": entire(first["sum"]),
            "sum1": entire(below["sum"]),
            "bias_pick": bias_pick,
            "pick0": picked(0, 0),
            "place": constant(place),
        },
        {
            "mixed": paired(shape_of(*fields.shape), WZ * group),
            "grad": paired(shape_of(*fields.shape), WZ * group),
            "bias_out": entire(shape_of(parts, 160, 2 * ROWS)),
        },
        {"sum": pltpu.VMEM((WIN, LANES), F32)},
    )
    mixed, grad = last["mixed"], last["grad"]
    bias_sums = lax.all_to_all(last["bias_out"], "lon", 0, 0, tiled=True)

    out_bias = shape_of(HEADS * per, 2, WIN, kind=F32)
    block = paired(shape_of(*fields.shape), WZ * group)
    mixed, grad = call(
        land_kernel,
        "land",
        steps,
        [
            paired(mixed, WZ * group),
            paired(grad, WZ * group),
            split(west),
            split(north),
            split(far_back),
            constant(land_picks()),
        ],
        [block, block],
        flops=10**11,
    )
    (grad_bias,) = call(bias_kernel, "bias_sum", 1, [entire(bias_sums)], [entire(out_bias)])
    grad_bias = grad_bias.reshape(HEADS, per, 2, WIN).transpose(2, 0, 1, 3)
    return mixed.transpose(0, 2, 1, 3), grad.transpose(0, 2, 1, 3), grad_bias


def solution(mesh):
    in_specs = (
        P(None, "lat", "lon", None),
        P(None, "lat", "lon", None),
        P(),
        P(),
        P(),
        P(None, None, "lon", None),
        P(),
        P(),
    )
    out_specs = (
        P(None, "lat", "lon", None),
        P(None, "lat", "lon", None),
        P("lat", None, "lon", None),
    )
    return jax.shard_map(local, mesh=mesh, in_specs=in_specs, out_specs=out_specs, check_vma=False)
```

time: 110 us -> 98.8 us (0.90)
  the two profiles are of different devices: /device:TPU:16 before, /device:TPU:1 now
where the time goes in v3:
time: 98.8 us; the launch traced here: 98.4 us
  Pallas kernels  55.8 us (56%)
  starting transfers between devices  23.9 us (24%)
  waiting for transfers between devices  17.4 us (18%)
    pallas_call x6, Pallas kernels, call(): pl.pallas_call(body, name=name, grid=(steps,), out_shape=tuple((a for a,...  55.8 us
    all_to_all x1, waiting for transfers between devices, local(): bias = lax.all_to_all(mine, 'lon', 0, 0, tiled=True)  10.5 us
    ppermute x6, starting transfers between devices, shift(): return lax.ppermute(block, ('lat', 'lon'), route)  9.34 us
    all_to_all x1, starting transfers between devices, local(): bias = lax.all_to_all(mine, 'lon', 0, 0, tiled=True)  7.3 us
    all_to_all x1, starting transfers between devices, local(): bias_sums = lax.all_to_all(last['bias_out'], 'lon', 0, 0, tiled=True)  7.26 us
    all_to_all x1, waiting for transfers between devices, local(): bias_sums = lax.all_to_all(last['bias_out'], 'lon', 0, 0, tiled=True)  6.92 us
  transfers between devices with their start and end apart: 8, of which 2 were waited for; matrix products, arithmetic and copies ran while one was open for 0% of the time, Pallas kernels for 31%

profile of v3, /device:TPU:1, one launch (start us, length us, event | category | flops | bytes accessed | tf_op | source)
XLA Modules:
  0.0 98.4 jit_solution(14730931723418317060)
XLA Ops:
  0.6 0.6 pad_add_fusion.at_ref.refs_5_
  1.2 4.4 %pack.1 = (bf16[4,336,128]{2,1,0:T(8,128)(2,1)}, bf16[4,336,128]{2,1,0:T(8,128)(2,1)}, bf16[4,144,128]{2,1,0:T(8,128)(2,1)}, bf16[16,144,128]{2,1,0:T(8,128)(2,1)}) custom-call(s32[3]{0:T(128)} %pad_add_fusion.at_ref.refs_5_, s32[16]{0:T(128)} %types_ref.1, bf16[8,12,24,192]{3,2,1,0:T(8,128)(2,1)} %bitcast.13, bf16[8,12,24,192]{3,2,1,0:T(8,128)(2,1)} %bitcast.17, ...), custom_call_target="tpu_custom_call" | custom-call | flops 1000000000 | bytes 3876364 | tf_op jit(solution)/shard_map/pack/pallas_call | solution.py:452
  5.6 7.3 %all-to-all-start = ((bf16[16,144,128]{2,1,0:T(8,128)(2,1)}), bf16[16,144,128]{2,1,0:T(8,128)(2,1)}, u32[]{:S(2)}, u32[]{:S(2)}) async-start(bf16[16,144,128]{2,1,0:T(8,128)(2,1)} %get-tuple-element.29), calls=%async_computation | async-start | bytes 1179648 | tf_op jit(solution)/shard_map/all_to_all | solution.py:538
  12.9 0.0 copy-done
  12.9 0.2 collective-permute-start
  13.1 10.5 %all-to-all-done.refs_7_.refs_12_ = bf16[16,144,128]{2,1,0:T(8,128)(2,1)} async-done(((bf16[16,144,128]{2,1,0:T(8,128)(2,1)}), bf16[16,144,128]{2,1,0:T(8,128)(2,1)}, u32[]{:S(2)}, u32[]{:S(2)}) %all-to-all-start) | async-done | bytes 589856 | tf_op jit(solution)/shard_map/all_to_all | solution.py:538
  23.6 6.7 %collective-permute-start.2 = (bf16[4,144,128]{2,1,0:T(8,128)(2,1)}, bf16[4,144,128]{2,1,0:T(8,128)(2,1)}, u32[]{:S(2)}, u32[]{:S(2)}) collective-permute-start(bf16[4,144,128]{2,1,0:T(8,128)(2,1)} %get-tuple-element.34), channel_id=1, source_target_pairs={{17,0},{18,1},{19,2},{20,3},{21,4},{22,5},{23,6},{24,7},{25,8},{26... | collective-permute-start | bytes 442376 | tf_op jit(solution)/shard_map/ppermute | solution.py:503
  30.3 0.5 collective-permute-start.1
  30.8 0.0 collective-permute-done.refs_5_.refs_6_
  30.8 10.6 %attend_first.1 = (bf16[4,144,192]{2,1,0:T(8,128)(2,1)}, bf16[4,144,192]{2,1,0:T(8,128)(2,1)}, bf16[6,192,192]{2,1,0:T(8,128)(2,1)}, f32[144,896]{1,0:T(8,128)}, f32[144,896]{1,0:T(8,128)}) custom-call(bf16[8,12,24,192]{3,2,1,0:T(8,128)(2,1)} %bitcast.14, bf16[8,12,24,192]{3,2,1,0:T(8,128)(2,1)} %bitcast.18, f32[1,192]{1,0:T(1,128)} %bitcast.22, ...), custom_call_target="tpu_custom_call" | custom-call | flops 10000000000 | bytes 6898432 | tf_op jit(solution)/shard_map/attend_first/pallas_call | solution.py:452
  41.3 0.0 collective-permute-done.2.refs_8_
  41.3 0.0 collective-permute-done.1.refs_7_
  41.3 19.2 %attend_south.1 = (bf16[4,288,192]{2,1,0:T(8,128)(2,1)}, bf16[4,288,192]{2,1,0:T(8,128)(2,1)}, bf16[4,336,128]{2,1,0:T(8,128)(2,1)}, bf16[4,336,128]{2,1,0:T(8,1...) custom-call(bf16[8,12,24,192]{3,2,1,0:T(8,128)(2,1)} %bitcast.15, bf16[8,12,24,192]{3,2,1,0:T(8,128)(2,1)} %bitcast.19, ...), custom_call_target="tpu_custom_call" | custom-call | flops 10000000000 | bytes 8916748 | tf_op jit(solution)/shard_map/attend_south/pallas_call | solution.py:452
  60.5 1.6 %collective-permute-start.5 = (bf16[4,144,128]{2,1,0:T(8,128)(2,1)}, bf16[4,144,128]{2,1,0:T(8,128)(2,1)}, u32[]{:S(2)}, u32[]{:S(2)}) collective-permute-start(bf16[4,144,128]{2,1,0:T(8,128)(2,1)} %get-tuple-element.45), channel_id=1, source_target_pairs={{127,0},{112,1},{113,2},{114,3},{115,4},{116,5},{117,6},{118,7},{1... | collective-permute-start | bytes 442376 | tf_op jit(solution)/shard_map/ppermute | solution.py:503
  62.2 0.0 collective-permute-start.3
  62.2 0.4 collective-permute-start.4
  62.5 15.1 %attend_last.1 = (bf16[8,12,24,192]{3,2,1,0:T(8,128)(2,1)}, bf16[8,12,24,192]{3,2,1,0:T(8,128)(2,1)}, bf16[16,160,128]{2,1,0:T(8,128)(2,1)}) custom-call(bf16[8,12,24,192]{3,2,1,0:T(8,128)(2,1)} %bitcast.16, bf16[8,12,24,192]{3,2,1,0:T(8,128)(2,1)} %bitcast.20, f32[1,192]{1,0:T(1,128)} %bitcast.24, bf16[192,192]{1,0:T(8,128)(2,1)} %refs_3_.5, ...), custom_call_target="tpu_custom_call" | custom-call | flops 10000000000 | bytes 10075904 | tf_op jit(solution)/shard_map/attend_last/pallas_call | solution.py:452
  77.6 7.3 %all-to-all-start.1 = ((bf16[16,160,128]{2,1,0:T(8,128)(2,1)}), bf16[16,160,128]{2,1,0:T(8,128)(2,1)}, u32[]{:S(2)}, u32[]{:S(2)}) async-start(bf16[16,160,128]{2,1,0:T(8,128)(2,1)} %get-tuple-element.48), calls=%async_computation.1 | async-start | bytes 1310720 | tf_op jit(solution)/shard_map/all_to_all | solution.py:659
  84.9 0.0 collective-permute-done.5.far_ref
  84.9 0.0 collective-permute-done.3.west_ref
  84.9 0.0 collective-permute-done.4.north_ref
  84.9 4.6 %land.1 = (bf16[8,12,24,192]{3,2,1,0:T(8,128)(2,1)}, bf16[8,12,24,192]{3,2,1,0:T(8,128)(2,1)}) custom-call(bf16[8,12,24,192]{3,2,1,0:T(8,128)(2,1)} %get-tuple-element.41.mixed_ref, bf16[8,12,24,192]{3,2,1,0:T(8,128)(2,1)} %get-tuple-element.42.grad_ref, bf16[4,336,128]{2,1,0:T(8,128)(2,1)} %collective-permute-done.3.west_ref, ...), custom_call_target="tpu_custom_call" | custom-call | flops 99999997952 | bytes 4687872 | tf_op jit(solution)/shard_map/land/pallas_call | solution.py:452
  89.5 6.9 %all-to-all-done.1.bias_ref = bf16[16,160,128]{2,1,0:T(8,128)(2,1)} async-done(((bf16[16,160,128]{2,1,0:T(8,128)(2,1)}), bf16[16,160,128]{2,1,0:T(8,128)(2,1)}, u32[]{:S(2)}, u32[]{:S(2)}) %all-to-all-start.1) | async-done | bytes 655392 | tf_op jit(solution)/shard_map/all_to_all | solution.py:659
  96.4 2.0 %bias_sum.1 = f32[54,2,144]{2,1,0:T(2,128)} custom-call(bf16[16,160,128]{2,1,0:T(8,128)(2,1)} %all-to-all-done.1.bias_ref), custom_call_target="tpu_custom_call" | custom-call | flops 1000000000 | bytes 717568 | tf_op jit(solution)/shard_map/bias_sum/pallas_call | solution.py:452
  (1 shorter events, 0.0 us)
Async XLA Ops:
  5.6 7.3 %copy-start = (bf16[4,336,128]{2,1,0:T(8,128)(2,1)S(1)}, bf16[4,336,128]{2,1,0:T(8,128)(2,1)}, u32[]{:S(2)}) copy-start(bf16[4,336,128]{2,1,0:T(8,128)(2,1)} %get-tuple-element.26) | copy-start | bytes 1032196
  5.6 18.0 %all-to-all-start = ((bf16[16,144,128]{2,1,0:T(8,128)(2,1)}), bf16[16,144,128]{2,1,0:T(8,128)(2,1)}, u32[]{:S(2)}, u32[]{:S(2)}) async-start(bf16[16,144,128]{2,1,0:T(8,128)(2,1)} %get-tuple-element.29), calls=%async_computation | async-start | bytes 1179648 | tf_op jit(solution)/shard_map/all_to_all | solution.py:538
  12.9 17.9 %collective-permute-start = (bf16[4,336,128]{2,1,0:T(8,128)(2,1)S(1)}, bf16[4,336,128]{2,1,0:T(8,128)(2,1)}, u32[]{:S(2)}, u32[]{:S(2)}) collective-permute-start(bf16[4,336,128]{2,1,0:T(8,128)(2,1)S(1)} %copy-done), channel_id=1, source_target_pairs={{1,0},{2,1},{3,2},{4,3},{5,4},{6,5},{7,6},{8,7},{9,8},{10,9},{11,1... | collective-permute-start | bytes 1032200 | tf_op jit(solution)/shard_map/ppermute | solution.py:503
  23.6 17.7 %collective-permute-start.2 = (bf16[4,144,128]{2,1,0:T(8,128)(2,1)}, bf16[4,144,128]{2,1,0:T(8,128)(2,1)}, u32[]{:S(2)}, u32[]{:S(2)}) collective-permute-start(bf16[4,144,128]{2,1,0:T(8,128)(2,1)} %get-tuple-element.34), channel_id=1, source_target_pairs={{17,0},{18,1},{19,2},{20,3},{21,4},{22,5},{23,6},{24,7},{25,8},{26... | collective-permute-start | bytes 442376 | tf_op jit(solution)/shard_map/ppermute | solution.py:503
  30.3 11.0 %collective-permute-start.1 = (bf16[4,336,128]{2,1,0:T(8,128)(2,1)}, bf16[4,336,128]{2,1,0:T(8,128)(2,1)}, u32[]{:S(2)}, u32[]{:S(2)}) collective-permute-start(bf16[4,336,128]{2,1,0:T(8,128)(2,1)} %get-tuple-element.33), channel_id=1, source_target_pairs={{16,0},{17,1},{18,2},{19,3},{20,4},{21,5},{22,6},{23,7},{24,8},{25... | collective-permute-start | bytes 1032200 | tf_op jit(solution)/shard_map/ppermute | solution.py:503
  60.5 24.3 %collective-permute-start.5 = (bf16[4,144,128]{2,1,0:T(8,128)(2,1)}, bf16[4,144,128]{2,1,0:T(8,128)(2,1)}, u32[]{:S(2)}, u32[]{:S(2)}) collective-permute-start(bf16[4,144,128]{2,1,0:T(8,128)(2,1)} %get-tuple-element.45), channel_id=1, source_target_pairs={{127,0},{112,1},{113,2},{114,3},{115,4},{116,5},{117,6},{118,7},{1... | collective-permute-start | bytes 442376 | tf_op jit(solution)/shard_map/ppermute | solution.py:503
  62.2 22.7 %collective-permute-start.3 = (bf16[4,336,128]{2,1,0:T(8,128)(2,1)}, bf16[4,336,128]{2,1,0:T(8,128)(2,1)}, u32[]{:S(2)}, u32[]{:S(2)}) collective-permute-start(bf16[4,336,128]{2,1,0:T(8,128)(2,1)} %get-tuple-element.43), channel_id=1, source_target_pairs={{15,0},{0,1},{1,2},{2,3},{3,4},{4,5},{5,6},{6,7},{7,8},{8,9},{9,10... | collective-permute-start | bytes 1032200 | tf_op jit(solution)/shard_map/ppermute | solution.py:503
  62.2 22.7 %collective-permute-start.4 = (bf16[4,336,128]{2,1,0:T(8,128)(2,1)}, bf16[4,336,128]{2,1,0:T(8,128)(2,1)}, u32[]{:S(2)}, u32[]{:S(2)}) collective-permute-start(bf16[4,336,128]{2,1,0:T(8,128)(2,1)} %get-tuple-element.44), channel_id=1, source_target_pairs={{112,0},{113,1},{114,2},{115,3},{116,4},{117,5},{118,6},{119,7},{1... | collective-permute-start | bytes 1032200 | tf_op jit(solution)/shard_map/ppermute | solution.py:503
  77.6 18.8 %all-to-all-start.1 = ((bf16[16,160,128]{2,1,0:T(8,128)(2,1)}), bf16[16,160,128]{2,1,0:T(8,128)(2,1)}, u32[]{:S(2)}, u32[]{:S(2)}) async-start(bf16[16,160,128]{2,1,0:T(8,128)(2,1)} %get-tuple-element.48), calls=%async_computation.1 | async-start | bytes 1310720 | tf_op jit(solution)/shard_map/all_to_all | solution.py:659

commit v4 on v3

--- a/solution.py
+++ b/solution.py
@@ -113,6 +113,9 @@
 
 def land_picks():
     sources = [
+        (window(0, 0), WIN),
+        (window(0, 1), WIN),
+        (window(1, 0) + window(1, 1), 2 * WIN),
         (tokens(range(SLON), range(SLAT, LATS)), STRIP),
         (tokens(range(SLON, COLS), range(SLAT)), STRIP),
         (tokens(range(SLON), range(SLAT)), CORNER),
@@ -170,20 +173,7 @@
     )
 
 
-def pack_kernel(
-    at_ref,
-    types_ref,
-    fields_ref,
-    cot_ref,
-    table_ref,
-    pick_ref,
-    eye_ref,
-    east_ref,
-    south_ref,
-    far_ref,
-    mine_ref,
-):
-    features = fields_ref.shape[-1]
+def choose_kernel(at_ref, types_ref, table_ref, eye_ref, mine_ref):
     table = table_ref[...].astype(F32)
     kind = lax.broadcasted_iota(jnp.int32, (1, table.shape[1], 1), 1)
     chosen = []
@@ -193,6 +183,10 @@
         chosen.append(jnp.zeros((ROWS - one.shape[0], WIN), BF16))
     mine = nt(eye_ref[...], jnp.concatenate(chosen, axis=0)).astype(BF16)
     mine_ref[...] = jnp.broadcast_to(mine[None], mine_ref.shape)
+
+
+def pack_kernel(fields_ref, cot_ref, pick_ref, east_ref, south_ref, far_ref):
+    features = fields_ref.shape[-1]
     for g in range(east_ref.shape[0]):
         rows = [
             nn(pick_ref[...], ref[WZ * g : WZ * (g + 1)].reshape(-1, features))
@@ -248,38 +242,49 @@
 def one_window(flat_f, flat_c, chosen, gain, proj_weight, weights, bias, eye, head_masks):
     x = nn(chosen, flat_f)
     cot = nn(chosen, flat_c).astype(BF16)
+    yield
     mean = jnp.mean(x, axis=1, keepdims=True)
     centered = x - mean
     variance = jnp.mean(centered * centered, axis=1, keepdims=True)
     inverse = lax.rsqrt(variance + EPSILON)
     hat = centered * inverse
     normed = (hat * gain).astype(BF16)
+    yield
     queries = nn(normed, weights[0]).astype(BF16)
     keys = nn(normed, weights[1]).astype(BF16)
     values = nn(normed, weights[2]).astype(BF16)
-    keys_t = nt(weights[3], normed).astype(BF16)
-    values_t = nt(weights[4], normed).astype(BF16)
+    keys_t = keys.T
+    values_t = values.T
     grad_att = nt(cot, proj_weight).astype(BF16)
+    yield
     q_blocks = head_blocks(queries, head_masks)
     g_blocks = head_blocks(grad_att, head_masks)
     scores = nt(keys, q_blocks) * (SCALE * LOG2E) + bias
+    yield
     exponent = jnp.exp2(scores - jnp.max(scores, axis=0, keepdims=True))
     soft = exponent * (1.0 / jnp.sum(exponent, axis=0, keepdims=True))
+    yield
     soft_bf = soft.astype(BF16)
     grad_soft = nt(values, g_blocks)
+    yield
     delta = jnp.sum(soft * grad_soft, axis=0, keepdims=True)
     grad_scores = soft * (grad_soft - delta)
+    yield
     grad_bf = grad_scores.astype(BF16)
     grad_values = nn(soft_bf, g_blocks).astype(BF16)
     grad_keys = (nn(grad_bf, q_blocks) * SCALE).astype(BF16)
+    yield
     attended_t = own_heads(nn(values_t, soft_bf)).astype(BF16)
     grad_queries_t = (own_heads(nn(keys_t, grad_bf)) * SCALE).astype(BF16)
+    yield
     projected_t = nn(weights[5], attended_t).astype(BF16)
-    projected = nt(eye[:WIN, :WIN], projected_t).astype(BF16)
-    grad_queries = nt(eye[:WIN, :WIN], grad_queries_t).astype(BF16)
+    projected = projected_t.T
+    grad_queries = grad_queries_t.T
+    yield
     grad_normed = (
         nt(grad_queries, weights[0]) + nt(grad_keys, weights[1]) + nt(grad_values, weights[2])
     )
+    yield
     grad_hat = grad_normed * gain
     grad_x = inverse * (
         grad_hat
@@ -289,39 +294,58 @@
     return projected, grad_x.astype(BF16), grad_scores
 
 
-def run_windows(todo, r, tables, pair):
+def together(windows):
+    results = [None] * len(windows)
+    left = dict(enumerate(windows))
+    while left:
+        for n in list(left):
+            try:
+                next(left[n])
+            except StopIteration as end:
+                results[n] = end.value
+                del left[n]
+    return results
+
+
+def run_windows(todo, r, tables, group):
     features = r["fields"].shape[-1]
-    levels = slice(WZ * pair, WZ * (pair + 1))
     lane_head = lax.broadcasted_iota(jnp.int32, (1, features), 1) // HEAD_DIM
     head_masks = [(lane_head == h).astype(F32).astype(BF16) for h in range(HEADS)]
     eye = r["eye"][...]
-    halos = {k: unpack(r[k][pair]) for k in ("east", "south", "far") if k in r}
-    done, total = [], None
-    for b, w in todo:
-        flats = []
-        for n, ref in enumerate((r["fields"], r["cot"])):
-            columns = slice(SLON, SLON + WLON) if w == 0 else slice(SLON + WLON, COLS)
-            parts = [ref[levels, columns].reshape(-1, features)]
-            if w == 1:
-                parts.append(halos["east"][n])
-            if b == 1:
-                parts.append(halos["south"][n])
+    windows = []
+    for pair in range(group):
+        levels = slice(WZ * pair, WZ * (pair + 1))
+        halos = {k: unpack(r[k][pair]) for k in ("east", "south", "far") if k in r}
+        for b, w in todo:
+            flats = []
+            for n, ref in enumerate((r["fields"], r["cot"])):
+                columns = slice(SLON, SLON + WLON) if w == 0 else slice(SLON + WLON, COLS)
+                parts = [ref[levels, columns].reshape(-1, features)]
                 if w == 1:
-                    parts.append(halos["far"][n])
-            flats.append(jnp.concatenate(parts, axis=0))
-        projected, grad, scores = one_window(
-            *flats,
-            r["pick%d" % w][...],
-            r["gain"][...],
-            r["proj"][...],
-            r["weights"],
-            tables(w),
-            eye,
-            head_masks,
-        )
-        done.append((projected, grad))
-        total = scores if total is None else total + scores
-    return done, total
+                    parts.append(halos["east"][n])
+                if b == 1:
+                    parts.append(halos["south"][n])
+                    if w == 1:
+                        parts.append(halos["far"][n])
+                flats.append(jnp.concatenate(parts, axis=0))
+            windows.append(
+                one_window(
+                    *flats,
+                    r["pick%d" % w][...],
+                    r["gain"][...],
+                    r["proj"][...],
+                    r["weights"],
+                    tables(w),
+                    eye,
+                    head_masks,
+                )
+            )
+    done = together(windows)
+    total = done[0][2]
+    for _, _, scores in done[1:]:
+        total = total + scores
+    each = len(todo)
+    return [[d[:2] for d in done[each * p : each * (p + 1)]] for p in range(group)], total
 
 
 def first_kernel(names, group, *refs):
@@ -333,12 +357,10 @@
         r["table"][...] = wide_bias(0, r["bias"], r["bias_pick"])
         r["sum"][...] = jnp.zeros_like(r["sum"])
 
-    totals = []
-    for pair in range(group):
-        done, total = run_windows([(0, 1)], r, lambda w: r["table"][...], pair)
+    pairs, total = run_windows([(0, 1)], r, lambda w: r["table"][...], group)
+    for pair, done in enumerate(pairs):
         r["win_p"][pair], r["win_g"][pair] = done[0]
-        totals.append(total)
-    r["sum"][...] += sum(totals[1:], totals[0])
+    r["sum"][...] += total
 
 
 def south_kernel(names, group, *refs):
@@ -350,9 +372,9 @@
         masked_tables(wide, r["at"], r["valid"], r["tables"])
         r["sum"][...] = jnp.zeros_like(r["sum"])
 
-    for pair in range(group):
-        done, total = run_windows([(1, 0), (1, 1)], r, lambda w: r["tables"][w], pair)
-        r["sum"][...] += total
+    pairs, total = run_windows([(1, 0), (1, 1)], r, lambda w: r["tables"][w], group)
+    r["sum"][...] += total
+    for pair, done in enumerate(pairs):
         placed = []
         for n, (first, out) in enumerate(
             ((r["first_p"], r["win_p"]), (r["first_g"], r["win_g"]))
@@ -368,27 +390,15 @@
 def last_kernel(names, group, *refs):
     r = dict(zip(names, refs))
     step = pl.program_id(0)
-    features = r["fields"].shape[-1]
 
     @pl.when(step == 0)
     def start():
         r["sum"][...] = r["sum0"][...]
 
-    for pair in range(group):
-        done, total = run_windows([(0, 0)], r, lambda w: r["table"][...], pair)
-        r["sum"][...] += total
-        levels = slice(WZ * pair, WZ * (pair + 1))
-        for n, (first, south, base, out) in enumerate(
-            (
-                (r["first_p"], r["south_p"], r["fields"], r["mixed"]),
-                (r["first_g"], r["south_g"], r["cot"], r["grad"]),
-            )
-        ):
-            every = jnp.concatenate([done[0][n], first[pair], south[pair]], axis=0)
-            part = nn(r["place"][...], every)
-            inner = part.reshape(WZ, COLS - SLON, LATS, features)
-            out[levels, :SLON] = base[levels, :SLON]
-            out[levels, SLON:] = (base[levels, SLON:].astype(F32) + inner).astype(BF16)
+    pairs, total = run_windows([(0, 0)], r, lambda w: r["table"][...], group)
+    r["sum"][...] += total
+    for pair, done in enumerate(pairs):
+        r["win_p"][pair], r["win_g"][pair] = done[0]
 
     @pl.when(step == pl.num_programs(0) - 1)
     def finish():
@@ -404,21 +414,34 @@
                 out[k, 80 * b : 80 * (b + 1)] = block
 
 
-def add_strips(strips, base_refs, place_ref, out_refs):
-    for pair in range(strips[0].shape[0]):
-        pieces = [unpack(ref[pair]) for ref in strips]
+def land_kernel(
+    fields_ref,
+    cot_ref,
+    last_p_ref,
+    last_g_ref,
+    first_p_ref,
+    first_g_ref,
+    south_p_ref,
+    south_g_ref,
+    west_ref,
+    north_ref,
+    far_ref,
+    place_ref,
+    out_m_ref,
+    out_g_ref,
+):
+    kinds = (
+        (fields_ref, (last_p_ref, first_p_ref, south_p_ref), out_m_ref),
+        (cot_ref, (last_g_ref, first_g_ref, south_g_ref), out_g_ref),
+    )
+    for pair in range(west_ref.shape[0]):
+        strips = [unpack(ref[pair]) for ref in (west_ref, north_ref, far_ref)]
         levels = slice(WZ * pair, WZ * (pair + 1))
-        for n, (base, out) in enumerate(zip(base_refs, out_refs)):
+        for n, (base, wins, out) in enumerate(kinds):
             own = base[levels]
-            part = nn(place_ref[...], jnp.concatenate([p[n] for p in pieces], axis=0))
+            pieces = [ref[pair] for ref in wins] + [strip[n] for strip in strips]
+            part = nn(place_ref[...], jnp.concatenate(pieces, axis=0))
             out[levels] = (own.astype(F32) + part.reshape(own.shape)).astype(BF16)
-
-
-def land_kernel(
-    mixed_ref, grad_ref, west_ref, north_ref, far_ref, place_ref, out_m_ref, out_g_ref
-):
-    strips = (west_ref, north_ref, far_ref)
-    add_strips(strips, (mixed_ref, grad_ref), place_ref, (out_m_ref, out_g_ref))
 
 
 def bias_kernel(bias_ref, out_ref):
@@ -519,20 +542,24 @@
     corner = shape_of(pairs, 3 * CORNER, MAIN)
 
     table = bias_table.transpose(1, 2, 0, 3).reshape(HEADS * per, -1, WIN)
-    east, south, far, mine = call(
-        pack_kernel,
-        "pack",
+    (mine,) = call(
+        choose_kernel,
+        "choose",
         1,
         [
             in_smem(at),
             in_smem(window_types),
-            entire(fields),
-            entire(cotangent),
             entire(table),
-            entire(jnp.asarray(send_picks(), BF16)),
             entire(jnp.asarray(np.eye(WIN), BF16)),
         ],
-        [entire(strip), entire(strip), entire(corner), entire(shape_of(parts, WIN, 2 * ROWS))],
+        [entire(shape_of(parts, WIN, 2 * ROWS))],
+    )
+    east, south, far = call(
+        pack_kernel,
+        "pack",
+        1,
+        [entire(fields), entire(cotangent), entire(jnp.asarray(send_picks(), BF16))],
+        [entire(strip), entire(strip), entire(corner)],
     )
     east = shift(east, 0, 1)
     bias = lax.all_to_all(mine, "lon", 0, 0, tiled=True)
@@ -542,7 +569,7 @@
 
     gain = norm_gain.reshape(1, -1)
     windows = {(b, w): window(b, w) for b in range(2) for w in range(2)}
-    steps = 2
+    steps = 1
     group = pairs // steps
 
     def constant(rows):
@@ -628,45 +655,44 @@
     north = shift(below["north"], -1, 0)
     far_back = shift(below["corner"], -1, -1)
     west = shift(below["west"], 0, -1)
-    every = [(windows[0, 0] + windows[0, 1] + windows[1, 0] + windows[1, 1], 4 * WIN)]
-    place = pick(tokens(range(SLON, COLS), range(LATS)), every)
     last = attend(
         last_kernel,
         "attend_last",
         steps,
         common
         | {
-            "first_p": split(first["win_p"]),
-            "first_g": split(first["win_g"]),
-            "south_p": split(below["win_p"]),
-            "south_g": split(below["win_g"]),
             "weights": entire(first["weights"]),
             "table": entire(first["table"]),
             "sum0": entire(first["sum"]),
             "sum1": entire(below["sum"]),
             "bias_pick": bias_pick,
             "pick0": picked(0, 0),
-            "place": constant(place),
         },
         {
-            "mixed": paired(shape_of(*fields.shape), WZ * group),
-            "grad": paired(shape_of(*fields.shape), WZ * group),
+            "win_p": tokens_of(WIN),
+            "win_g": tokens_of(WIN),
             "bias_out": entire(shape_of(parts, 160, 2 * ROWS)),
         },
         {"sum": pltpu.VMEM((WIN, LANES), F32)},
     )
-    mixed, grad = last["mixed"], last["grad"]
     bias_sums = lax.all_to_all(last["bias_out"], "lon", 0, 0, tiled=True)
 
     out_bias = shape_of(HEADS * per, 2, WIN, kind=F32)
+    steps, group = 2, pairs // 2
     block = paired(shape_of(*fields.shape), WZ * group)
     mixed, grad = call(
         land_kernel,
         "land",
         steps,
         [
-            paired(mixed, WZ * group),
-            paired(grad, WZ * group),
+            paired(fields, WZ * group),
+            paired(cotangent, WZ * group),
+            split(last["win_p"]),
+            split(last["win_g"]),
+            split(first["win_p"]),
+            split(first["win_g"]),
+            split(below["win_p"]),
+            split(below["win_g"]),
             split(west),
             split(north),
             split(far_back),

time: 98.8 us -> 83.8 us (0.85)
  the two profiles are of different devices: /device:TPU:1 before, /device:TPU:8 now
where the time goes in v4:
time: 83.8 us; the launch traced here: 83.4 us
  Pallas kernels  45.9 us (55%)
  starting transfers between devices  25.7 us (31%)
  waiting for transfers between devices  10.5 us (13%)
    pallas_call x7, Pallas kernels, call(): pl.pallas_call(body, name=name, grid=(steps,), out_shape=tuple((a for a,...  45.9 us
    ppermute x6, starting transfers between devices, shift(): return lax.ppermute(block, ('lat', 'lon'), route)  14.9 us
    all_to_all x1, waiting for transfers between devices, local(): bias_sums = lax.all_to_all(last['bias_out'], 'lon', 0, 0, tiled=True)  5.93 us
    all_to_all x1, starting transfers between devices, local(): bias = lax.all_to_all(mine, 'lon', 0, 0, tiled=True)  5.81 us
    all_to_all x1, starting transfers between devices, local(): bias_sums = lax.all_to_all(last['bias_out'], 'lon', 0, 0, tiled=True)  4.99 us
    all_to_all x1, waiting for transfers between devices, local(): bias = lax.all_to_all(mine, 'lon', 0, 0, tiled=True)  4.23 us
  transfers between devices with their start and end apart: 8, of which 3 were waited for; matrix products, arithmetic and copies ran while one was open for 0% of the time, Pallas kernels for 33%

profile of v4, /device:TPU:8, one launch (start us, length us, event | category | flops | bytes accessed | tf_op | source)
XLA Modules:
  0.0 83.4 jit_solution(10395905784040251088)
XLA Ops:
  0.6 0.7 pad_add_fusion.at_ref.refs_5_
  1.3 2.6 %choose.1 = bf16[16,144,128]{2,1,0:T(8,128)(2,1)} custom-call(s32[3]{0:T(128)} %pad_add_fusion.at_ref.refs_5_, s32[16]{0:T(128)} %types_ref.1, bf16[54,21,144]{2,1,0:T(8,128)(2,1)} %bitcast.23, bf16[144,144]{1,0:T(8,128)(2,1)} %constant.31.clone.eye_ref), custom_call_target="tpu_custom_call" | custom-call | flops 1000000000 | bytes 957964 | tf_op jit(solution)/shard_map/choose/pallas_call | solution.py:475
  3.9 5.8 %all-to-all-start = ((bf16[16,144,128]{2,1,0:T(8,128)(2,1)}), bf16[16,144,128]{2,1,0:T(8,128)(2,1)}, u32[]{:S(2)}, u32[]{:S(2)}) async-start(bf16[16,144,128]{2,1,0:T(8,128)(2,1)} %choose.1), calls=%async_computation | async-start | bytes 1179648 | tf_op jit(solution)/shard_map/all_to_all | solution.py:565
  9.7 3.6 %pack.1 = (bf16[4,336,128]{2,1,0:T(8,128)(2,1)}, bf16[4,336,128]{2,1,0:T(8,128)(2,1)}, bf16[4,144,128]{2,1,0:T(8,128)(2,1)}) custom-call(bf16[8,12,24,192]{3,2,1,0:T(8,128)(2,1)} %bitcast.13, bf16[8,12,24,192]{3,2,1,0:T(8,128)(2,1)} %bitcast.18, bf16[272,576]{1,0:T(8,128)(2,1)} %constant.32.clone.pick_ref), custom_call_target="tpu_custom_call" | custom-call | flops 1000000000 | bytes 2918400 | tf_op jit(solution)/shard_map/pack/pallas_call | solution.py:475
  13.4 3.7 %collective-permute-start = (bf16[4,336,128]{2,1,0:T(8,128)(2,1)}, bf16[4,336,128]{2,1,0:T(8,128)(2,1)}, u32[]{:S(2)}, u32[]{:S(2)}) collective-permute-start(bf16[4,336,128]{2,1,0:T(8,128)(2,1)} %get-tuple-element.25), channel_id=1, source_target_pairs={{1,0},{2,1},{3,2},{4,3},{5,4},{6,5},{7,6},{8,7},{9,8},{10,9},{11,1... | collective-permute-start | bytes 1032200 | tf_op jit(solution)/shard_map/ppermute | solution.py:526
  17.1 4.2 %all-to-all-done.refs_7_.refs_12_ = bf16[16,144,128]{2,1,0:T(8,128)(2,1)} async-done(((bf16[16,144,128]{2,1,0:T(8,128)(2,1)}), bf16[16,144,128]{2,1,0:T(8,128)(2,1)}, u32[]{:S(2)}, u32[]{:S(2)}) %all-to-all-start) | async-done | bytes 589856 | tf_op jit(solution)/shard_map/all_to_all | solution.py:565
  21.4 0.4 collective-permute-start.2
  21.7 5.1 %collective-permute-start.1 = (bf16[4,336,128]{2,1,0:T(8,128)(2,1)}, bf16[4,336,128]{2,1,0:T(8,128)(2,1)}, u32[]{:S(2)}, u32[]{:S(2)}) collective-permute-start(bf16[4,336,128]{2,1,0:T(8,128)(2,1)} %get-tuple-element.32), channel_id=1, source_target_pairs={{16,0},{17,1},{18,2},{19,3},{20,4},{21,5},{22,6},{23,7},{24,8},{25... | collective-permute-start | bytes 1032200 | tf_op jit(solution)/shard_map/ppermute | solution.py:526
  26.9 0.0 collective-permute-done.refs_5_.refs_6_
  26.9 8.3 %attend_first.1 = (bf16[4,144,192]{2,1,0:T(8,128)(2,1)}, bf16[4,144,192]{2,1,0:T(8,128)(2,1)}, bf16[6,192,192]{2,1,0:T(8,128)(2,1)}, f32[144,896]{1,0:T(8,128)}, f32[144,896]{1,0:T(8,128)}) custom-call(bf16[8,12,24,192]{3,2,1,0:T(8,128)(2,1)} %bitcast.14, bf16[8,12,24,192]{3,2,1,0:T(8,128)(2,1)} %bitcast.19, f32[1,192]{1,0:T(1,128)} %bitcast.24, ...), custom_call_target="tpu_custom_call" | custom-call | flops 10000000000 | bytes 6898432 | tf_op jit(solution)/shard_map/attend_first/pallas_call | solution.py:475
  35.2 0.0 collective-permute-done.2.refs_8_
  35.2 0.4 collective-permute-done.1.refs_7_
  35.5 13.8 %attend_south.1 = (bf16[4,288,192]{2,1,0:T(8,128)(2,1)}, bf16[4,288,192]{2,1,0:T(8,128)(2,1)}, bf16[4,336,128]{2,1,0:T(8,128)(2,1)}, bf16[4,336,128]{2,1,0:T(8,1...) custom-call(bf16[8,12,24,192]{3,2,1,0:T(8,128)(2,1)} %bitcast.15, bf16[8,12,24,192]{3,2,1,0:T(8,128)(2,1)} %bitcast.20, ...), custom_call_target="tpu_custom_call" | custom-call | flops 10000000000 | bytes 8916748 | tf_op jit(solution)/shard_map/attend_south/pallas_call | solution.py:475
  49.3 0.8 collective-permute-start.5
  50.1 0.0 collective-permute-start.3
  50.1 4.9 %collective-permute-start.4 = (bf16[4,336,128]{2,1,0:T(8,128)(2,1)}, bf16[4,336,128]{2,1,0:T(8,128)(2,1)}, u32[]{:S(2)}, u32[]{:S(2)}) collective-permute-start(bf16[4,336,128]{2,1,0:T(8,128)(2,1)} %get-tuple-element.42), channel_id=1, source_target_pairs={{112,0},{113,1},{114,2},{115,3},{116,4},{117,5},{118,6},{119,7},{1... | collective-permute-start | bytes 1032200 | tf_op jit(solution)/shard_map/ppermute | solution.py:526
  55.0 9.1 %attend_last.1 = (bf16[4,144,192]{2,1,0:T(8,128)(2,1)}, bf16[4,144,192]{2,1,0:T(8,128)(2,1)}, bf16[16,160,128]{2,1,0:T(8,128)(2,1)}) custom-call(bf16[8,12,24,192]{3,2,1,0:T(8,128)(2,1)} %bitcast.16, bf16[8,12,24,192]{3,2,1,0:T(8,128)(2,1)} %bitcast.21, f32[1,192]{1,0:T(1,128)} %bitcast.26, bf16[192,192]{1,0:T(8,128)(2,1)} %refs_3_.5, ...), custom_call_target="tpu_custom_call" | custom-call | flops 10000000000 | bytes 6924032 | tf_op jit(solution)/shard_map/attend_last/pallas_call | solution.py:475
  64.1 5.0 %all-to-all-start.1 = ((bf16[16,160,128]{2,1,0:T(8,128)(2,1)}), bf16[16,160,128]{2,1,0:T(8,128)(2,1)}, u32[]{:S(2)}, u32[]{:S(2)}) async-start(bf16[16,160,128]{2,1,0:T(8,128)(2,1)} %get-tuple-element.46), calls=%async_computation.1 | async-start | bytes 1310720 | tf_op jit(solution)/shard_map/all_to_all | solution.py:678
  69.1 0.0 collective-permute-done.5.far_ref
  69.1 0.0 collective-permute-done.3.west_ref
  69.1 0.0 collective-permute-done.4.north_ref
  69.2 6.4 %land.1 = (bf16[8,12,24,192]{3,2,1,0:T(8,128)(2,1)}, bf16[8,12,24,192]{3,2,1,0:T(8,128)(2,1)}) custom-call(bf16[8,12,24,192]{3,2,1,0:T(8,128)(2,1)} %bitcast.17, bf16[8,12,24,192]{3,2,1,0:T(8,128)(2,1)} %bitcast.22, bf16[4,144,192]{2,1,0:T(8,128)(2,1)} %get-tuple-element.37.last_p_ref, bf16[4,144,192]{2,1,0:T(8,128)(2,1)} %get-tuple-element.38.last_g_ref, ...), custom_call_target="tpu_custom_call" | custom-call | flops 99999997952 | bytes 7120896 | tf_op jit(solution)/shard_map/land/pallas_call | solution.py:475
  75.5 5.9 %all-to-all-done.1.bias_ref = bf16[16,160,128]{2,1,0:T(8,128)(2,1)} async-done(((bf16[16,160,128]{2,1,0:T(8,128)(2,1)}), bf16[16,160,128]{2,1,0:T(8,128)(2,1)}, u32[]{:S(2)}, u32[]{:S(2)}) %all-to-all-start.1) | async-done | bytes 655392 | tf_op jit(solution)/shard_map/all_to_all | solution.py:678
  81.4 2.0 %bias_sum.1 = f32[54,2,144]{2,1,0:T(2,128)} custom-call(bf16[16,160,128]{2,1,0:T(8,128)(2,1)} %all-to-all-done.1.bias_ref), custom_call_target="tpu_custom_call" | custom-call | flops 1000000000 | bytes 717568 | tf_op jit(solution)/shard_map/bias_sum/pallas_call | solution.py:475
Async XLA Ops:
  3.9 17.4 %all-to-all-start = ((bf16[16,144,128]{2,1,0:T(8,128)(2,1)}), bf16[16,144,128]{2,1,0:T(8,128)(2,1)}, u32[]{:S(2)}, u32[]{:S(2)}) async-start(bf16[16,144,128]{2,1,0:T(8,128)(2,1)} %choose.1), calls=%async_computation | async-start | bytes 1179648 | tf_op jit(solution)/shard_map/all_to_all | solution.py:565
  13.4 13.5 %collective-permute-start = (bf16[4,336,128]{2,1,0:T(8,128)(2,1)}, bf16[4,336,128]{2,1,0:T(8,128)(2,1)}, u32[]{:S(2)}, u32[]{:S(2)}) collective-permute-start(bf16[4,336,128]{2,1,0:T(8,128)(2,1)} %get-tuple-element.25), channel_id=1, source_target_pairs={{1,0},{2,1},{3,2},{4,3},{5,4},{6,5},{7,6},{8,7},{9,8},{10,9},{11,1... | collective-permute-start | bytes 1032200 | tf_op jit(solution)/shard_map/ppermute | solution.py:526
  21.4 13.8 %collective-permute-start.2 = (bf16[4,144,128]{2,1,0:T(8,128)(2,1)}, bf16[4,144,128]{2,1,0:T(8,128)(2,1)}, u32[]{:S(2)}, u32[]{:S(2)}) collective-permute-start(bf16[4,144,128]{2,1,0:T(8,128)(2,1)} %get-tuple-element.33), channel_id=1, source_target_pairs={{17,0},{18,1},{19,2},{20,3},{21,4},{22,5},{23,6},{24,7},{25,8},{26... | collective-permute-start | bytes 442376 | tf_op jit(solution)/shard_map/ppermute | solution.py:526
  21.7 13.8 %collective-permute-start.1 = (bf16[4,336,128]{2,1,0:T(8,128)(2,1)}, bf16[4,336,128]{2,1,0:T(8,128)(2,1)}, u32[]{:S(2)}, u32[]{:S(2)}) collective-permute-start(bf16[4,336,128]{2,1,0:T(8,128)(2,1)} %get-tuple-element.32), channel_id=1, source_target_pairs={{16,0},{17,1},{18,2},{19,3},{20,4},{21,5},{22,6},{23,7},{24,8},{25... | collective-permute-start | bytes 1032200 | tf_op jit(solution)/shard_map/ppermute | solution.py:526
  49.3 19.8 %collective-permute-start.5 = (bf16[4,144,128]{2,1,0:T(8,128)(2,1)}, bf16[4,144,128]{2,1,0:T(8,128)(2,1)}, u32[]{:S(2)}, u32[]{:S(2)}) collective-permute-start(bf16[4,144,128]{2,1,0:T(8,128)(2,1)} %get-tuple-element.43), channel_id=1, source_target_pairs={{127,0},{112,1},{113,2},{114,3},{115,4},{116,5},{117,6},{118,7},{1... | collective-permute-start | bytes 442376 | tf_op jit(solution)/shard_map/ppermute | solution.py:526
  50.1 19.0 %collective-permute-start.3 = (bf16[4,336,128]{2,1,0:T(8,128)(2,1)}, bf16[4,336,128]{2,1,0:T(8,128)(2,1)}, u32[]{:S(2)}, u32[]{:S(2)}) collective-permute-start(bf16[4,336,128]{2,1,0:T(8,128)(2,1)} %get-tuple-element.41), channel_id=1, source_target_pairs={{15,0},{0,1},{1,2},{2,3},{3,4},{4,5},{5,6},{6,7},{7,8},{8,9},{9,10... | collective-permute-start | bytes 1032200 | tf_op jit(solution)/shard_map/ppermute | solution.py:526
  50.1 19.0 %collective-permute-start.4 = (bf16[4,336,128]{2,1,0:T(8,128)(2,1)}, bf16[4,336,128]{2,1,0:T(8,128)(2,1)}, u32[]{:S(2)}, u32[]{:S(2)}) collective-permute-start(bf16[4,336,128]{2,1,0:T(8,128)(2,1)} %get-tuple-element.42), channel_id=1, source_target_pairs={{112,0},{113,1},{114,2},{115,3},{116,4},{117,5},{118,6},{119,7},{1... | collective-permute-start | bytes 1032200 | tf_op jit(solution)/shard_map/ppermute | solution.py:526
  64.1 17.3 %all-to-all-start.1 = ((bf16[16,160,128]{2,1,0:T(8,128)(2,1)}), bf16[16,160,128]{2,1,0:T(8,128)(2,1)}, u32[]{:S(2)}, u32[]{:S(2)}) async-start(bf16[16,160,128]{2,1,0:T(8,128)(2,1)} %get-tuple-element.46), calls=%async_computation.1 | async-start | bytes 1310720 | tf_op jit(solution)/shard_map/all_to_all | solution.py:678

commit v5 on v4

--- a/solution.py
+++ b/solution.py
@@ -50,7 +50,7 @@
 LATS = 2 * WLAT
 PAIR = WZ * COLS * LATS
 STRIP = 112
-CORNER = 48
+CORNER = 36
 
 
 def tokens(columns, rows):
@@ -108,7 +108,7 @@
     west = pick(tokens(range(SLON), range(SLAT, LATS)), own)
     north = pick(tokens(range(SLON, COLS), range(SLAT)), own)
     corner = pick(tokens(range(SLON), range(SLAT)), own)
-    return np.concatenate([padded(west, STRIP), padded(north, STRIP), padded(corner, CORNER)])
+    return np.concatenate([padded(west, STRIP), padded(north, STRIP), padded(corner, CORNER + 4)])
 
 
 def land_picks():
@@ -140,13 +140,17 @@
     return jnp.concatenate(pieces, axis=0)
 
 
-def own_heads(wide):
-    main, rest = [], []
-    for h in range(HEADS):
-        rows = wide[h * HEAD_DIM : (h + 1) * HEAD_DIM]
-        main.append(rows[:, h * MAIN : (h + 1) * MAIN])
-        left = HEADS * MAIN + h * REST
-        rest.append(rows[:, left : left + REST])
+def per_head(left, right):
+    main = []
+    for h in range(0, HEADS, 2):
+        both = nn(
+            left[h * HEAD_DIM : (h + 2) * HEAD_DIM], right[:, h * MAIN : (h + 2) * MAIN]
+        )
+        main += [both[:HEAD_DIM, :MAIN], both[HEAD_DIM:, MAIN:]]
+    wide = nn(left, right[:, HEADS * MAIN :])
+    rest = [
+        wide[h * HEAD_DIM : (h + 1) * HEAD_DIM, h * REST : (h + 1) * REST] for h in range(HEADS)
+    ]
     return jnp.concatenate(
         [jnp.concatenate(main, axis=0), jnp.concatenate(rest, axis=0)], axis=1
     )
@@ -274,8 +278,8 @@
     grad_values = nn(soft_bf, g_blocks).astype(BF16)
     grad_keys = (nn(grad_bf, q_blocks) * SCALE).astype(BF16)
     yield
-    attended_t = own_heads(nn(values_t, soft_bf)).astype(BF16)
-    grad_queries_t = (own_heads(nn(keys_t, grad_bf)) * SCALE).astype(BF16)
+    attended_t = per_head(values_t, soft_bf).astype(BF16)
+    grad_queries_t = (per_head(keys_t, grad_bf) * SCALE).astype(BF16)
     yield
     projected_t = nn(weights[5], attended_t).astype(BF16)
     projected = projected_t.T
@@ -307,45 +311,46 @@
     return results
 
 
-def run_windows(todo, r, tables, group):
+def run_windows(todo, r, tables):
     features = r["fields"].shape[-1]
     lane_head = lax.broadcasted_iota(jnp.int32, (1, features), 1) // HEAD_DIM
     head_masks = [(lane_head == h).astype(F32).astype(BF16) for h in range(HEADS)]
     eye = r["eye"][...]
+    halos = {}
     windows = []
-    for pair in range(group):
+    for pair, b, w in todo:
         levels = slice(WZ * pair, WZ * (pair + 1))
-        halos = {k: unpack(r[k][pair]) for k in ("east", "south", "far") if k in r}
-        for b, w in todo:
-            flats = []
-            for n, ref in enumerate((r["fields"], r["cot"])):
-                columns = slice(SLON, SLON + WLON) if w == 0 else slice(SLON + WLON, COLS)
-                parts = [ref[levels, columns].reshape(-1, features)]
+        for k in ("east", "south", "far"):
+            if k in r and (k, pair) not in halos:
+                halos[k, pair] = unpack(r[k][pair])
+        flats = []
+        for n, ref in enumerate((r["fields"], r["cot"])):
+            columns = slice(SLON, SLON + WLON) if w == 0 else slice(SLON + WLON, COLS)
+            parts = [ref[levels, columns].reshape(-1, features)]
+            if w == 1:
+                parts.append(halos["east", pair][n])
+            if b == 1:
+                parts.append(halos["south", pair][n])
                 if w == 1:
-                    parts.append(halos["east"][n])
-                if b == 1:
-                    parts.append(halos["south"][n])
-                    if w == 1:
-                        parts.append(halos["far"][n])
-                flats.append(jnp.concatenate(parts, axis=0))
-            windows.append(
-                one_window(
-                    *flats,
-                    r["pick%d" % w][...],
-                    r["gain"][...],
-                    r["proj"][...],
-                    r["weights"],
-                    tables(w),
-                    eye,
-                    head_masks,
-                )
+                    parts.append(halos["far", pair][n])
+            flats.append(jnp.concatenate(parts, axis=0))
+        windows.append(
+            one_window(
+                *flats,
+                r["pick%d" % w][...],
+                r["gain"][...],
+                r["proj"][...],
+                r["weights"],
+                tables(w),
+                eye,
+                head_masks,
             )
+        )
     done = together(windows)
     total = done[0][2]
     for _, _, scores in done[1:]:
         total = total + scores
-    each = len(todo)
-    return [[d[:2] for d in done[each * p : each * (p + 1)]] for p in range(group)], total
+    return [d[:2] for d in done], total
 
 
 def first_kernel(names, group, *refs):
@@ -357,9 +362,13 @@
         r["table"][...] = wide_bias(0, r["bias"], r["bias_pick"])
         r["sum"][...] = jnp.zeros_like(r["sum"])
 
-    pairs, total = run_windows([(0, 1)], r, lambda w: r["table"][...], group)
-    for pair, done in enumerate(pairs):
-        r["win_p"][pair], r["win_g"][pair] = done[0]
+    inner = r["in_p"].shape[0]
+    todo = [(pair, 0, 1) for pair in range(group)] + [(pair, 0, 0) for pair in range(inner)]
+    done, total = run_windows(todo, r, lambda w: r["table"][...])
+    for pair in range(group):
+        r["win_p"][pair], r["win_g"][pair] = done[pair]
+    for pair in range(inner):
+        r["in_p"][pair], r["in_g"][pair] = done[group + pair]
     r["sum"][...] += total
 
 
@@ -372,9 +381,11 @@
         masked_tables(wide, r["at"], r["valid"], r["tables"])
         r["sum"][...] = jnp.zeros_like(r["sum"])
 
-    pairs, total = run_windows([(1, 0), (1, 1)], r, lambda w: r["tables"][w], group)
+    todo = [(pair, 1, w) for pair in range(group) for w in range(2)]
+    results, total = run_windows(todo, r, lambda w: r["tables"][w])
     r["sum"][...] += total
-    for pair, done in enumerate(pairs):
+    for pair in range(group):
+        done = results[2 * pair : 2 * pair + 2]
         placed = []
         for n, (first, out) in enumerate(
             ((r["first_p"], r["win_p"]), (r["first_g"], r["win_g"]))
@@ -384,7 +395,7 @@
             placed.append(nn(r["place"][...], jnp.concatenate([first[pair], both], axis=0)))
         r["west"][pair] = pack(*(p[:STRIP] for p in placed))
         r["north"][pair] = pack(*(p[STRIP : 2 * STRIP] for p in placed))
-        r["corner"][pair] = pack(*(p[2 * STRIP :] for p in placed))
+        r["corner"][pair] = pack(*(p[2 * STRIP : 2 * STRIP + CORNER] for p in placed))
 
 
 def last_kernel(names, group, *refs):
@@ -395,28 +406,25 @@
     def start():
         r["sum"][...] = r["sum0"][...]
 
-    pairs, total = run_windows([(0, 0)], r, lambda w: r["table"][...], group)
+    todo = [(pair, 0, 0) for pair in range(group)]
+    done, total = run_windows(todo, r, lambda w: r["table"][...])
     r["sum"][...] += total
-    for pair, done in enumerate(pairs):
-        r["win_p"][pair], r["win_g"][pair] = done[0]
+    for pair in range(group):
+        r["win_p"][pair], r["win_g"][pair] = done[pair]
 
     @pl.when(step == pl.num_programs(0) - 1)
     def finish():
-        out = r["bias_out"]
-        for b, ref in enumerate((r["sum"], r["sum1"])):
-            wide = nt(ref[...].astype(BF16), r["bias_pick"][...])
-            top, low = wide[:80], wide[80:]
-            for k in range(out.shape[0]):
-                left = top[:, k * ROWS : (k + 1) * ROWS]
-                right = low[:, k * ROWS : (k + 1) * ROWS]
-                right = jnp.concatenate([right, jnp.zeros((160 - WIN, ROWS), F32)], axis=0)
-                block = jnp.concatenate([left, right], axis=1).astype(BF16)
-                out[k, 80 * b : 80 * (b + 1)] = block
+        wide = [nt(r[n][...].astype(BF16), r["bias_pick"][...]) for n in ("sum", "sum1")]
+        for k in range(r["bias_out"].shape[0]):
+            blocks = [part[:, k * ROWS : (k + 1) * ROWS] for part in wide]
+            r["bias_out"][k] = jnp.concatenate(blocks, axis=1).astype(BF16)
 
 
 def land_kernel(
     fields_ref,
     cot_ref,
+    in_p_ref,
+    in_g_ref,
     last_p_ref,
     last_g_ref,
     first_p_ref,
@@ -431,15 +439,17 @@
     out_g_ref,
 ):
     kinds = (
-        (fields_ref, (last_p_ref, first_p_ref, south_p_ref), out_m_ref),
-        (cot_ref, (last_g_ref, first_g_ref, south_g_ref), out_g_ref),
-    )
+        (fields_ref, (in_p_ref, last_p_ref), (first_p_ref, south_p_ref), out_m_ref),
+        (cot_ref, (in_g_ref, last_g_ref), (first_g_ref, south_g_ref), out_g_ref),
+    )
+    early = pl.program_id(0) == 0
     for pair in range(west_ref.shape[0]):
         strips = [unpack(ref[pair]) for ref in (west_ref, north_ref, far_ref)]
         levels = slice(WZ * pair, WZ * (pair + 1))
-        for n, (base, wins, out) in enumerate(kinds):
+        for n, (base, inner, wins, out) in enumerate(kinds):
             own = base[levels]
-            pieces = [ref[pair] for ref in wins] + [strip[n] for strip in strips]
+            pieces = [jnp.where(early, inner[0][pair], inner[1][pair])]
+            pieces += [ref[pair] for ref in wins] + [strip[n] for strip in strips]
             part = nn(place_ref[...], jnp.concatenate(pieces, axis=0))
             out[levels] = (own.astype(F32) + part.reshape(own.shape)).astype(BF16)
 
@@ -449,10 +459,9 @@
     total = bias_ref[0].astype(F32)
     for k in range(1, bias_ref.shape[0]):
         total = total + bias_ref[k].astype(F32)
+    turned = total.T
     for b in range(2):
-        turned = total[80 * b : 80 * (b + 1)].T
-        whole = jnp.concatenate([turned[:ROWS], turned[ROWS:, : WIN - 80]], axis=1)
-        out_ref[:, b, :] = whole[:count]
+        out_ref[:, b, :] = turned[b * ROWS : b * ROWS + count]
 
 
 def by_pair(array, size=1):
@@ -596,6 +605,8 @@
         "eye": constant(np.eye(features)),
     }
     bias_pick = constant(bias_picks(parts))
+    half = entire(shape_of(pairs // 2, WIN, features))
+    upper = pl.BlockSpec((levels // 2,) + fields.shape[1:], lambda g: (1, 0, 0, 0))
     first = attend(
         first_kernel,
         "attend_first",
@@ -606,11 +617,14 @@
             "qkv": entire(qkv_weight),
             "bias": entire(bias),
             "bias_pick": bias_pick,
+            "pick0": picked(0, 0),
             "pick1": picked(0, 1),
         },
         {
             "win_p": tokens_of(WIN),
             "win_g": tokens_of(WIN),
+            "in_p": half,
+            "in_g": half,
             "weights": entire(shape_of(6, features, features)),
             "table": wide_sum,
             "sum": wide_sum,
@@ -620,7 +634,7 @@
     place = [
         padded(pick(EAST, order), STRIP),
         padded(pick(SOUTH, order), STRIP),
-        padded(pick(FAR, order), CORNER),
+        padded(pick(FAR, order), CORNER + 4),
     ]
     below = attend(
         south_kernel,
@@ -661,6 +675,8 @@
         steps,
         common
         | {
+            "fields": (fields, upper),
+            "cot": (cotangent, upper),
             "weights": entire(first["weights"]),
             "table": entire(first["table"]),
             "sum0": entire(first["sum"]),
@@ -669,9 +685,9 @@
             "pick0": picked(0, 0),
         },
         {
-            "win_p": tokens_of(WIN),
-            "win_g": tokens_of(WIN),
-            "bias_out": entire(shape_of(parts, 160, 2 * ROWS)),
+            "win_p": half,
+            "win_g": half,
+            "bias_out": entire(shape_of(parts, WIN, 2 * ROWS)),
         },
         {"sum": pltpu.VMEM((WIN, LANES), F32)},
     )
@@ -687,8 +703,10 @@
         [
             paired(fields, WZ * group),
             paired(cotangent, WZ * group),
-            split(last["win_p"]),
-            split(last["win_g"]),
+            entire(first["in_p"]),
+            entire(first["in_g"]),
+            entire(last["win_p"]),
+            entire(last["win_g"]),
             split(first["win_p"]),
             split(first["win_g"]),
             split(below["win_p"]),

time: 83.8 us -> 79.4 us (0.947)
  the two profiles are of different devices: /device:TPU:8 before, /device:TPU:1 now
where the time goes in v5:
time: 79.4 us; the launch traced here: 78.6 us
  Pallas kernels  44.2 us (56%)
  starting transfers between devices  20.7 us (26%)
  waiting for transfers between devices  12.5 us (16%)
    pallas_call x7, Pallas kernels, call(): pl.pallas_call(body, name=name, grid=(steps,), out_shape=tuple((a for a,...  44.2 us
    ppermute x6, starting transfers between devices, shift(): return lax.ppermute(block, ('lat', 'lon'), route)  8.87 us
    all_to_all x1, starting transfers between devices, local(): bias = lax.all_to_all(mine, 'lon', 0, 0, tiled=True)  7.17 us
    all_to_all x1, waiting for transfers between devices, local(): bias = lax.all_to_all(mine, 'lon', 0, 0, tiled=True)  6.94 us
    ppermute x6, waiting for transfers between devices, shift(): return lax.ppermute(block, ('lat', 'lon'), route)  5.09 us
    all_to_all x1, starting transfers between devices, local(): bias_sums = lax.all_to_all(last['bias_out'], 'lon', 0, 0, tiled=True)  4.62 us
  transfers between devices with their start and end apart: 8, of which 4 were waited for; matrix products, arithmetic and copies ran while one was open for 0% of the time, Pallas kernels for 34%

profile of v5, /device:TPU:1, one launch (start us, length us, event | category | flops | bytes accessed | tf_op | source)
XLA Modules:
  0.0 78.6 jit_solution(17354172817575339454)
XLA Ops:
  0.6 0.7 pad_add_fusion.at_ref.refs_5_
  1.3 2.6 %choose.1 = bf16[16,144,128]{2,1,0:T(8,128)(2,1)} custom-call(s32[3]{0:T(128)} %pad_add_fusion.at_ref.refs_5_, s32[16]{0:T(128)} %types_ref.1, bf16[54,21,144]{2,1,0:T(8,128)(2,1)} %bitcast.23, bf16[144,144]{1,0:T(8,128)(2,1)} %constant.31.clone.eye_ref), custom_call_target="tpu_custom_call" | custom-call | flops 1000000000 | bytes 957964 | tf_op jit(solution)/shard_map/choose/pallas_call | solution.py:484
  3.9 7.2 %all-to-all-start = ((bf16[16,144,128]{2,1,0:T(8,128)(2,1)}), bf16[16,144,128]{2,1,0:T(8,128)(2,1)}, u32[]{:S(2)}, u32[]{:S(2)}) async-start(bf16[16,144,128]{2,1,0:T(8,128)(2,1)} %choose.1), calls=%async_computation | async-start | bytes 1179648 | tf_op jit(solution)/shard_map/all_to_all | solution.py:574
  11.1 3.6 %pack.1 = (bf16[4,336,128]{2,1,0:T(8,128)(2,1)}, bf16[4,336,128]{2,1,0:T(8,128)(2,1)}, bf16[4,108,128]{2,1,0:T(8,128)(2,1)}) custom-call(bf16[8,12,24,192]{3,2,1,0:T(8,128)(2,1)} %bitcast.13, bf16[8,12,24,192]{3,2,1,0:T(8,128)(2,1)} %bitcast.18, bf16[264,576]{1,0:T(8,128)(2,1)} %constant.32.clone.pick_ref), custom_call_target="tpu_custom_call" | custom-call | flops 1000000000 | bytes 2872320 | tf_op jit(solution)/shard_map/pack/pallas_call | solution.py:484
  14.7 0.2 collective-permute-start
  14.9 6.9 %all-to-all-done.refs_7_.refs_12_ = bf16[16,144,128]{2,1,0:T(8,128)(2,1)} async-done(((bf16[16,144,128]{2,1,0:T(8,128)(2,1)}), bf16[16,144,128]{2,1,0:T(8,128)(2,1)}, u32[]{:S(2)}, u32[]{:S(2)}) %all-to-all-start) | async-done | bytes 589856 | tf_op jit(solution)/shard_map/all_to_all | solution.py:574
  21.8 6.7 %collective-permute-start.2 = (bf16[4,108,128]{2,1,0:T(8,128)(2,1)}, bf16[4,108,128]{2,1,0:T(8,128)(2,1)}, u32[]{:S(2)}, u32[]{:S(2)}) collective-permute-start(bf16[4,108,128]{2,1,0:T(8,128)(2,1)} %get-tuple-element.37), channel_id=1, source_target_pairs={{17,0},{18,1},{19,2},{20,3},{21,4},{22,5},{23,6},{24,7},{25,8},{26... | collective-permute-start | bytes 331784 | tf_op jit(solution)/shard_map/ppermute | solution.py:535
  28.5 0.5 collective-permute-start.1
  29.0 0.0 collective-permute-done.refs_5_.refs_6_
  29.0 9.7 %attend_first.1 = (bf16[4,144,192]{2,1,0:T(8,128)(2,1)}, bf16[4,144,192]{2,1,0:T(8,128)(2,1)}, bf16[2,144,192]{2,1,0:T(8,128)(2,1)}, bf16[2,144,192]{2,1,0:T(8,1...) custom-call(bf16[8,12,24,192]{3,2,1,0:T(8,128)(2,1)} %bitcast.14, ...), custom_call_target="tpu_custom_call" | custom-call | flops 10000000000 | bytes 7202560 | tf_op jit(solution)/shard_map/attend_first/pallas_call | solution.py:484
  38.7 0.0 collective-permute-done.2.refs_8_
  38.7 0.4 collective-permute-done.1.refs_7_
  39.2 13.1 %attend_south.1 = (bf16[4,288,192]{2,1,0:T(8,128)(2,1)}, bf16[4,288,192]{2,1,0:T(8,128)(2,1)}, bf16[4,336,128]{2,1,0:T(8,128)(2,1)}, bf16[4,336,128]{2,1,0:T(8,1...) custom-call(bf16[8,12,24,192]{3,2,1,0:T(8,128)(2,1)} %bitcast.15, bf16[8,12,24,192]{3,2,1,0:T(8,128)(2,1)} %bitcast.20, ...), custom_call_target="tpu_custom_call" | custom-call | flops 10000000000 | bytes 8832652 | tf_op jit(solution)/shard_map/attend_south/pallas_call | solution.py:484
  52.3 1.2 %collective-permute-start.5 = (bf16[4,108,128]{2,1,0:T(8,128)(2,1)}, bf16[4,108,128]{2,1,0:T(8,128)(2,1)}, u32[]{:S(2)}, u32[]{:S(2)}) collective-permute-start(bf16[4,108,128]{2,1,0:T(8,128)(2,1)} %get-tuple-element.47), channel_id=1, source_target_pairs={{127,0},{112,1},{113,2},{114,3},{115,4},{116,5},{117,6},{118,7},{1... | collective-permute-start | bytes 331784 | tf_op jit(solution)/shard_map/ppermute | solution.py:535
  53.5 0.0 collective-permute-start.3
  53.5 0.4 collective-permute-start.4
  53.9 6.8 %attend_last.1 = (bf16[2,144,192]{2,1,0:T(8,128)(2,1)}, bf16[2,144,192]{2,1,0:T(8,128)(2,1)}, bf16[16,144,128]{2,1,0:T(8,128)(2,1)}) custom-call(bf16[8,12,24,192]{3,2,1,0:T(8,128)(2,1)} %bitcast.16, bf16[8,12,24,192]{3,2,1,0:T(8,128)(2,1)} %bitcast.21, f32[1,192]{1,0:T(1,128)} %bitcast.26, bf16[192,192]{1,0:T(8,128)(2,1)} %refs_3_.5, ...), custom_call_target="tpu_custom_call" | custom-call | flops 10000000000 | bytes 6637312 | tf_op jit(solution)/shard_map/attend_last/pallas_call | solution.py:484
  60.6 4.6 %all-to-all-start.1 = ((bf16[16,144,128]{2,1,0:T(8,128)(2,1)}), bf16[16,144,128]{2,1,0:T(8,128)(2,1)}, u32[]{:S(2)}, u32[]{:S(2)}) async-start(bf16[16,144,128]{2,1,0:T(8,128)(2,1)} %get-tuple-element.50), calls=%async_computation.1 | async-start | bytes 1179648 | tf_op jit(solution)/shard_map/all_to_all | solution.py:694
  65.2 0.0 collective-permute-done.5.far_ref
  65.2 0.0 collective-permute-done.3.west_ref
  65.3 4.6 %collective-permute-done.4.north_ref = bf16[4,336,128]{2,1,0:T(8,128)(2,1)} collective-permute-done((bf16[4,336,128]{2,1,0:T(8,128)(2,1)}, bf16[4,336,128]{2,1,0:T(8,128)(2,1)}, u32[]{:S(2)}, u32[]{:S(2)}) %collective-permute-start.4) | collective-permute-done | bytes 344096 | tf_op jit(solution)/shard_map/ppermute | solution.py:535
  69.9 6.4 %land.1 = (bf16[8,12,24,192]{3,2,1,0:T(8,128)(2,1)}, bf16[8,12,24,192]{3,2,1,0:T(8,128)(2,1)}) custom-call(bf16[8,12,24,192]{3,2,1,0:T(8,128)(2,1)} %bitcast.17, bf16[8,12,24,192]{3,2,1,0:T(8,128)(2,1)} %bitcast.22, bf16[2,144,192]{2,1,0:T(8,128)(2,1)} %get-tuple-element.31.in_p_ref, bf16[2,144,192]{2,1,0:T(8,128)(2,1)} %get-tuple-element.32.in_g_ref, ...), custom_call_target="tpu_custom_call" | custom-call | flops 99999997952 | bytes 7070208 | tf_op jit(solution)/shard_map/land/pallas_call | solution.py:484
  76.3 0.5 all-to-all-done.1.bias_ref
  76.8 1.9 %bias_sum.1 = f32[54,2,144]{2,1,0:T(2,128)} custom-call(bf16[16,144,128]{2,1,0:T(8,128)(2,1)} %all-to-all-done.1.bias_ref), custom_call_target="tpu_custom_call" | custom-call | flops 1000000000 | bytes 652032 | tf_op jit(solution)/shard_map/bias_sum/pallas_call | solution.py:484
Async XLA Ops:
  3.9 17.9 %all-to-all-start = ((bf16[16,144,128]{2,1,0:T(8,128)(2,1)}), bf16[16,144,128]{2,1,0:T(8,128)(2,1)}, u32[]{:S(2)}, u32[]{:S(2)}) async-start(bf16[16,144,128]{2,1,0:T(8,128)(2,1)} %choose.1), calls=%async_computation | async-start | bytes 1179648 | tf_op jit(solution)/shard_map/all_to_all | solution.py:574
  14.7 14.2 %collective-permute-start = (bf16[4,336,128]{2,1,0:T(8,128)(2,1)}, bf16[4,336,128]{2,1,0:T(8,128)(2,1)}, u32[]{:S(2)}, u32[]{:S(2)}) collective-permute-start(bf16[4,336,128]{2,1,0:T(8,128)(2,1)} %get-tuple-element.27), channel_id=1, source_target_pairs={{1,0},{2,1},{3,2},{4,3},{5,4},{6,5},{7,6},{8,7},{9,8},{10,9},{11,1... | collective-permute-start | bytes 1032200 | tf_op jit(solution)/shard_map/ppermute | solution.py:535
  21.8 16.9 %collective-permute-start.2 = (bf16[4,108,128]{2,1,0:T(8,128)(2,1)}, bf16[4,108,128]{2,1,0:T(8,128)(2,1)}, u32[]{:S(2)}, u32[]{:S(2)}) collective-permute-start(bf16[4,108,128]{2,1,0:T(8,128)(2,1)} %get-tuple-element.37), channel_id=1, source_target_pairs={{17,0},{18,1},{19,2},{20,3},{21,4},{22,5},{23,6},{24,7},{25,8},{26... | collective-permute-start | bytes 331784 | tf_op jit(solution)/shard_map/ppermute | solution.py:535
  28.5 10.7 %collective-permute-start.1 = (bf16[4,336,128]{2,1,0:T(8,128)(2,1)}, bf16[4,336,128]{2,1,0:T(8,128)(2,1)}, u32[]{:S(2)}, u32[]{:S(2)}) collective-permute-start(bf16[4,336,128]{2,1,0:T(8,128)(2,1)} %get-tuple-element.36), channel_id=1, source_target_pairs={{16,0},{17,1},{18,2},{19,3},{20,4},{21,5},{22,6},{23,7},{24,8},{25... | collective-permute-start | bytes 1032200 | tf_op jit(solution)/shard_map/ppermute | solution.py:535
  52.3 13.0 %collective-permute-start.5 = (bf16[4,108,128]{2,1,0:T(8,128)(2,1)}, bf16[4,108,128]{2,1,0:T(8,128)(2,1)}, u32[]{:S(2)}, u32[]{:S(2)}) collective-permute-start(bf16[4,108,128]{2,1,0:T(8,128)(2,1)} %get-tuple-element.47), channel_id=1, source_target_pairs={{127,0},{112,1},{113,2},{114,3},{115,4},{116,5},{117,6},{118,7},{1... | collective-permute-start | bytes 331784 | tf_op jit(solution)/shard_map/ppermute | solution.py:535
  53.5 11.8 %collective-permute-start.3 = (bf16[4,336,128]{2,1,0:T(8,128)(2,1)}, bf16[4,336,128]{2,1,0:T(8,128)(2,1)}, u32[]{:S(2)}, u32[]{:S(2)}) collective-permute-start(bf16[4,336,128]{2,1,0:T(8,128)(2,1)} %get-tuple-element.45), channel_id=1, source_target_pairs={{15,0},{0,1},{1,2},{2,3},{3,4},{4,5},{5,6},{6,7},{7,8},{8,9},{9,10... | collective-permute-start | bytes 1032200 | tf_op jit(solution)/shard_map/ppermute | solution.py:535
  53.5 16.4 %collective-permute-start.4 = (bf16[4,336,128]{2,1,0:T(8,128)(2,1)}, bf16[4,336,128]{2,1,0:T(8,128)(2,1)}, u32[]{:S(2)}, u32[]{:S(2)}) collective-permute-start(bf16[4,336,128]{2,1,0:T(8,128)(2,1)} %get-tuple-element.46), channel_id=1, source_target_pairs={{112,0},{113,1},{114,2},{115,3},{116,4},{117,5},{118,6},{119,7},{1... | collective-permute-start | bytes 1032200 | tf_op jit(solution)/shard_map/ppermute | solution.py:535
  60.6 16.1 %all-to-all-start.1 = ((bf16[16,144,128]{2,1,0:T(8,128)(2,1)}), bf16[16,144,128]{2,1,0:T(8,128)(2,1)}, u32[]{:S(2)}, u32[]{:S(2)}) async-start(bf16[16,144,128]{2,1,0:T(8,128)(2,1)} %get-tuple-element.50), calls=%async_computation.1 | async-start | bytes 1179648 | tf_op jit(solution)/shard_map/all_to_all | solution.py:694

commit v6 on v5

--- a/solution.py
+++ b/solution.py
@@ -51,6 +51,7 @@
 PAIR = WZ * COLS * LATS
 STRIP = 112
 CORNER = 36
+WEST = 72
 
 
 def tokens(columns, rows):
@@ -116,8 +117,9 @@
         (window(0, 0), WIN),
         (window(0, 1), WIN),
         (window(1, 0) + window(1, 1), 2 * WIN),
-        (tokens(range(SLON), range(SLAT, LATS)), STRIP),
         (tokens(range(SLON, COLS), range(SLAT)), STRIP),
+        (tokens(range(SLON), range(SLAT, SLAT + WLAT)), WEST),
+        (tokens(range(SLON), range(SLAT + WLAT, LATS)), CORNER),
         (tokens(range(SLON), range(SLAT)), CORNER),
     ]
     return pick(tokens(range(COLS), range(LATS)), sources)
@@ -177,12 +179,12 @@
     )
 
 
-def choose_kernel(at_ref, types_ref, table_ref, eye_ref, mine_ref):
+def choose_kernel(types_ref, table_ref, eye_ref, mine_ref):
     table = table_ref[...].astype(F32)
     kind = lax.broadcasted_iota(jnp.int32, (1, table.shape[1], 1), 1)
     chosen = []
     for b in range(2):
-        one = jnp.sum(jnp.where(kind == types_ref[2 * at_ref[0] + b], table, 0.0), axis=1)
+        one = jnp.sum(jnp.where(kind == types_ref[2 * lax.axis_index("lat") + b], table, 0.0), axis=1)
         chosen.append(one.astype(BF16))
         chosen.append(jnp.zeros((ROWS - one.shape[0], WIN), BF16))
     mine = nt(eye_ref[...], jnp.concatenate(chosen, axis=0)).astype(BF16)
@@ -218,13 +220,13 @@
     return nn(table, bias_pick_ref[...]) * LOG2E
 
 
-def masked_tables(wide, at_ref, valid_ref, tables):
+def masked_tables(wide, valid_ref, tables):
     key = lax.broadcasted_iota(jnp.int32, (WIN, 1), 0)
     lane = lax.broadcasted_iota(jnp.int32, (1, LANES), 1)
     query = jnp.where(lane < HEADS * MAIN, lane % MAIN, MAIN + (lane - HEADS * MAIN) % REST)
     key_row = (key // WLON) % WLAT
     query_row = (query // WLON) % WLAT
-    last = at_ref[0] == at_ref[2] - 1
+    last = lax.axis_index("lat") == lax.axis_size("lat") - 1
     same = (key_row < SLAT) == (query_row < SLAT)
     lat_rows, lon_columns = valid_ref.shape
     valid_rows = jnp.concatenate(
@@ -234,7 +236,7 @@
     key_valid = nn(row_pick, valid_rows)
     column = lax.broadcasted_iota(jnp.int32, (WIN, lon_columns), 1)
     for w in range(2):
-        wanted = at_ref[1] * COLS + SLON + WLON * w + key % WLON
+        wanted = lax.axis_index("lon") * COLS + SLON + WLON * w + key % WLON
         wanted = jnp.where(wanted >= lon_columns, wanted - lon_columns, wanted)
         is_valid = (
             jnp.sum(jnp.where(column == wanted, key_valid, 0.0), axis=1, keepdims=True) > 0.5
@@ -367,6 +369,7 @@
     done, total = run_windows(todo, r, lambda w: r["table"][...])
     for pair in range(group):
         r["win_p"][pair], r["win_g"][pair] = done[pair]
+        r["west"][pair] = pack(*(nn(r["place"][...], part) for part in done[pair]))
     for pair in range(inner):
         r["in_p"][pair], r["in_g"][pair] = done[group + pair]
     r["sum"][...] += total
@@ -378,7 +381,7 @@
     @pl.when(pl.program_id(0) == 0)
     def start():
         wide = wide_bias(1, r["bias"], r["bias_pick"])
-        masked_tables(wide, r["at"], r["valid"], r["tables"])
+        masked_tables(wide, r["valid"], r["tables"])
         r["sum"][...] = jnp.zeros_like(r["sum"])
 
     todo = [(pair, 1, w) for pair in range(group) for w in range(2)]
@@ -387,37 +390,37 @@
     for pair in range(group):
         done = results[2 * pair : 2 * pair + 2]
         placed = []
-        for n, (first, out) in enumerate(
-            ((r["first_p"], r["win_p"]), (r["first_g"], r["win_g"]))
-        ):
+        for n, out in enumerate((r["win_p"], r["win_g"])):
             both = jnp.concatenate([done[0][n], done[1][n]], axis=0)
             out[pair] = both
-            placed.append(nn(r["place"][...], jnp.concatenate([first[pair], both], axis=0)))
-        r["west"][pair] = pack(*(p[:STRIP] for p in placed))
-        r["north"][pair] = pack(*(p[STRIP : 2 * STRIP] for p in placed))
-        r["corner"][pair] = pack(*(p[2 * STRIP : 2 * STRIP + CORNER] for p in placed))
+            placed.append(nn(r["place"][...], both))
+        r["north"][pair] = pack(*(p[:STRIP] for p in placed))
+        r["west"][pair] = pack(*(p[STRIP : STRIP + CORNER] for p in placed))
+        at = STRIP + CORNER + 4
+        r["corner"][pair] = pack(*(p[at : at + CORNER] for p in placed))
 
 
 def last_kernel(names, group, *refs):
     r = dict(zip(names, refs))
-    step = pl.program_id(0)
-
-    @pl.when(step == 0)
-    def start():
-        r["sum"][...] = r["sum0"][...]
-
+    late = [
+        pltpu.make_async_copy(r[n], r[n + "_here"], r["arrived"].at[k])
+        for k, n in enumerate(("bias_pick", "sum0", "sum1"))
+    ]
+    for copy in late:
+        copy.start()
     todo = [(pair, 0, 0) for pair in range(group)]
     done, total = run_windows(todo, r, lambda w: r["table"][...])
-    r["sum"][...] += total
     for pair in range(group):
         r["win_p"][pair], r["win_g"][pair] = done[pair]
-
-    @pl.when(step == pl.num_programs(0) - 1)
-    def finish():
-        wide = [nt(r[n][...].astype(BF16), r["bias_pick"][...]) for n in ("sum", "sum1")]
-        for k in range(r["bias_out"].shape[0]):
-            blocks = [part[:, k * ROWS : (k + 1) * ROWS] for part in wide]
-            r["bias_out"][k] = jnp.concatenate(blocks, axis=1).astype(BF16)
+    for pair in range(r["west"].shape[0]):
+        r["west_p"][pair], r["west_g"][pair] = unpack(r["west"][pair])
+    for copy in late:
+        copy.wait()
+    sums = (r["sum0_here"][...] + total, r["sum1_here"][...])
+    wide = [nt(part.astype(BF16), r["bias_pick_here"][...]) for part in sums]
+    for k in range(r["bias_out"].shape[0]):
+        blocks = [part[:, k * ROWS : (k + 1) * ROWS] for part in wide]
+        r["bias_out"][k] = jnp.concatenate(blocks, axis=1).astype(BF16)
 
 
 def land_kernel(
@@ -431,6 +434,8 @@
     first_g_ref,
     south_p_ref,
     south_g_ref,
+    west_p_ref,
+    west_g_ref,
     west_ref,
     north_ref,
     far_ref,
@@ -439,17 +444,18 @@
     out_g_ref,
 ):
     kinds = (
-        (fields_ref, (in_p_ref, last_p_ref), (first_p_ref, south_p_ref), out_m_ref),
-        (cot_ref, (in_g_ref, last_g_ref), (first_g_ref, south_g_ref), out_g_ref),
+        (fields_ref, (in_p_ref, last_p_ref), (first_p_ref, south_p_ref), west_p_ref, out_m_ref),
+        (cot_ref, (in_g_ref, last_g_ref), (first_g_ref, south_g_ref), west_g_ref, out_g_ref),
     )
     early = pl.program_id(0) == 0
     for pair in range(west_ref.shape[0]):
-        strips = [unpack(ref[pair]) for ref in (west_ref, north_ref, far_ref)]
+        strips = [unpack(ref[pair]) for ref in (north_ref, west_ref, far_ref)]
         levels = slice(WZ * pair, WZ * (pair + 1))
-        for n, (base, inner, wins, out) in enumerate(kinds):
+        for n, (base, inner, wins, edge, out) in enumerate(kinds):
             own = base[levels]
             pieces = [jnp.where(early, inner[0][pair], inner[1][pair])]
-            pieces += [ref[pair] for ref in wins] + [strip[n] for strip in strips]
+            pieces += [ref[pair] for ref in wins]
+            pieces += [strips[0][n], edge[pair], strips[1][n], strips[2][n]]
             part = nn(place_ref[...], jnp.concatenate(pieces, axis=0))
             out[levels] = (own.astype(F32) + part.reshape(own.shape)).astype(BF16)
 
@@ -505,6 +511,10 @@
     return (array, whole(array))
 
 
+def in_place(array):
+    return (array, pl.BlockSpec(memory_space=pl.ANY))
+
+
 def in_smem(array):
     return (array, pl.BlockSpec(memory_space=pltpu.SMEM))
 
@@ -541,12 +551,9 @@
     fields = fields.transpose(0, 2, 1, 3)
     cotangent = cotangent.transpose(0, 2, 1, 3)
     levels, lon_cells, lat_cells, features = fields.shape
-    lat_at = lax.axis_index("lat")
-    lon_at = lax.axis_index("lon")
     parts = lax.axis_size("lon")
     per = WIN // parts
     pairs = levels // WZ
-    at = jnp.stack([lat_at, lon_at, lax.axis_size("lat")]).astype(jnp.int32)
     strip = shape_of(pairs, 3 * STRIP, MAIN)
     corner = shape_of(pairs, 3 * CORNER, MAIN)
 
@@ -556,7 +563,6 @@
         "choose",
         1,
         [
-            in_smem(at),
             in_smem(window_types),
             entire(table),
             entire(jnp.asarray(np.eye(WIN), BF16)),
@@ -619,8 +625,14 @@
             "bias_pick": bias_pick,
             "pick0": picked(0, 0),
             "pick1": picked(0, 1),
+            "place": constant(
+                pick(
+                    tokens(EAST_COLUMNS, range(SLAT, SLAT + WLAT)), [(windows[0, 1], WIN)]
+                )
+            ),
         },
         {
+            "west": strip_of(WEST),
             "win_p": tokens_of(WIN),
             "win_g": tokens_of(WIN),
             "in_p": half,
@@ -630,10 +642,11 @@
             "sum": wide_sum,
         },
     )
-    order = [(windows[0, 1] + windows[1, 0] + windows[1, 1], 3 * WIN)]
+    west0 = shift(first["west"], 0, -1)
+    order = [(windows[1, 0] + windows[1, 1], 2 * WIN)]
     place = [
-        padded(pick(EAST, order), STRIP),
         padded(pick(SOUTH, order), STRIP),
+        padded(pick(tokens(EAST_COLUMNS, range(SLAT + WLAT, LATS)), order), CORNER + 4),
         padded(pick(FAR, order), CORNER + 4),
     ]
     below = attend(
@@ -642,12 +655,9 @@
         steps,
         common
         | {
-            "at": in_smem(at),
             "east": split(east),
             "south": split(south),
             "far": split(far),
-            "first_p": split(first["win_p"]),
-            "first_g": split(first["win_g"]),
             "weights": entire(first["weights"]),
             "bias": entire(bias),
             "valid": entire(valid_mask),
@@ -659,7 +669,7 @@
         {
             "win_p": tokens_of(2 * WIN),
             "win_g": tokens_of(2 * WIN),
-            "west": strip_of(STRIP),
+            "west": strip_of(CORNER),
             "north": strip_of(STRIP),
             "corner": strip_of(CORNER),
             "sum": wide_sum,
@@ -679,17 +689,25 @@
             "cot": (cotangent, upper),
             "weights": entire(first["weights"]),
             "table": entire(first["table"]),
-            "sum0": entire(first["sum"]),
-            "sum1": entire(below["sum"]),
-            "bias_pick": bias_pick,
+            "west": entire(west0),
+            "sum0": in_place(first["sum"]),
+            "sum1": in_place(below["sum"]),
+            "bias_pick": in_place(bias_pick[0]),
             "pick0": picked(0, 0),
         },
         {
             "win_p": half,
             "win_g": half,
+            "west_p": tokens_of(WEST),
+            "west_g": tokens_of(WEST),
             "bias_out": entire(shape_of(parts, WIN, 2 * ROWS)),
         },
-        {"sum": pltpu.VMEM((WIN, LANES), F32)},
+        {
+            "sum0_here": pltpu.VMEM((WIN, LANES), F32),
+            "sum1_here": pltpu.VMEM((WIN, LANES), F32),
+            "bias_pick_here": pltpu.VMEM((parts * ROWS, LANES), BF16),
+            "arrived": pltpu.SemaphoreType.DMA((3,)),
+        },
     )
     bias_sums = lax.all_to_all(last["bias_out"], "lon", 0, 0, tiled=True)
 
@@ -711,6 +729,8 @@
             split(first["win_g"]),
             split(below["win_p"]),
             split(below["win_g"]),
+            split(last["west_p"]),
+            split(last["west_g"]),
             split(west),
             split(north),
             split(far_back),

time: 79.4 us -> 77.6 us (0.977)
  Pallas kernels: 44.2 us -> 42.7 us
  starting transfers between devices: 20.7 us -> 22 us
  waiting for transfers between devices: 12.5 us -> 11.2 us
    ppermute x6 -> x7, waiting for transfers between devices: 5.09 us -> 3.18 us  [shift(): return lax.ppermute(block, ('lat', 'lon'), route)]
    pallas_call x7, Pallas kernels: 44.2 us -> 42.7 us  [call(): pl.pallas_call(body, name=name, grid=(steps,), out_shape=tuple((a for a,...]
    ppermute x6 -> x7, starting transfers between devices: 8.87 us -> 9.8 us  [shift(): return lax.ppermute(block, ('lat', 'lon'), route)]
  transfers between devices with their start and end apart: 8 -> 9, of which waited for: 4 -> 3; matrix products, arithmetic and copies ran while one was open for 0% -> 0% of each run, Pallas kernels for 34% -> 50%
where the time goes in v6:
time: 77.6 us; the launch traced here: 76.6 us
  Pallas kernels  42.7 us (55%)
  starting transfers between devices  22 us (28%)
  waiting for transfers between devices  11.2 us (14%)
    pallas_call x7, Pallas kernels, call(): pl.pallas_call(body, name=name, grid=(steps,), out_shape=tuple((a for a,...  42.7 us
    ppermute x7, starting transfers between devices, shift(): return lax.ppermute(block, ('lat', 'lon'), route)  9.8 us
    all_to_all x1, starting transfers between devices, local(): bias = lax.all_to_all(mine, 'lon', 0, 0, tiled=True)  7.17 us
    all_to_all x1, waiting for transfers between devices, local(): bias = lax.all_to_all(mine, 'lon', 0, 0, tiled=True)  6.94 us
    all_to_all x1, starting transfers between devices, local(): bias_sums = lax.all_to_all(last['bias_out'], 'lon', 0, 0, tiled=True)  5 us
    ppermute x7, waiting for transfers between devices, shift(): return lax.ppermute(block, ('lat', 'lon'), route)  3.18 us
  transfers between devices with their start and end apart: 9, of which 3 were waited for; matrix products, arithmetic and copies ran while one was open for 0% of the time, Pallas kernels for 50%

profile of v6, /device:TPU:1, one launch (start us, length us, event | category | flops | bytes accessed | tf_op | source)
XLA Modules:
  0.0 76.6 jit_solution(6073370082806927567)
XLA Ops:
  0.6 2.7 %choose.1 = bf16[16,144,128]{2,1,0:T(8,128)(2,1)} custom-call(s32[16]{0:T(128)} %types_ref.1, bf16[54,21,144]{2,1,0:T(8,128)(2,1)} %bitcast.21, bf16[144,144]{1,0:T(8,128)(2,1)} %constant.22.clone.eye_ref), custom_call_target="tpu_custom_call" | custom-call | flops 1000000000 | bytes 957952 | tf_op jit(solution)/shard_map/choose/pallas_call | solution.py:490
  3.3 7.2 %all-to-all-start = ((bf16[16,144,128]{2,1,0:T(8,128)(2,1)}), bf16[16,144,128]{2,1,0:T(8,128)(2,1)}, u32[]{:S(2)}, u32[]{:S(2)}) async-start(bf16[16,144,128]{2,1,0:T(8,128)(2,1)} %choose.1), calls=%async_computation | async-start | bytes 1179648 | tf_op jit(solution)/shard_map/all_to_all | solution.py:580
  10.5 3.6 %pack.1 = (bf16[4,336,128]{2,1,0:T(8,128)(2,1)}, bf16[4,336,128]{2,1,0:T(8,128)(2,1)}, bf16[4,108,128]{2,1,0:T(8,128)(2,1)}) custom-call(bf16[8,12,24,192]{3,2,1,0:T(8,128)(2,1)} %bitcast.11, bf16[8,12,24,192]{3,2,1,0:T(8,128)(2,1)} %bitcast.16, bf16[264,576]{1,0:T(8,128)(2,1)} %constant.23.clone.pick_ref), custom_call_target="tpu_custom_call" | custom-call | flops 1000000000 | bytes 2872320 | tf_op jit(solution)/shard_map/pack/pallas_call | solution.py:490
  14.1 0.1 collective-permute-start
  14.2 6.9 %all-to-all-done.refs_7_.refs_9_ = bf16[16,144,128]{2,1,0:T(8,128)(2,1)} async-done(((bf16[16,144,128]{2,1,0:T(8,128)(2,1)}), bf16[16,144,128]{2,1,0:T(8,128)(2,1)}, u32[]{:S(2)}, u32[]{:S(2)}) %all-to-all-start) | async-done | bytes 589856 | tf_op jit(solution)/shard_map/all_to_all | solution.py:580
  21.2 6.7 %collective-permute-start.3 = (bf16[4,108,128]{2,1,0:T(8,128)(2,1)}, bf16[4,108,128]{2,1,0:T(8,128)(2,1)}, u32[]{:S(2)}, u32[]{:S(2)}) collective-permute-start(bf16[4,108,128]{2,1,0:T(8,128)(2,1)} %get-tuple-element.41), channel_id=1, source_target_pairs={{17,0},{18,1},{19,2},{20,3},{21,4},{22,5},{23,6},{24,7},{25,8},{26... | collective-permute-start | bytes 331784 | tf_op jit(solution)/shard_map/ppermute | solution.py:545
  27.9 0.5 collective-permute-start.2
  28.3 0.0 collective-permute-done.refs_5_
  28.3 9.8 %attend_first.1 = (bf16[4,216,128]{2,1,0:T(8,128)(2,1)}, bf16[4,144,192]{2,1,0:T(8,128)(2,1)}, bf16[4,144,192]{2,1,0:T(8,128)(2,1)}, bf16[2,144,192]{2,1,0:T(8,1...) custom-call(bf16[8,12,24,192]{3,2,1,0:T(8,128)(2,1)} %bitcast.12, ...), custom_call_target="tpu_custom_call" | custom-call | flops 10000000000 | bytes 7444480 | tf_op jit(solution)/shard_map/attend_first/pallas_call | solution.py:490
  38.1 1.1 %collective-permute-start.1 = (bf16[4,216,128]{2,1,0:T(8,128)(2,1)}, bf16[4,216,128]{2,1,0:T(8,128)(2,1)}, u32[]{:S(2)}, u32[]{:S(2)}) collective-permute-start(bf16[4,216,128]{2,1,0:T(8,128)(2,1)} %get-tuple-element.38), channel_id=1, source_target_pairs={{15,0},{0,1},{1,2},{2,3},{3,4},{4,5},{5,6},{6,7},{7,8},{8,9},{9,10... | collective-permute-start | bytes 663560 | tf_op jit(solution)/shard_map/ppermute | solution.py:545
  39.2 0.0 collective-permute-done.3.refs_7_
  39.2 0.0 collective-permute-done.2.refs_6_
  39.2 12.0 %attend_south.1 = (bf16[4,288,192]{2,1,0:T(8,128)(2,1)}, bf16[4,288,192]{2,1,0:T(8,128)(2,1)}, bf16[4,108,128]{2,1,0:T(8,128)(2,1)}, bf16[4,336,128]{2,1,0:T(8,1...) custom-call(bf16[8,12,24,192]{3,2,1,0:T(8,128)(2,1)} %bitcast.13, bf16[8,12,24,192]{3,2,1,0:T(8,128)(2,1)} %bitcast.18, ...), custom_call_target="tpu_custom_call" | custom-call | flops 10000000000 | bytes 8039296 | tf_op jit(solution)/shard_map/attend_south/pallas_call | solution.py:490
  51.2 0.1 collective-permute-start.4
  51.3 0.8 %collective-permute-start.6 = (bf16[4,108,128]{2,1,0:T(8,128)(2,1)}, bf16[4,108,128]{2,1,0:T(8,128)(2,1)}, u32[]{:S(2)}, u32[]{:S(2)}) collective-permute-start(bf16[4,108,128]{2,1,0:T(8,128)(2,1)} %get-tuple-element.53), channel_id=1, source_target_pairs={{127,0},{112,1},{113,2},{114,3},{115,4},{116,5},{117,6},{118,7},{1... | collective-permute-start | bytes 331784 | tf_op jit(solution)/shard_map/ppermute | solution.py:545
  52.1 0.5 collective-permute-start.5
  52.7 0.0 collective-permute-done.1.refs_7_
  52.7 6.3 %attend_last.1 = (bf16[2,144,192]{2,1,0:T(8,128)(2,1)}, bf16[2,144,192]{2,1,0:T(8,128)(2,1)}, bf16[4,72,192]{2,1,0:T(8,128)(2,1)}, bf16[4,72,192]{2,1,0:T(8,128)(2,1)}, bf16[16,144,128]{2,1,0:T(8,128)(2,1)}) custom-call(bf16[8,12,24,192]{3,2,1,0:T(8,128)(2,1)} %bitcast.14, bf16[8,12,24,192]{3,2,1,0:T(8,128)(2,1)} %bitcast.19, f32[1,192]{1,0:T(1,128)} %bitcast.24, ...), custom_call_target="tpu_custom_call" | custom-call | flops 10000000000 | bytes 7079680 | tf_op jit(solution)/shard_map/attend_last/pallas_call | solution.py:490
  59.0 5.0 %all-to-all-start.1 = ((bf16[16,144,128]{2,1,0:T(8,128)(2,1)}), bf16[16,144,128]{2,1,0:T(8,128)(2,1)}, u32[]{:S(2)}, u32[]{:S(2)}) async-start(bf16[16,144,128]{2,1,0:T(8,128)(2,1)} %get-tuple-element.56), calls=%async_computation.1 | async-start | bytes 1179648 | tf_op jit(solution)/shard_map/all_to_all | solution.py:712
  64.0 0.0 collective-permute-done.4.west_ref
  64.0 3.2 %collective-permute-done.5.north_ref = bf16[4,336,128]{2,1,0:T(8,128)(2,1)} collective-permute-done((bf16[4,336,128]{2,1,0:T(8,128)(2,1)}, bf16[4,336,128]{2,1,0:T(8,128)(2,1)}, u32[]{:S(2)}, u32[]{:S(2)}) %collective-permute-start.5) | collective-permute-done | bytes 344096 | tf_op jit(solution)/shard_map/ppermute | solution.py:545
  67.2 6.4 %land.1 = (bf16[8,12,24,192]{3,2,1,0:T(8,128)(2,1)}, bf16[8,12,24,192]{3,2,1,0:T(8,128)(2,1)}) custom-call(bf16[8,12,24,192]{3,2,1,0:T(8,128)(2,1)} %bitcast.15, bf16[8,12,24,192]{3,2,1,0:T(8,128)(2,1)} %bitcast.20, bf16[2,144,192]{2,1,0:T(8,128)(2,1)} %get-tuple-element.34.in_p_ref, bf16[2,144,192]{2,1,0:T(8,128)(2,1)} %get-tuple-element.35.in_g_ref, ...), custom_call_target="tpu_custom_call" | custom-call | flops 99999997952 | bytes 7053312 | tf_op jit(solution)/shard_map/land/pallas_call | solution.py:490
  73.6 1.1 %all-to-all-done.1.bias_ref = bf16[16,144,128]{2,1,0:T(8,128)(2,1)} async-done(((bf16[16,144,128]{2,1,0:T(8,128)(2,1)}), bf16[16,144,128]{2,1,0:T(8,128)(2,1)}, u32[]{:S(2)}, u32[]{:S(2)}) %all-to-all-start.1) | async-done | bytes 589856 | tf_op jit(solution)/shard_map/all_to_all | solution.py:712
  74.7 1.9 %bias_sum.1 = f32[54,2,144]{2,1,0:T(2,128)} custom-call(bf16[16,144,128]{2,1,0:T(8,128)(2,1)} %all-to-all-done.1.bias_ref), custom_call_target="tpu_custom_call" | custom-call | flops 1000000000 | bytes 652032 | tf_op jit(solution)/shard_map/bias_sum/pallas_call | solution.py:490
  (1 shorter events, 0.0 us)
Async XLA Ops:
  3.3 17.9 %all-to-all-start = ((bf16[16,144,128]{2,1,0:T(8,128)(2,1)}), bf16[16,144,128]{2,1,0:T(8,128)(2,1)}, u32[]{:S(2)}, u32[]{:S(2)}) async-start(bf16[16,144,128]{2,1,0:T(8,128)(2,1)} %choose.1), calls=%async_computation | async-start | bytes 1179648 | tf_op jit(solution)/shard_map/all_to_all | solution.py:580
  14.1 14.2 %collective-permute-start = (bf16[4,336,128]{2,1,0:T(8,128)(2,1)}, bf16[4,336,128]{2,1,0:T(8,128)(2,1)}, u32[]{:S(2)}, u32[]{:S(2)}) collective-permute-start(bf16[4,336,128]{2,1,0:T(8,128)(2,1)} %get-tuple-element.30), channel_id=1, source_target_pairs={{1,0},{2,1},{3,2},{4,3},{5,4},{6,5},{7,6},{8,7},{9,8},{10,9},{11,1... | collective-permute-start | bytes 1032200 | tf_op jit(solution)/shard_map/ppermute | solution.py:545
  21.2 18.0 %collective-permute-start.3 = (bf16[4,108,128]{2,1,0:T(8,128)(2,1)}, bf16[4,108,128]{2,1,0:T(8,128)(2,1)}, u32[]{:S(2)}, u32[]{:S(2)}) collective-permute-start(bf16[4,108,128]{2,1,0:T(8,128)(2,1)} %get-tuple-element.41), channel_id=1, source_target_pairs={{17,0},{18,1},{19,2},{20,3},{21,4},{22,5},{23,6},{24,7},{25,8},{26... | collective-permute-start | bytes 331784 | tf_op jit(solution)/shard_map/ppermute | solution.py:545
  27.9 11.3 %collective-permute-start.2 = (bf16[4,336,128]{2,1,0:T(8,128)(2,1)}, bf16[4,336,128]{2,1,0:T(8,128)(2,1)}, u32[]{:S(2)}, u32[]{:S(2)}) collective-permute-start(bf16[4,336,128]{2,1,0:T(8,128)(2,1)} %get-tuple-element.40), channel_id=1, source_target_pairs={{16,0},{17,1},{18,2},{19,3},{20,4},{21,5},{22,6},{23,7},{24,8},{25... | collective-permute-start | bytes 1032200 | tf_op jit(solution)/shard_map/ppermute | solution.py:545
  38.1 14.6 %collective-permute-start.1 = (bf16[4,216,128]{2,1,0:T(8,128)(2,1)}, bf16[4,216,128]{2,1,0:T(8,128)(2,1)}, u32[]{:S(2)}, u32[]{:S(2)}) collective-permute-start(bf16[4,216,128]{2,1,0:T(8,128)(2,1)} %get-tuple-element.38), channel_id=1, source_target_pairs={{15,0},{0,1},{1,2},{2,3},{3,4},{4,5},{5,6},{6,7},{7,8},{8,9},{9,10... | collective-permute-start | bytes 663560 | tf_op jit(solution)/shard_map/ppermute | solution.py:545
  51.2 12.8 %collective-permute-start.4 = (bf16[4,108,128]{2,1,0:T(8,128)(2,1)}, bf16[4,108,128]{2,1,0:T(8,128)(2,1)}, u32[]{:S(2)}, u32[]{:S(2)}) collective-permute-start(bf16[4,108,128]{2,1,0:T(8,128)(2,1)} %get-tuple-element.51), channel_id=1, source_target_pairs={{15,0},{0,1},{1,2},{2,3},{3,4},{4,5},{5,6},{6,7},{7,8},{8,9},{9,10... | collective-permute-start | bytes 331784 | tf_op jit(solution)/shard_map/ppermute | solution.py:545
  51.3 12.7 %collective-permute-start.6 = (bf16[4,108,128]{2,1,0:T(8,128)(2,1)}, bf16[4,108,128]{2,1,0:T(8,128)(2,1)}, u32[]{:S(2)}, u32[]{:S(2)}) collective-permute-start(bf16[4,108,128]{2,1,0:T(8,128)(2,1)} %get-tuple-element.53), channel_id=1, source_target_pairs={{127,0},{112,1},{113,2},{114,3},{115,4},{116,5},{117,6},{118,7},{1... | collective-permute-start | bytes 331784 | tf_op jit(solution)/shard_map/ppermute | solution.py:545
  52.1 15.1 %collective-permute-start.5 = (bf16[4,336,128]{2,1,0:T(8,128)(2,1)}, bf16[4,336,128]{2,1,0:T(8,128)(2,1)}, u32[]{:S(2)}, u32[]{:S(2)}) collective-permute-start(bf16[4,336,128]{2,1,0:T(8,128)(2,1)} %get-tuple-element.52), channel_id=1, source_target_pairs={{112,0},{113,1},{114,2},{115,3},{116,4},{117,5},{118,6},{119,7},{1... | collective-permute-start | bytes 1032200 | tf_op jit(solution)/shard_map/ppermute | solution.py:545
  59.0 15.7 %all-to-all-start.1 = ((bf16[16,144,128]{2,1,0:T(8,128)(2,1)}), bf16[16,144,128]{2,1,0:T(8,128)(2,1)}, u32[]{:S(2)}, u32[]{:S(2)}) async-start(bf16[16,144,128]{2,1,0:T(8,128)(2,1)} %get-tuple-element.56), calls=%async_computation.1 | async-start | bytes 1179648 | tf_op jit(solution)/shard_map/all_to_all | solution.py:712

commit v7 on v6

--- a/solution.py
+++ b/solution.py
@@ -578,7 +578,7 @@
     )
     east = shift(east, 0, 1)
     bias = lax.all_to_all(mine, "lon", 0, 0, tiled=True)
-    south, far, bias = lax.optimization_barrier((south, far, bias))
+    south, bias = lax.optimization_barrier((south, bias))
     south = shift(south, 1, 0)
     far = shift(far, 1, 1)
 

time: 77.6 us -> 76.4 us (0.985)
  waiting for transfers between devices: 11.2 us -> 4.28 us
  starting transfers between devices: 22 us -> 27.1 us
    all_to_all x1, waiting for transfers between devices: 6.94 us -> 0.01 us  [local(): bias = lax.all_to_all(mine, 'lon', 0, 0, tiled=True)]
    ppermute x7, starting transfers between devices: 9.8 us -> 13.5 us  [shift(): return lax.ppermute(block, ('lat', 'lon'), route)]
    all_to_all x1, starting transfers between devices: 5 us -> 6.45 us  [local(): bias_sums = lax.all_to_all(last['bias_out'], 'lon', 0, 0, tiled=True)]
  transfers between devices with their start and end apart: 9 -> 9, of which waited for: 3 -> 2; matrix products, arithmetic and copies ran while one was open for 0% -> 0% of each run, Pallas kernels for 50% -> 51%
where the time goes in v7:
time: 76.4 us; the launch traced here: 74.9 us
  Pallas kernels  42.8 us (56%)
  starting transfers between devices  27.1 us (35%)
  waiting for transfers between devices  4.28 us (6%)
    pallas_call x7, Pallas kernels, call(): pl.pallas_call(body, name=name, grid=(steps,), out_shape=tuple((a for a,...  42.8 us
    ppermute x7, starting transfers between devices, shift(): return lax.ppermute(block, ('lat', 'lon'), route)  13.5 us
    all_to_all x1, starting transfers between devices, local(): bias = lax.all_to_all(mine, 'lon', 0, 0, tiled=True)  7.17 us
    all_to_all x1, starting transfers between devices, local(): bias_sums = lax.all_to_all(last['bias_out'], 'lon', 0, 0, tiled=True)  6.45 us
    ppermute x7, waiting for transfers between devices, shift(): return lax.ppermute(block, ('lat', 'lon'), route)  2.89 us
  transfers between devices with their start and end apart: 9, of which 2 were waited for; matrix products, arithmetic and copies ran while one was open for 0% of the time, Pallas kernels for 51%

profile of v7, /device:TPU:1, one launch (start us, length us, event | category | flops | bytes accessed | tf_op | source)
XLA Modules:
  0.0 74.9 jit_solution(4412592118279547190)
XLA Ops:
  0.6 2.7 %choose.1 = bf16[16,144,128]{2,1,0:T(8,128)(2,1)} custom-call(s32[16]{0:T(128)} %types_ref.1, bf16[54,21,144]{2,1,0:T(8,128)(2,1)} %bitcast.21, bf16[144,144]{1,0:T(8,128)(2,1)} %constant.22.clone.eye_ref), custom_call_target="tpu_custom_call" | custom-call | flops 1000000000 | bytes 957952 | tf_op jit(solution)/shard_map/choose/pallas_call | solution.py:490
  3.3 7.2 %all-to-all-start = ((bf16[16,144,128]{2,1,0:T(8,128)(2,1)}), bf16[16,144,128]{2,1,0:T(8,128)(2,1)}, u32[]{:S(2)}, u32[]{:S(2)}) async-start(bf16[16,144,128]{2,1,0:T(8,128)(2,1)} %choose.1), calls=%async_computation | async-start | bytes 1179648 | tf_op jit(solution)/shard_map/all_to_all | solution.py:580
  10.5 3.6 %pack.1 = (bf16[4,336,128]{2,1,0:T(8,128)(2,1)}, bf16[4,336,128]{2,1,0:T(8,128)(2,1)}, bf16[4,108,128]{2,1,0:T(8,128)(2,1)}) custom-call(bf16[8,12,24,192]{3,2,1,0:T(8,128)(2,1)} %bitcast.11, bf16[8,12,24,192]{3,2,1,0:T(8,128)(2,1)} %bitcast.16, bf16[264,576]{1,0:T(8,128)(2,1)} %constant.23.clone.pick_ref), custom_call_target="tpu_custom_call" | custom-call | flops 1000000000 | bytes 2872320 | tf_op jit(solution)/shard_map/pack/pallas_call | solution.py:490
  14.1 0.1 collective-permute-start
  14.2 9.4 %collective-permute-start.3 = (bf16[4,108,128]{2,1,0:T(8,128)(2,1)}, bf16[4,108,128]{2,1,0:T(8,128)(2,1)}, u32[]{:S(2)}, u32[]{:S(2)}) collective-permute-start(bf16[4,108,128]{2,1,0:T(8,128)(2,1)} %get-tuple-element.39), channel_id=1, source_target_pairs={{17,0},{18,1},{19,2},{20,3},{21,4},{22,5},{23,6},{24,7},{25,8},{26... | collective-permute-start | bytes 331784 | tf_op jit(solution)/shard_map/ppermute | solution.py:545
  23.6 0.0 all-to-all-done.refs_7_.refs_9_
  23.6 3.3 %collective-permute-start.2 = (bf16[4,336,128]{2,1,0:T(8,128)(2,1)}, bf16[4,336,128]{2,1,0:T(8,128)(2,1)}, u32[]{:S(2)}, u32[]{:S(2)}) collective-permute-start(bf16[4,336,128]{2,1,0:T(8,128)(2,1)} %get-tuple-element.38), channel_id=1, source_target_pairs={{16,0},{17,1},{18,2},{19,3},{20,4},{21,5},{22,6},{23,7},{24,8},{25... | collective-permute-start | bytes 1032200 | tf_op jit(solution)/shard_map/ppermute | solution.py:545
  26.9 9.8 %attend_first.1 = (bf16[4,216,128]{2,1,0:T(8,128)(2,1)}, bf16[4,144,192]{2,1,0:T(8,128)(2,1)}, bf16[4,144,192]{2,1,0:T(8,128)(2,1)}, bf16[2,144,192]{2,1,0:T(8,1...) custom-call(bf16[8,12,24,192]{3,2,1,0:T(8,128)(2,1)} %bitcast.12, ...), custom_call_target="tpu_custom_call" | custom-call | flops 10000000000 | bytes 7444480 | tf_op jit(solution)/shard_map/attend_first/pallas_call | solution.py:490
  36.7 0.3 collective-permute-start.1
  37.0 0.0 collective-permute-done.3.refs_7_
  37.0 0.0 collective-permute-done.2.refs_6_
  37.0 12.1 %attend_south.1 = (bf16[4,288,192]{2,1,0:T(8,128)(2,1)}, bf16[4,288,192]{2,1,0:T(8,128)(2,1)}, bf16[4,108,128]{2,1,0:T(8,128)(2,1)}, bf16[4,336,128]{2,1,0:T(8,1...) custom-call(bf16[8,12,24,192]{3,2,1,0:T(8,128)(2,1)} %bitcast.13, bf16[8,12,24,192]{3,2,1,0:T(8,128)(2,1)} %bitcast.18, ...), custom_call_target="tpu_custom_call" | custom-call | flops 10000000000 | bytes 8039296 | tf_op jit(solution)/shard_map/attend_south/pallas_call | solution.py:490
  49.1 0.1 collective-permute-start.4
  49.2 0.1 collective-permute-start.6
  49.2 0.3 collective-permute-start.5
  49.5 0.0 collective-permute-done.1.refs_7_
  49.5 6.3 %attend_last.1 = (bf16[2,144,192]{2,1,0:T(8,128)(2,1)}, bf16[2,144,192]{2,1,0:T(8,128)(2,1)}, bf16[4,72,192]{2,1,0:T(8,128)(2,1)}, bf16[4,72,192]{2,1,0:T(8,128)(2,1)}, bf16[16,144,128]{2,1,0:T(8,128)(2,1)}) custom-call(bf16[8,12,24,192]{3,2,1,0:T(8,128)(2,1)} %bitcast.14, bf16[8,12,24,192]{3,2,1,0:T(8,128)(2,1)} %bitcast.19, f32[1,192]{1,0:T(1,128)} %bitcast.24, ...), custom_call_target="tpu_custom_call" | custom-call | flops 10000000000 | bytes 7079680 | tf_op jit(solution)/shard_map/attend_last/pallas_call | solution.py:490
  55.9 6.4 %all-to-all-start.1 = ((bf16[16,144,128]{2,1,0:T(8,128)(2,1)}), bf16[16,144,128]{2,1,0:T(8,128)(2,1)}, u32[]{:S(2)}, u32[]{:S(2)}) async-start(bf16[16,144,128]{2,1,0:T(8,128)(2,1)} %get-tuple-element.54), calls=%async_computation.1 | async-start | bytes 1179648 | tf_op jit(solution)/shard_map/all_to_all | solution.py:712
  62.3 0.0 collective-permute-done.4.west_ref
  62.3 0.0 collective-permute-done.6.far_ref
  62.4 2.9 %collective-permute-done.5.north_ref = bf16[4,336,128]{2,1,0:T(8,128)(2,1)} collective-permute-done((bf16[4,336,128]{2,1,0:T(8,128)(2,1)}, bf16[4,336,128]{2,1,0:T(8,128)(2,1)}, u32[]{:S(2)}, u32[]{:S(2)}) %collective-permute-start.5) | collective-permute-done | bytes 344096 | tf_op jit(solution)/shard_map/ppermute | solution.py:545
  65.2 6.4 %land.1 = (bf16[8,12,24,192]{3,2,1,0:T(8,128)(2,1)}, bf16[8,12,24,192]{3,2,1,0:T(8,128)(2,1)}) custom-call(bf16[8,12,24,192]{3,2,1,0:T(8,128)(2,1)} %bitcast.15, bf16[8,12,24,192]{3,2,1,0:T(8,128)(2,1)} %bitcast.20, bf16[2,144,192]{2,1,0:T(8,128)(2,1)} %get-tuple-element.32.in_p_ref, bf16[2,144,192]{2,1,0:T(8,128)(2,1)} %get-tuple-element.33.in_g_ref, ...), custom_call_target="tpu_custom_call" | custom-call | flops 99999997952 | bytes 7053312 | tf_op jit(solution)/shard_map/land/pallas_call | solution.py:490
  71.7 1.4 %all-to-all-done.1.bias_ref = bf16[16,144,128]{2,1,0:T(8,128)(2,1)} async-done(((bf16[16,144,128]{2,1,0:T(8,128)(2,1)}), bf16[16,144,128]{2,1,0:T(8,128)(2,1)}, u32[]{:S(2)}, u32[]{:S(2)}) %all-to-all-start.1) | async-done | bytes 589856 | tf_op jit(solution)/shard_map/all_to_all | solution.py:712
  73.1 1.9 %bias_sum.1 = f32[54,2,144]{2,1,0:T(2,128)} custom-call(bf16[16,144,128]{2,1,0:T(8,128)(2,1)} %all-to-all-done.1.bias_ref), custom_call_target="tpu_custom_call" | custom-call | flops 1000000000 | bytes 652032 | tf_op jit(solution)/shard_map/bias_sum/pallas_call | solution.py:490
  (1 shorter events, 0.0 us)
Async XLA Ops:
  3.3 20.4 %all-to-all-start = ((bf16[16,144,128]{2,1,0:T(8,128)(2,1)}), bf16[16,144,128]{2,1,0:T(8,128)(2,1)}, u32[]{:S(2)}, u32[]{:S(2)}) async-start(bf16[16,144,128]{2,1,0:T(8,128)(2,1)} %choose.1), calls=%async_computation | async-start | bytes 1179648 | tf_op jit(solution)/shard_map/all_to_all | solution.py:580
  14.1 12.8 %collective-permute-start = (bf16[4,336,128]{2,1,0:T(8,128)(2,1)}, bf16[4,336,128]{2,1,0:T(8,128)(2,1)}, u32[]{:S(2)}, u32[]{:S(2)}) collective-permute-start(bf16[4,336,128]{2,1,0:T(8,128)(2,1)} %get-tuple-element.29), channel_id=1, source_target_pairs={{1,0},{2,1},{3,2},{4,3},{5,4},{6,5},{7,6},{8,7},{9,8},{10,9},{11,1... | collective-permute-start | bytes 1032200 | tf_op jit(solution)/shard_map/ppermute | solution.py:545
  14.2 22.7 %collective-permute-start.3 = (bf16[4,108,128]{2,1,0:T(8,128)(2,1)}, bf16[4,108,128]{2,1,0:T(8,128)(2,1)}, u32[]{:S(2)}, u32[]{:S(2)}) collective-permute-start(bf16[4,108,128]{2,1,0:T(8,128)(2,1)} %get-tuple-element.39), channel_id=1, source_target_pairs={{17,0},{18,1},{19,2},{20,3},{21,4},{22,5},{23,6},{24,7},{25,8},{26... | collective-permute-start | bytes 331784 | tf_op jit(solution)/shard_map/ppermute | solution.py:545
  23.6 13.4 %collective-permute-start.2 = (bf16[4,336,128]{2,1,0:T(8,128)(2,1)}, bf16[4,336,128]{2,1,0:T(8,128)(2,1)}, u32[]{:S(2)}, u32[]{:S(2)}) collective-permute-start(bf16[4,336,128]{2,1,0:T(8,128)(2,1)} %get-tuple-element.38), channel_id=1, source_target_pairs={{16,0},{17,1},{18,2},{19,3},{20,4},{21,5},{22,6},{23,7},{24,8},{25... | collective-permute-start | bytes 1032200 | tf_op jit(solution)/shard_map/ppermute | solution.py:545
  36.7 12.8 %collective-permute-start.1 = (bf16[4,216,128]{2,1,0:T(8,128)(2,1)}, bf16[4,216,128]{2,1,0:T(8,128)(2,1)}, u32[]{:S(2)}, u32[]{:S(2)}) collective-permute-start(bf16[4,216,128]{2,1,0:T(8,128)(2,1)} %get-tuple-element.36), channel_id=1, source_target_pairs={{15,0},{0,1},{1,2},{2,3},{3,4},{4,5},{5,6},{6,7},{7,8},{8,9},{9,10... | collective-permute-start | bytes 663560 | tf_op jit(solution)/shard_map/ppermute | solution.py:545
  49.1 13.2 %collective-permute-start.4 = (bf16[4,108,128]{2,1,0:T(8,128)(2,1)}, bf16[4,108,128]{2,1,0:T(8,128)(2,1)}, u32[]{:S(2)}, u32[]{:S(2)}) collective-permute-start(bf16[4,108,128]{2,1,0:T(8,128)(2,1)} %get-tuple-element.49), channel_id=1, source_target_pairs={{15,0},{0,1},{1,2},{2,3},{3,4},{4,5},{5,6},{6,7},{7,8},{8,9},{9,10... | collective-permute-start | bytes 331784 | tf_op jit(solution)/shard_map/ppermute | solution.py:545
  49.2 13.2 %collective-permute-start.6 = (bf16[4,108,128]{2,1,0:T(8,128)(2,1)}, bf16[4,108,128]{2,1,0:T(8,128)(2,1)}, u32[]{:S(2)}, u32[]{:S(2)}) collective-permute-start(bf16[4,108,128]{2,1,0:T(8,128)(2,1)} %get-tuple-element.51), channel_id=1, source_target_pairs={{127,0},{112,1},{113,2},{114,3},{115,4},{116,5},{117,6},{118,7},{1... | collective-permute-start | bytes 331784 | tf_op jit(solution)/shard_map/ppermute | solution.py:545
  49.2 16.0 %collective-permute-start.5 = (bf16[4,336,128]{2,1,0:T(8,128)(2,1)}, bf16[4,336,128]{2,1,0:T(8,128)(2,1)}, u32[]{:S(2)}, u32[]{:S(2)}) collective-permute-start(bf16[4,336,128]{2,1,0:T(8,128)(2,1)} %get-tuple-element.50), channel_id=1, source_target_pairs={{112,0},{113,1},{114,2},{115,3},{116,4},{117,5},{118,6},{119,7},{1... | collective-permute-start | bytes 1032200 | tf_op jit(solution)/shard_map/ppermute | solution.py:545
  55.9 17.2 %all-to-all-start.1 = ((bf16[16,144,128]{2,1,0:T(8,128)(2,1)}), bf16[16,144,128]{2,1,0:T(8,128)(2,1)}, u32[]{:S(2)}, u32[]{:S(2)}) async-start(bf16[16,144,128]{2,1,0:T(8,128)(2,1)} %get-tuple-element.54), calls=%async_computation.1 | async-start | bytes 1179648 | tf_op jit(solution)/shard_map/all_to_all | solution.py:712
